TPU v7x, 32 devices: a whole 2x2x4 slice. The times are simulated.
32 devices in a mesh: dp: 4 (over x, core), expert: 8 (over z, y).
Axes of the slice: x: 2, y: 2, z: 4, core: 2. Of those that a mesh axis runs over, the one named last changes fastest.
Arguments:
- tokens: bfloat16 [16384, 1280], P(('dp', 'expert')), may hold values from -6 to 6
- w_qkv: bfloat16 [1280, 3840], P(('dp', 'expert')), may hold values from -0.15625 to 0.15625
- w_attn_out: bfloat16 [1280, 1280], P(('dp', 'expert')), may hold values from -1.25 to 1.25
- w_shared_in: bfloat16 [1280, 1792], P(('dp', 'expert')), may hold values from -0.15625 to 0.15625
- w_shared_out: bfloat16 [896, 1280], P(('dp', 'expert')), may hold values from -0.375 to 0.375
- gain_attn: bfloat16 [1280], P(('dp', 'expert')), may hold values from 0.5 to 1.5
- gain_ffn: bfloat16 [1280], P(('dp', 'expert')), may hold values from 0.5 to 1.5
- w_expert_in: bfloat16 [16, 1280, 1792], P('expert'), may hold values from -0.15625 to 0.15625
- w_expert_out: bfloat16 [16, 896, 1280], P('expert'), may hold values from -0.75 to 0.75
- route_ids: int32 [16384, 6], P(('dp', 'expert')), may hold values from 0 to 15, all different within a row; in each aligned block of 512 rows (0 to 511, 512 to 1023, ...) at most 240 rows name the same one
- route_gates: float32 [16384, 6], P(('dp', 'expert')), may hold values from 0.08 to 0.25
- seq_lengths: int32 [32], P(('dp', 'expert')), may hold values from 1 to 512, 12288 in all
- cotangent: bfloat16 [16384, 1280], P(('dp', 'expert')), may hold values from -6 to 6
Outputs:
- block_out: bfloat16 [16384, 1280], P(('dp', 'expert'))
- grad_tokens: float32 [16384, 1280], P(('dp', 'expert'))
- grad_qkv: float32 [1280, 3840], P(('dp', 'expert'))
- grad_attn_out: float32 [1280, 1280], P(('dp', 'expert'))
- grad_shared_in: float32 [1280, 1792], P(('dp', 'expert'))
- grad_shared_out: float32 [896, 1280], P(('dp', 'expert'))
- grad_gain_attn: float32 [1280], P(('dp', 'expert'))
- grad_gain_ffn: float32 [1280], P(('dp', 'expert'))
- grad_expert_in: float32 [16, 1280, 1792], P('expert')
- grad_expert_out: float32 [16, 896, 1280], P('expert')
- expert_counts: int32 [16], replicated
Inputs may be any that keep to these rules, and one draw needn't show every extreme that they name: `route_ids`: each row names 6 different experts. Within the rows of one sequence no expert is named more than 240 times, and in some sequence some expert is named exactly 240 times. `seq_lengths`: live tokens are the first ones of a sequence; some sequence is full.
All inputs are finite; a program needn't handle non-finite values. No bound on the sum of `seq_lengths` on one device may be relied on, other than what follows from the above.
Results may differ from a plain program's by a relative error of at most 0.014.
Values may be sent and summed in bfloat16 or wider, within the bound.
No kernel may reach another device: no remote copies, remote signals or barrier semaphores. Data moves between devices by JAX's collectives and lax.ppermute only.
A program may use at most 320 MiB of HBM per device.

v0:
```python
import jax
import jax.numpy as jnp
from jax import lax
from jax.sharding import PartitionSpec as P

HEADS = 10
HEAD_DIM = 128
TOP = 6


norm_eps = 1e-06


def rotary_tables(positions, head_dim):
    half_dim = head_dim // 2
    frequencies = 10000.0 ** (-(2.0 * jnp.arange(half_dim, dtype=jnp.float32)) / head_dim)
    angles = positions.astype(jnp.float32)[:, None] * frequencies[None, :]
    return (jnp.cos(angles)[:, None, :], jnp.sin(angles)[:, None, :])


def rotate(head_rows, cosine, sine_table):
    half_dim = head_rows.shape[-1] // 2
    first_half = head_rows[..., :half_dim]
    second = head_rows[..., half_dim:]
    return jnp.concatenate(
        [first_half * cosine - second * sine_table, second * cosine + first_half * sine_table],
        axis=-1,
    )


def unrotate(head_grads, cosine, sine_table):
    half_dim = head_grads.shape[-1] // 2
    first_half = head_grads[..., :half_dim]
    second = head_grads[..., half_dim:]
    return jnp.concatenate(
        [first_half * cosine + second * sine_table, second * cosine - first_half * sine_table],
        axis=-1,
    )


def contract_rows(left, right):
    return lax.dot_general(
        left, right, (((0,), (0,)), ((), ())), preferred_element_type=jnp.float32
    )


def times_transposed(left, right):
    return lax.dot_general(
        left, right, (((1,), (1,)), ((), ())), preferred_element_type=jnp.float32
    )


def swish_product(gate_up, hidden_width):
    gate_part = gate_up[..., :hidden_width]
    return gate_part * jax.nn.sigmoid(gate_part) * gate_up[..., hidden_width:]


def swish_back(grad_hidden, gate_up, hidden_width):
    gate_part = gate_up[..., :hidden_width]
    up_part = gate_up[..., hidden_width:]
    sigmoid_gate = jax.nn.sigmoid(gate_part)
    grad_gate = grad_hidden * up_part * sigmoid_gate * (1.0 + gate_part * (1.0 - sigmoid_gate))
    grad_up = grad_hidden * gate_part * sigmoid_gate
    return jnp.concatenate([grad_gate, grad_up], axis=-1)


def norm_scale(activation):
    return lax.rsqrt(jnp.mean(activation * activation, axis=-1, keepdims=True) + norm_eps)


def norm_back(grad_normed, activation, row_scale, norm_gain):
    weighted = grad_normed * norm_gain
    grad_input = row_scale * weighted - activation * row_scale**3 * jnp.mean(
        weighted * activation, axis=-1, keepdims=True
    )
    return (grad_input, jnp.sum(grad_normed * activation * row_scale, axis=0))


def on_device(
    tokens,
    w_qkv,
    w_attn_out,
    w_shared_in,
    w_shared_out,
    gain_attn,
    gain_ffn,
    w_expert_in,
    w_expert_out,
    route_ids,
    route_gates,
    seq_lengths,
    cotangent,
):
    row_count = tokens.shape[0]
    model_width = tokens.shape[1]
    groups = lax.axis_size("expert")
    local_experts = w_expert_in.shape[0]
    experts_total = local_experts * groups
    capacity = row_count * TOP * 5 // (4 * experts_total)
    slots_total = experts_total * capacity
    hidden_width = w_expert_out.shape[1]
    assignments = row_count * TOP
    dense = (
        lax.all_gather(w_qkv, ("dp", "expert"), axis=0, tiled=True),
        lax.all_gather(w_attn_out, ("dp", "expert"), axis=0, tiled=True),
        lax.all_gather(w_shared_in, ("dp", "expert"), axis=0, tiled=True),
        lax.all_gather(w_shared_out, ("dp", "expert"), axis=0, tiled=True),
        lax.all_gather(gain_attn, ("dp", "expert"), axis=0, tiled=True),
        lax.all_gather(gain_ffn, ("dp", "expert"), axis=0, tiled=True),
    )
    qkv_full, out_full, shared_in_full, shared_out_full, gain_first, gain_second = dense
    shared_width = shared_out_full.shape[0]
    score_scale = HEAD_DIM ** (-0.5)
    positions = jnp.arange(row_count)
    cosine, sine_table = rotary_tables(positions, HEAD_DIM)
    length = seq_lengths[0]
    live_rows = positions < length
    allowed = (positions[None, :] <= positions[:, None]) & (positions[None, :] < length)
    head_shape = (row_count, HEADS, HEAD_DIM)
    tokens_f = tokens.astype(jnp.float32)
    scale_first = norm_scale(tokens_f)
    normed_first = (tokens_f * scale_first * gain_first.astype(jnp.float32)).astype(jnp.bfloat16)
    projected = jnp.dot(normed_first, qkv_full, preferred_element_type=jnp.float32)
    queries = rotate(projected[:, :model_width].reshape(head_shape), cosine, sine_table).astype(
        jnp.bfloat16
    )
    key_rows = rotate(
        projected[:, model_width : 2 * model_width].reshape(head_shape), cosine, sine_table
    ).astype(jnp.bfloat16)
    value_rows = projected[:, 2 * model_width :].reshape(head_shape).astype(jnp.bfloat16)
    scores = (
        jnp.einsum("qhd,khd->hqk", queries, key_rows, preferred_element_type=jnp.float32)
        * score_scale
    )
    scores = jnp.where(allowed[None], scores, -1e30)
    row_peak = jnp.max(scores, axis=-1, keepdims=True)
    exp_scores = jnp.exp(scores - row_peak)
    row_sum = jnp.sum(exp_scores, axis=-1, keepdims=True)
    log_total = row_peak + jnp.log(row_sum)
    attention_weights = (exp_scores / row_sum).astype(jnp.bfloat16)
    attended = (
        jnp.einsum(
            "hqk,khd->qhd", attention_weights, value_rows, preferred_element_type=jnp.float32
        )
        .reshape(row_count, model_width)
        .astype(jnp.bfloat16)
    )
    residual = tokens_f + jnp.dot(attended, out_full, preferred_element_type=jnp.float32)
    scale_second = norm_scale(residual)
    normed_second = (residual * scale_second * gain_second.astype(jnp.float32)).astype(jnp.bfloat16)
    shared_gate_up = jnp.dot(normed_second, shared_in_full, preferred_element_type=jnp.float32)
    shared_hidden = swish_product(shared_gate_up, shared_width).astype(jnp.bfloat16)
    layer_sum = residual + jnp.dot(
        shared_hidden, shared_out_full, preferred_element_type=jnp.float32
    )
    flat_ids = route_ids.reshape(assignments)
    flat_live = jnp.repeat(live_rows, TOP)
    chosen = (
        (flat_ids[:, None] == jnp.arange(experts_total)[None, :]) & flat_live[:, None]
    ).astype(jnp.int32)
    before = jnp.cumsum(chosen, axis=0) - chosen
    ranks = jnp.sum(before * chosen, axis=1)
    slot_of = jnp.where(flat_live, flat_ids * capacity + ranks, slots_total)
    source_of = (
        jnp.full((slots_total,), assignments, jnp.int32)
        .at[slot_of]
        .set(jnp.arange(assignments, dtype=jnp.int32), mode="drop")
    )
    counts = lax.psum(jnp.sum(chosen, axis=0), ("dp", "expert"))
    send_rows = jnp.take(normed_second, source_of // TOP, axis=0, mode="fill", fill_value=0)
    received = lax.all_to_all(
        send_rows.reshape(groups, local_experts * capacity, model_width),
        "expert",
        split_axis=0,
        concat_axis=0,
        tiled=True,
    )
    received = received.reshape(groups, local_experts, capacity, model_width)
    expert_gate_up = jnp.einsum(
        "nesd,edf->nesf", received, w_expert_in, preferred_element_type=jnp.float32
    )
    expert_hidden = swish_product(expert_gate_up, hidden_width).astype(jnp.bfloat16)
    expert_result = jnp.einsum(
        "nesf,efd->nesd", expert_hidden, w_expert_out, preferred_element_type=jnp.float32
    ).astype(jnp.bfloat16)
    returned = lax.all_to_all(
        expert_result.reshape(groups, local_experts * capacity, model_width),
        "expert",
        split_axis=0,
        concat_axis=0,
        tiled=True,
    )
    returned = returned.reshape(slots_total, model_width)
    picked = jnp.take(returned, slot_of, axis=0, mode="fill", fill_value=0).reshape(
        row_count, TOP, model_width
    )
    live_gates = route_gates * live_rows.astype(jnp.float32)[:, None]
    routed = jnp.einsum("sk,skd->sd", live_gates, picked.astype(jnp.float32))
    block_out = (layer_sum + routed).astype(jnp.bfloat16)
    gradient = cotangent.astype(jnp.float32)
    again = (
        lax.all_gather(w_qkv, ("dp", "expert"), axis=0, tiled=True),
        lax.all_gather(w_attn_out, ("dp", "expert"), axis=0, tiled=True),
        lax.all_gather(w_shared_in, ("dp", "expert"), axis=0, tiled=True),
        lax.all_gather(w_shared_out, ("dp", "expert"), axis=0, tiled=True),
        lax.all_gather(gain_attn, ("dp", "expert"), axis=0, tiled=True),
        lax.all_gather(gain_ffn, ("dp", "expert"), axis=0, tiled=True),
    )
    qkv_full, out_full, shared_in_full, shared_out_full, gain_first, gain_second = again
    grad_rows = (
        (live_gates[:, :, None] * gradient[:, None, :])
        .astype(jnp.bfloat16)
        .reshape(assignments, model_width)
    )
    send_grad = jnp.take(grad_rows, source_of, axis=0, mode="fill", fill_value=0)
    grad_received = lax.all_to_all(
        send_grad.reshape(groups, local_experts * capacity, model_width),
        "expert",
        split_axis=0,
        concat_axis=0,
        tiled=True,
    )
    grad_received = grad_received.reshape(groups, local_experts, capacity, model_width)
    grad_down = jnp.einsum(
        "nesf,nesd->efd", expert_hidden, grad_received, preferred_element_type=jnp.float32
    )
    grad_hidden = jnp.einsum(
        "nesd,efd->nesf", grad_received, w_expert_out, preferred_element_type=jnp.float32
    )
    grad_gate_up = swish_back(grad_hidden, expert_gate_up, hidden_width).astype(jnp.bfloat16)
    grad_in = jnp.einsum(
        "nesd,nesf->edf", received, grad_gate_up, preferred_element_type=jnp.float32
    )
    grad_back_rows = jnp.einsum(
        "nesf,edf->nesd", grad_gate_up, w_expert_in, preferred_element_type=jnp.float32
    ).astype(jnp.bfloat16)
    grad_returned = lax.all_to_all(
        grad_back_rows.reshape(groups, local_experts * capacity, model_width),
        "expert",
        split_axis=0,
        concat_axis=0,
        tiled=True,
    )
    grad_returned = grad_returned.reshape(slots_total, model_width)
    grad_normed_routed = jnp.sum(
        jnp.take(grad_returned, slot_of, axis=0, mode="fill", fill_value=0)
        .reshape(row_count, TOP, model_width)
        .astype(jnp.float32),
        axis=1,
    )
    grad_in, grad_down = (
        lax.psum(grad_in.astype(jnp.bfloat16), "dp").astype(jnp.float32),
        lax.psum(grad_down.astype(jnp.bfloat16), "dp").astype(jnp.float32),
    )
    grad_shared_out = contract_rows(shared_hidden, gradient)
    grad_shared_hidden = times_transposed(gradient, shared_out_full)
    grad_shared_gate_up = swish_back(grad_shared_hidden, shared_gate_up, shared_width).astype(
        jnp.bfloat16
    )
    grad_shared_in = contract_rows(normed_second, grad_shared_gate_up)
    grad_normed_second = times_transposed(grad_shared_gate_up, shared_in_full) + grad_normed_routed
    grad_residual_part, grad_gain_second = norm_back(
        grad_normed_second, residual, scale_second, gain_second.astype(jnp.float32)
    )
    grad_residual = gradient + grad_residual_part
    grad_out_proj = contract_rows(attended, grad_residual)
    grad_attended = (
        times_transposed(grad_residual, out_full).astype(jnp.bfloat16).reshape(head_shape)
    )
    scores = (
        jnp.einsum("qhd,khd->hqk", queries, key_rows, preferred_element_type=jnp.float32)
        * score_scale
    )
    scores = jnp.where(allowed[None], scores, -1e30)
    attention_probs = jnp.exp(scores - log_total)
    grad_weights = jnp.einsum(
        "qhd,khd->hqk", grad_attended, value_rows, preferred_element_type=jnp.float32
    )
    row_delta = jnp.sum(grad_weights * attention_probs, axis=-1, keepdims=True)
    grad_scores = (attention_probs * (grad_weights - row_delta)).astype(jnp.bfloat16)
    grad_values = jnp.einsum(
        "hqk,qhd->khd",
        attention_probs.astype(jnp.bfloat16),
        grad_attended,
        preferred_element_type=jnp.float32,
    )
    grad_queries = unrotate(
        jnp.einsum("hqk,khd->qhd", grad_scores, key_rows, preferred_element_type=jnp.float32)
        * score_scale,
        cosine,
        sine_table,
    )
    grad_keys = unrotate(
        jnp.einsum("hqk,qhd->khd", grad_scores, queries, preferred_element_type=jnp.float32)
        * score_scale,
        cosine,
        sine_table,
    )
    grad_projected = jnp.concatenate(
        [
            grad_queries.reshape(row_count, model_width),
            grad_keys.reshape(row_count, model_width),
            grad_values.reshape(row_count, model_width),
        ],
        axis=1,
    ).astype(jnp.bfloat16)
    grad_qkv = contract_rows(normed_first, grad_projected)
    grad_normed_first = times_transposed(grad_projected, qkv_full)
    grad_tokens_part, grad_gain_first = norm_back(
        grad_normed_first, tokens_f, scale_first, gain_first.astype(jnp.float32)
    )
    grad_tokens = grad_residual + grad_tokens_part
    shares = (
        lax.psum_scatter(grad_qkv, ("dp", "expert"), scatter_dimension=0, tiled=True),
        lax.psum_scatter(grad_out_proj, ("dp", "expert"), scatter_dimension=0, tiled=True),
        lax.psum_scatter(grad_shared_in, ("dp", "expert"), scatter_dimension=0, tiled=True),
        lax.psum_scatter(grad_shared_out, ("dp", "expert"), scatter_dimension=0, tiled=True),
        lax.psum_scatter(grad_gain_first, ("dp", "expert"), scatter_dimension=0, tiled=True),
        lax.psum_scatter(grad_gain_second, ("dp", "expert"), scatter_dimension=0, tiled=True),
    )
    return (
        block_out,
        grad_tokens,
        shares[0],
        shares[1],
        shares[2],
        shares[3],
        shares[4],
        shares[5],
        grad_in,
        grad_down,
        counts,
    )


def solution(mesh):
    placed = (
        P(("dp", "expert"), None),
        P(("dp", "expert"), None),
        P(("dp", "expert"), None),
        P(("dp", "expert"), None),
        P(("dp", "expert"), None),
        P(("dp", "expert")),
        P(("dp", "expert")),
        P("expert", None, None),
        P("expert", None, None),
        P(("dp", "expert"), None),
        P(("dp", "expert"), None),
        P(("dp", "expert")),
        P(("dp", "expert"), None),
    )
    return jax.shard_map(
        on_device,
        mesh=mesh,
        in_specs=placed,
        out_specs=(
            P(("dp", "expert"), None),
            P(("dp", "expert"), None),
            P(("dp", "expert"), None),
            P(("dp", "expert"), None),
            P(("dp", "expert"), None),
            P(("dp", "expert"), None),
            P(("dp", "expert")),
            P(("dp", "expert")),
            P("expert", None, None),
            P("expert", None, None),
            P(),
        ),
        check_vma=False,
    )
```

profile of v0, /device:TPU:0, one launch (start us, length us, event | category | flops | bytes accessed | tf_op | source)
XLA Modules:
  0.0 2101.3 jit_solution(2690681099844653045)
XLA Ops:
  14.5 4.6 reduce-window.6
  20.9 11.8 scatter_custom_fusion
  33.3 43.2 %all-reduce.7 = (bf16[1280]{0:T(1024)(128)(2,1)S(1)}, bf16[1280]{0:T(1024)(128)(2,1)S(1)}) all-reduce(bf16[1280]{0:T(1024)(128)(2,1)S(1)} %dynamic-update-slice, bf16[1280]{0:T(1024)(128)(2,1)S(1)} %dynamic-update-slice.1), channel_id=1, replica_groups=mesh['dp'=4,'expert'=8] {'dp','expert'}, use_global_device_ids=true, to_apply=%add | all-reduce | flops 2560 | bytes 10240
  77.8 21.2 %all-gather.6.cloned.1.call-done = bf16[1280,3840]{1,0:T(8,128)(2,1)} async-done(((bf16[40,3840]{1,0:T(8,128)(2,1)}), bf16[1280,3840]{1,0:T(8,128)(2,1)}) %all-gather.6.cloned.1.call-update) | async-done | bytes 9830416 | tf_op jit(solution)/shard_map/all_gather | solution.py:104
  99.0 7.7 fusion.51
  112.8 3.5 fusion.70
  125.5 3.6 fusion.71
  136.5 4.8 subtract_convert_fusion.3
  151.4 8.3 all-gather.8.cloned.1.call-done
  159.8 4.1 multiply_reduce_fusion.3
  165.6 13.1 gather_fusion
  178.8 9.6 broadcast_select_fusion.1
  188.4 5.2 all-to-all-start
  194.0 7.5 mul.561
  201.5 18.4 mul.562
  220.0 8.8 multiply_convert_fusion
  228.8 24.7 %gather_fusion.1 = bf16[3840,1280]{1,0:T(8,128)(2,1)} fusion(bf16[3072,1280]{1,0:T(8,128)(2,1)} %multiply_convert_fusion, s32[4096]{0:T(1024)S(1)} %pad_clamp_fusion), kind=kCustom, calls=%fused_computation.3 | custom fusion | bytes 19676160 | tf_op jit(solution)/shard_map/jit(_take)/gather | solution.py:215
  253.5 9.6 broadcast_select_fusion
  263.1 145.2 %all-to-all-done = bf16[8,480,1280]{2,1,0:T(8,128)(2,1)} async-done(((bf16[8,480,1280]{2,1,0:T(8,128)(2,1)}), bf16[8,480,1280]{2,1,0:T(8,128)(2,1)}, u32[]{:S(2)}, u32[]{:S(2)}) %all-to-all-start) | async-done | bytes 9830432 | tf_op jit(solution)/shard_map/all_to_all | solution.py:171
  408.3 5.5 all-to-all-start.2
  413.8 25.8 %convolution_bitcast_fusion = f32[8,2,240,1792]{3,2,0,1:T(8,128)} fusion(bf16[8,2,240,1280]{3,2,1,0:T(8,128)(2,1)} %bitcast.12, bf16[2,1280,1792]{2,1,0:T(8,128)(2,1)} %param.22), kind=kOutput, calls=%fused_computation.19 | convolution fusion | flops 17616076800 | bytes 46530560 | tf_op jit(solution)/shard_map/nesd,edf->nesf/dot_general | solution.py:179
  439.6 188.1 %all-to-all-done.2 = bf16[8,480,1280]{2,1,0:T(8,128)(2,1)} async-done(((bf16[8,480,1280]{2,1,0:T(8,128)(2,1)}), bf16[8,480,1280]{2,1,0:T(8,128)(2,1)}, u32[]{:S(2)}, u32[]{:S(2)}) %all-to-all-start.2) | async-done | bytes 9830432 | tf_op jit(solution)/shard_map/all_to_all | solution.py:216
  627.7 28.3 %fusion.3 = (bf16[8,2,240,896]{3,2,0,1:T(8,128)(2,1)}, bf16[8,2,240,896]{3,2,0,1:T(8,128)(2,1)}, bf16[8,2,240,896]{3,2,0,1:T(8,128)(2,1)}) fusion(f32[8,2,240,1792]{3,2,0,1:T(8,128)} %convolution_bitcast_fusion, bf16[2,896,1280]{2,1,0:T(8,128)(2,1)} %param.23, bf16[8,2,240,1280]{3,2,1,0:T(8,128)(2,1)} %bitcast.23), kind=kOutput, calls=%fused_computation.12 | convolution fusion | flops 8863088640 | bytes 62586880 | tf_op jit(solution)/shard_map/nesd,efd->nesf/dot_general | solution.py:227
  656.0 16.1 fusion.18
  672.1 8.2 copy.82
  680.3 5.1 all-to-all-start.1
  686.8 15.0 bitcast_convert_fusion.1
  701.8 25.1 %bitcast_convert_fusion = bf16[2,1280,1792]{2,1,0:T(8,128)(2,1)} fusion(bf16[8,2,240,1280]{3,2,1,0:T(8,128)(2,1)} %bitcast.12, bf16[8,2,240,896]{3,2,0,1:T(8,128)(2,1)} %get-tuple-element.27, bf16[8,2,240,896]{3,2,0,1:T(8,128)(2,1)} %get-tuple-element.26), kind=kOutput, calls=%fused_computation.5 | convolution fusion | flops 17648189440 | bytes 32768000 | tf_op jit(solution)/shard_map/nesd,nesf->edf/dot_general | solution.py:231
  726.9 25.3 %fusion.19 = bf16[8,2,240,1280]{3,2,0,1:T(8,128)(2,1)} fusion(bf16[2,1280,1792]{2,1,0:T(8,128)(2,1)} %param.22, bf16[8,2,240,896]{3,2,0,1:T(8,128)(2,1)} %get-tuple-element.27, bf16[8,2,240,896]{3,2,0,1:T(8,128)(2,1)} %get-tuple-element.26), kind=kOutput, calls=%fused_computation.40 | convolution fusion | flops 17648517120 | bytes 32768000 | tf_op jit(solution)/shard_map/nesf,edf->nesd/dot_general | solution.py:234
  752.2 8.1 copy.85
  760.3 143.5 %all-to-all-done.1 = bf16[8,480,1280]{2,1,0:T(8,128)(2,1)} async-done(((bf16[8,480,1280]{2,1,0:T(8,128)(2,1)}), bf16[8,480,1280]{2,1,0:T(8,128)(2,1)}, u32[]{:S(2)}, u32[]{:S(2)}) %all-to-all-start.1) | async-done | bytes 9830432 | tf_op jit(solution)/shard_map/all_to_all | solution.py:186
  903.8 5.1 all-to-all-start.3
  908.9 67.4 %all-gather.12.cloned.1.call-done = bf16[32,28,1280]{2,1,0:T(8,128)(2,1)} async-done(((bf16[1,28,1280]{2,1,0:T(8,128)(2,1)}), bf16[32,28,1280]{2,1,0:T(8,128)(2,1)}) %all-gather.12.cloned.1.call-update) | async-done | bytes 2293776 | tf_op jit(solution)/shard_map/all_gather | solution.py:107
  976.4 4.1 reshape.380
  980.4 193.5 %all-gather.10.cloned.1.call-done = bf16[1280,1792]{1,0:T(8,128)(2,1)} async-done(((bf16[40,1792]{1,0:T(8,128)(2,1)}), bf16[1280,1792]{1,0:T(8,128)(2,1)}) %all-gather.10.cloned.1.call-update) | async-done | bytes 4587536 | tf_op jit(solution)/shard_map/all_gather | solution.py:106
  1174.0 5.0 fusion.73
  1182.4 6.0 fusion.48
  1189.1 22.6 %gather_fusion.2 = bf16[3072,1280]{1,0:T(8,128)(2,1)} fusion(bf16[3840,1280]{1,0:T(8,128)(2,1)} %bitcast.20, s32[3072]{0:T(1024)S(1)} %broadcast_clamp_fusion), kind=kCustom, calls=%fused_computation.clone | custom fusion | bytes 15740928 | tf_op jit(solution)/shard_map/jit(_take)/gather | solution.py:194
  1211.7 22.7 %gather_fusion.3 = bf16[3072,1280]{1,0:T(8,128)(2,1)} fusion(bf16[3840,1280]{1,0:T(8,128)(2,1)} %bitcast.29, s32[3072]{0:T(1024)S(1)} %broadcast_clamp_fusion), kind=kCustom, calls=%fused_computation.1.clone | custom fusion | bytes 15740928 | tf_op jit(solution)/shard_map/jit(_take)/gather | solution.py:246
  1234.4 15.5 select_convert_fusion
  1249.9 17.8 reshape.330
  1267.6 12.5 reduce_sum.106
  1280.2 7.3 multiply_reduce_fusion.1
  1289.7 4.7 fusion.75
  1295.9 5.7 fusion.77
  1304.3 11.4 multiply_reduce_fusion
  1315.8 6.4 multiply_convert_fusion.2
  1339.3 6.4 fusion.45
  1346.8 13.1 fusion.42
  1360.6 39.9 %psum.23 = s32[16]{0:T(128)} all-reduce(s32[16]{0:T(128)S(1)} %copy-done.63), channel_id=1, replica_groups=mesh['dp'=4,'expert'=8] {'dp','expert'}, use_global_device_ids=true, to_apply=%region_23.25 | all-reduce | flops 16 | bytes 128 | tf_op jit(solution)/shard_map/psum | solution.py:169
  1400.5 4.8 fusion.76
  1405.4 212.1 %fusion = f32[32,1280]{1,0:T(8,128)S(1)} fusion(f32[896,1280]{1,0:T(8,128)} %fusion.76), kind=kCustom, calls=%all-reduce-scatter | all-reduce-scatter fusion | flops 1310721 | bytes 4751360
  1620.1 6.7 collective-permute-start.1
  1630.6 10.2 collective-permute-done.3
  1640.8 7.0 concatenate.35
  1649.4 11.7 convert_element_type.174
  1661.2 6.8 convert_element_type.176
  1668.1 11.1 fusion.41
  1679.1 61.0 %all-reduce.6 = (f32[1280]{0:T(1024)S(1)}, f32[1280]{0:T(1024)S(1)}) all-reduce(f32[1280]{0:T(1024)S(1)} %get-tuple-element.14, f32[1280]{0:T(1024)S(1)} %copy-done.58), channel_id=6, replica_groups=mesh['dp'=4,'expert'=8] {'dp','expert'}, use_global_device_ids=true, to_apply=%region_17.19.clone | all-reduce | flops 2560 | bytes 20480
  1741.3 13.1 reshape.322
  1754.4 8.6 fusion.74
  1763.0 5.2 fusion.32
  1770.4 105.6 %reduce-scatter.8.cloned.1.call-done = f32[40,1280]{1,0:T(8,128)} async-done(((f32[1280,1280]{1,0:T(8,128)}), f32[40,1280]{1,0:T(8,128)}) %reduce-scatter.8.cloned.1.call-update) | async-done | bytes 204816 | tf_op jit(solution)/shard_map/reduce_scatter | solution.py:315
  1876.0 218.0 %reduce-scatter.6.cloned.1.call-done = f32[40,3840]{1,0:T(8,128)} async-done(((f32[1280,3840]{1,0:T(8,128)}), f32[40,3840]{1,0:T(8,128)}) %reduce-scatter.6.cloned.1.call-update) | async-done | bytes 614416 | tf_op jit(solution)/shard_map/reduce_scatter | solution.py:314
  (243 shorter events, 87.1 us)
Async XLA Ops:
  7.2 25.6 %copy-start.64 = (bf16[40]{0:T(256)(128)(2,1)S(1)}, bf16[40]{0:T(256)(128)(2,1)}, u32[]{:S(2)}) copy-start(bf16[40]{0:T(256)(128)(2,1)} %param.20) | copy-start | bytes 244
  7.2 25.9 %copy-start.65 = (bf16[40]{0:T(256)(128)(2,1)S(1)}, bf16[40]{0:T(256)(128)(2,1)}, u32[]{:S(2)}) copy-start(bf16[40]{0:T(256)(128)(2,1)} %param.21) | copy-start | bytes 244
  7.2 91.8 %all-gather.6.cloned.1.call-start = ((), (), s32[]{:S(2)}) async-start(), calls=%async_computation.7 | async-start | bytes 10137600 | tf_op jit(solution)/shard_map/all_gather | solution.py:104
  7.9 151.8 %all-gather.8.cloned.1.call-start = ((), (), s32[]{:S(2)}) async-start(), calls=%async_computation.8 | async-start | bytes 3379200 | tf_op jit(solution)/shard_map/all_gather | solution.py:105
  9.3 184.3 %copy-start.54 = (f32[512]{0:T(512)}, f32[512]{0:T(512)S(1)}, u32[]{:S(2)}) copy-start(f32[512]{0:T(512)S(1)} %get-tuple-element.68) | copy-start | bytes 6148
  9.9 67.8 %copy-start.50 = (pred[3072]{0:T(1024)(128)(4,1)}, pred[3072]{0:T(1024)(128)(4,1)S(1)}, u32[]{:S(2)}) copy-start(pred[3072]{0:T(1024)(128)(4,1)S(1)} %and.50) | copy-start | bytes 9220
  9.9 89.1 %copy-start.9 = (bf16[512,1280]{1,0:T(8,128)(2,1)S(1)}, bf16[512,1280]{1,0:T(8,128)(2,1)}, u32[]{:S(2)}) copy-start(bf16[512,1280]{1,0:T(8,128)(2,1)} %param.15) | copy-start | bytes 3932164
  11.2 87.7 %copy-start.41 = (s32[3072]{0:T(1024)}, s32[3072]{0:T(1024)S(1)}, u32[]{:S(2)}) copy-start(s32[3072]{0:T(1024)S(1)} %eq.25) | copy-start | bytes 36868
  14.4 84.5 %copy-start.60 = (f32[512]{0:T(512)}, f32[512]{0:T(512)S(1)}, u32[]{:S(2)}) copy-start(f32[512]{0:T(512)S(1)} %get-tuple-element.56) | copy-start | bytes 6148
  20.9 78.1 %copy-start.43 = (s32[3072]{0:T(1024)}, s32[3072]{0:T(1024)S(1)}, u32[]{:S(2)}) copy-start(s32[3072]{0:T(1024)S(1)} %get-tuple-element.17) | copy-start | bytes 36868
  76.5 22.5 %copy-start.52 = (f32[1280]{0:T(1024)}, f32[1280]{0:T(1024)S(1)}, u32[]{:S(2)}) copy-start(f32[1280]{0:T(1024)S(1)} %convert_element_type.146) | copy-start | bytes 15364
  76.5 88.0 %copy-start.46 = (f32[1280]{0:T(1024)}, f32[1280]{0:T(1024)S(1)}, u32[]{:S(2)}) copy-start(f32[1280]{0:T(1024)S(1)} %convert_element_type.154) | copy-start | bytes 15364
  77.8 58.8 %copy-start.26 = (f32[512,64]{1,0:T(8,128)}, f32[512,64]{1,0:T(8,128)S(1)}, u32[]{:S(2)}) copy-start(f32[512,64]{1,0:T(8,128)S(1)} %get-tuple-element.53) | copy-start | bytes 393220
  77.8 58.8 %copy-start.28 = (f32[512,64]{1,0:T(8,128)}, f32[512,64]{1,0:T(8,128)S(1)}, u32[]{:S(2)}) copy-start(f32[512,64]{1,0:T(8,128)S(1)} %get-tuple-element.54) | copy-start | bytes 393220
  151.4 12.4 copy-start.7
  164.5 14.3 copy-start.56
  165.6 13.1 copy-start
  188.4 5.2 copy-start.48
  188.4 5.6 copy-start.21
  188.4 219.9 %all-to-all-start = ((bf16[8,480,1280]{2,1,0:T(8,128)(2,1)}), bf16[8,480,1280]{2,1,0:T(8,128)(2,1)}, u32[]{:S(2)}, u32[]{:S(2)}) async-start(bf16[8,480,1280]{2,1,0:T(8,128)(2,1)} %broadcast_select_fusion.1), calls=%async_computation | async-start | bytes 19660800 | tf_op jit(solution)/shard_map/all_to_all | solution.py:171
  408.3 219.4 %all-to-all-start.2 = ((bf16[8,480,1280]{2,1,0:T(8,128)(2,1)}), bf16[8,480,1280]{2,1,0:T(8,128)(2,1)}, u32[]{:S(2)}, u32[]{:S(2)}) async-start(bf16[8,480,1280]{2,1,0:T(8,128)(2,1)} %broadcast_select_fusion), calls=%async_computation.2 | async-start | bytes 19660800 | tf_op jit(solution)/shard_map/all_to_all | solution.py:216
  680.3 223.5 %all-to-all-start.1 = ((bf16[8,480,1280]{2,1,0:T(8,128)(2,1)}), bf16[8,480,1280]{2,1,0:T(8,128)(2,1)}, u32[]{:S(2)}, u32[]{:S(2)}) async-start(bf16[8,480,1280]{2,1,0:T(8,128)(2,1)} %bitcast.116), calls=%async_computation.1 | async-start | bytes 19660800 | tf_op jit(solution)/shard_map/all_to_all | solution.py:186
  685.4 290.9 %all-gather.12.cloned.1.call-start = ((), (), s32[]{:S(2)}) async-start(), calls=%async_computation.13 | async-start | bytes 2703360 | tf_op jit(solution)/shard_map/all_gather | solution.py:107
  686.2 487.8 %all-gather.10.cloned.1.call-start = ((), (), s32[]{:S(2)}) async-start(), calls=%async_computation.9 | async-start | bytes 4730880 | tf_op jit(solution)/shard_map/all_gather | solution.py:106
  686.7 962.7 %all-reduce.11.cloned.1.call-start = ((), (), s32[]{:S(2)}) async-start(), calls=%async_computation.14 | async-start | bytes 27525120 | tf_op jit(solution)/shard_map/psum | solution.py:252
  903.8 307.9 %all-to-all-start.3 = ((bf16[8,480,1280]{2,1,0:T(8,128)(2,1)}), bf16[8,480,1280]{2,1,0:T(8,128)(2,1)}, u32[]{:S(2)}, u32[]{:S(2)}) async-start(bf16[8,480,1280]{2,1,0:T(8,128)(2,1)} %bitcast.117), calls=%async_computation.3 | async-start | bytes 19660800 | tf_op jit(solution)/shard_map/all_to_all | solution.py:237
  908.8 265.1 %copy-start.1 = (bf16[512,1280]{1,0:T(8,128)(2,1)S(1)}, bf16[512,1280]{1,0:T(8,128)(2,1)}, u32[]{:S(2)}) copy-start(bf16[512,1280]{1,0:T(8,128)(2,1)} %copy-done) | copy-start | bytes 3932164
  908.9 861.5 %reduce-scatter.10.cloned.1.call-start = ((), (), s32[]{:S(2)}) async-start(), calls=%async_computation.12 | async-start | bytes 9461760 | tf_op jit(solution)/shard_map/reduce_scatter | solution.py:316
  980.4 198.5 %copy-start.22 = (bf16[512,1280]{1,0:T(8,128)(2,1)S(1)}, bf16[512,1280]{1,0:T(8,128)(2,1)}, u32[]{:S(2)}) copy-start(bf16[512,1280]{1,0:T(8,128)(2,1)} %param.27) | copy-start | bytes 3932164
  1181.1 219.4 %copy-start.37 = (bf16[512,896]{1,0:T(8,128)(2,1)}, bf16[512,896]{1,0:T(8,128)(2,1)S(1)}, u32[]{:S(2)}) copy-start(bf16[512,896]{1,0:T(8,128)(2,1)S(1)} %get-tuple-element.37) | copy-start | bytes 2752516
  1188.4 687.6 %reduce-scatter.8.cloned.1.call-start = ((), (), s32[]{:S(2)}) async-start(), calls=%async_computation.11 | async-start | bytes 6758400 | tf_op jit(solution)/shard_map/reduce_scatter | solution.py:315
  1267.6 12.5 copy-start.4
  1267.6 12.5 copy-start.47
  1267.6 12.5 copy-start.57
  1280.1 7.4 copy-start.23
  1280.2 7.4 copy-start.62
  1294.4 799.5 %reduce-scatter.6.cloned.1.call-start = ((), (), s32[]{:S(2)}) async-start(), calls=%async_computation.10 | async-start | bytes 20275200 | tf_op jit(solution)/shard_map/reduce_scatter | solution.py:314
  1304.3 11.4 slice-start
  1304.3 11.4 slice-start.1
  1304.3 11.4 slice-start.2
  1304.3 11.4 copy-start.39
  1315.8 6.4 copy-start.18
  1315.8 6.4 copy-start.20
  1339.3 7.5 copy-start.10
  1339.3 7.5 copy-start.33
  1339.3 7.5 copy-start.35
  1339.3 7.5 copy-start.53
  1339.3 7.5 copy-start.61
  1405.4 224.2 %copy-start.49 = (f32[512,6]{0,1:T(8,128)S(1)}, f32[512,6]{0,1:T(8,128)}, u32[]{:S(2)}) copy-start(f32[512,6]{0,1:T(8,128)} %param.25) | copy-start | bytes 36868
  1405.4 224.2 %copy-start.55 = (f32[512]{0:T(512)S(1)}, f32[512]{0:T(512)}, u32[]{:S(2)}) copy-start(f32[512]{0:T(512)} %copy-done.54) | copy-start | bytes 6148
  1618.2 22.7 %collective-permute-start = (f32[32,1280]{1,0:T(8,128)S(1)}, f32[32,1280]{1,0:T(8,128)S(1)}, u32[]{:S(2)}, u32[]{:S(2)}) collective-permute-start(f32[32,1280]{1,0:T(8,128)S(1)} %fusion), channel_id=1, source_target_pairs={{0,1},{1,2},{2,3},{3,4},{4,5},{5,6},{6,7},{7,8},{8,9},{9,10},{10,1... | collective-permute-start | bytes 491528
  1620.1 20.7 collective-permute-start.1
  1626.9 13.9 collective-permute-start.2
  1628.3 12.6 collective-permute-start.3
  1661.2 6.8 copy-start.11
  1661.2 6.8 copy-start.32
  1661.2 6.8 copy-start.34
  1661.2 6.8 copy-start.36
  1668.0 11.1 copy-start.58
  1754.4 8.6 copy-start.38
  1763.0 5.2 copy-start.6
  1763.0 5.2 copy-start.12
  1763.0 5.2 copy-start.25
  1763.0 5.2 copy-start.59
  (23 other events, 54.9 us)
Sparse Core Ops, SparseCore 0:
  10.9 87.9 all-gather.5
  101.8 57.9 all-gather.7
  689.2 287.1 all-gather.11
  979.1 194.7 all-gather.9
  1177.0 239.7 all-reduce.10
  1419.7 301.9 reduce-scatter.9
  1724.7 151.3 reduce-scatter.7
  1884.1 209.7 reduce-scatter.5
where the time goes:
time: 2110 us; the launch traced here: 2100 us
  waiting for transfers between devices  1100 us (52%)
  blocking collectives  356 us (17%)
  matrix products  249 us (12%)
  local copies, waits for them, and re-layouts  233 us (11%)
  other arithmetic  111 us (5%)
  starting transfers between devices  33.1 us (2%)
    unnamed x3, blocking collectives  316 us
    reduce_scatter x1, waiting for transfers between devices, on_device(): lax.psum_scatter(grad_qkv, ('dp', 'expert'), scatter_dimension=0, tiled=T...  218 us
    all_gather x1, waiting for transfers between devices, on_device(): lax.all_gather(w_shared_in, ('dp', 'expert'), axis=0, tiled=True)  194 us
    all_to_all x1, waiting for transfers between devices, on_device(): lax.all_to_all(send_grad.reshape(groups, local_experts * capacity, model_...  188 us
    all_to_all x1, waiting for transfers between devices, on_device(): lax.all_to_all(send_rows.reshape(groups, local_experts * capacity, model_...  145 us
    all_to_all x1, waiting for transfers between devices, on_device(): lax.all_to_all(expert_result.reshape(groups, local_experts * capacity, mo...  143 us
    reduce_scatter x1, waiting for transfers between devices, on_device(): lax.psum_scatter(grad_out_proj, ('dp', 'expert'), scatter_dimension=0, ti...  106 us
    all_gather x1, waiting for transfers between devices, on_device(): lax.all_gather(w_shared_out, ('dp', 'expert'), axis=0, tiled=True)  67.4 us
  transfers between devices with their start and end apart: 16, of which 10 were waited for; matrix products, arithmetic and copies ran while one was open for 34% of the time, Pallas kernels for 0%

commit v1 on v0

v1 whole, which is shorter than its diff:
```python
import functools

import jax
import jax.numpy as jnp
from jax import lax
from jax.experimental import pallas as pl
from jax.experimental.pallas import tpu as pltpu
from jax.sharding import PartitionSpec as P

HEADS = 10
HEAD_DIM = 128
TOP = 6
norm_eps = 1e-06

BF = jnp.bfloat16
F32 = jnp.float32
BOTH = ("dp", "expert")


def rotary_tables(positions, head_dim):
    half_dim = head_dim // 2
    frequencies = 10000.0 ** (-(2.0 * jnp.arange(half_dim, dtype=F32)) / head_dim)
    angles = positions.astype(F32)[:, None] * frequencies[None, :]
    return (jnp.cos(angles)[:, None, :], jnp.sin(angles)[:, None, :])


def rotate(head_rows, cosine, sine_table):
    half_dim = head_rows.shape[-1] // 2
    first_half = head_rows[..., :half_dim]
    second = head_rows[..., half_dim:]
    return jnp.concatenate(
        [first_half * cosine - second * sine_table, second * cosine + first_half * sine_table],
        axis=-1,
    )


def unrotate(head_grads, cosine, sine_table):
    return rotate(head_grads, cosine, -sine_table)


def contract_rows(left, right):
    return lax.dot_general(left, right, (((0,), (0,)), ((), ())), preferred_element_type=F32)


def times_transposed(left, right):
    return lax.dot_general(left, right, (((1,), (1,)), ((), ())), preferred_element_type=F32)


def swish_product(gate_up, hidden_width):
    gate_part = gate_up[..., :hidden_width]
    return gate_part * jax.nn.sigmoid(gate_part) * gate_up[..., hidden_width:]


def swish_back(grad_hidden, gate_up, hidden_width):
    gate_part = gate_up[..., :hidden_width]
    up_part = gate_up[..., hidden_width:]
    sigmoid_gate = jax.nn.sigmoid(gate_part)
    grad_gate = grad_hidden * up_part * sigmoid_gate * (1.0 + gate_part * (1.0 - sigmoid_gate))
    grad_up = grad_hidden * gate_part * sigmoid_gate
    return jnp.concatenate([grad_gate, grad_up], axis=-1)


def norm_scale(activation):
    return lax.rsqrt(jnp.mean(activation * activation, axis=-1, keepdims=True) + norm_eps)


def norm_back(grad_normed, activation, row_scale, norm_gain):
    weighted = grad_normed * norm_gain
    grad_input = row_scale * weighted - activation * row_scale**3 * jnp.mean(
        weighted * activation, axis=-1, keepdims=True
    )
    return (grad_input, jnp.sum(grad_normed * activation * row_scale, axis=0))


def dot(left, right, left_dim=1, right_dim=0):
    return lax.dot_general(
        left, right, (((left_dim,), (right_dim,)), ((), ())), preferred_element_type=F32
    )


def expert_body(
    rank_ref, gate_ref, rows_ref, grads_ref, win_ref, wout_ref,
    pdx_ref, pout_ref, x_ref, h_ref, gr_ref, dgu_ref, *, capacity, hidden,
):
    experts = win_ref.shape[0]
    slot = lax.broadcasted_iota(jnp.int32, (capacity, rows_ref.shape[1]), 0)
    rows, grads = rows_ref[0], grads_ref[0]
    picks, back_rows, results = [], [], []
    for e in range(experts):
        mask = slot == rank_ref[0, e : e + 1, :]
        pick = jnp.where(mask, 1.0, 0.0).astype(BF)
        gate_col = jnp.sum(
            jnp.where(mask, gate_ref[0, e : e + 1, :], 0.0), axis=1, keepdims=True
        )
        x = dot(pick, rows).astype(BF)
        x_ref[e, 0] = x
        gate_up = dot(x, win_ref[e])
        a, b = gate_up[:, :hidden], gate_up[:, hidden:]
        s = jax.nn.sigmoid(a)
        swish = a * s
        h = (swish * b).astype(BF)
        h_ref[e, 0] = h
        gr = (dot(pick, grads) * gate_col).astype(BF)
        gr_ref[e, 0] = gr
        gh = dot(gr, wout_ref[e], 1, 1)
        dgu_ref[e, 0, :, :hidden] = (gh * b * s * (1.0 + a * (1.0 - s))).astype(BF)
        dgu_ref[e, 0, :, hidden:] = (gh * swish).astype(BF)
        back_rows.append(dot(dgu_ref[e, 0], win_ref[e], 1, 1).astype(BF))
        results.append((dot(h, wout_ref[e]) * gate_col).astype(BF))
        picks.append(pick)
    picks = jnp.concatenate(picks, axis=0)
    pdx_ref[0] = dot(picks, jnp.concatenate(back_rows, axis=0), 0, 0).astype(BF)
    pout_ref[0] = dot(picks, jnp.concatenate(results, axis=0), 0, 0).astype(BF)


def expert_rows(rank, gate, rows, grads, w_in, w_out, capacity):
    n, row_count, width = rows.shape
    experts, hidden, _ = w_out.shape
    full = lambda shape: pl.BlockSpec(
        shape, lambda i: (0,) * len(shape), pipeline_mode=pl.Buffered(1)
    )
    block = lambda *shape: pl.BlockSpec((1,) + shape, lambda i: (i, 0, 0))
    slots = lambda w: pl.BlockSpec((experts, 1, capacity, w), lambda i: (0, i, 0, 0))
    widths = (width, hidden, width, 2 * hidden)
    return pl.pallas_call(
        functools.partial(expert_body, capacity=capacity, hidden=hidden),
        grid=(n,),
        in_specs=[
            block(experts, row_count),
            block(experts, row_count),
            block(row_count, width),
            block(row_count, width),
            full(w_in.shape),
            full(w_out.shape),
        ],
        out_specs=[block(row_count, width), block(row_count, width)] + [slots(w) for w in widths],
        out_shape=[jax.ShapeDtypeStruct((n, row_count, width), BF)] * 2
        + [jax.ShapeDtypeStruct((experts, n, capacity, w), BF) for w in widths],
        compiler_params=pltpu.CompilerParams(vmem_limit_bytes=60 * 2**20),
        cost_estimate=pl.CostEstimate(
            flops=n * 9_300_000_000, bytes_accessed=n * 8_000_000 + 14_000_000, transcendentals=0
        ),
        name="expert_rows",
    )(rank, gate, rows, grads, w_in, w_out)


def sum_over_dp(array):
    count = lax.axis_size("dp")
    index = lax.axis_index("dp")
    core = index % 2
    swap = [(i, i ^ 1) for i in range(count)]
    first, second = array[0], array[1]
    mine = jnp.where(core == 0, first, second)
    other = jnp.where(core == 0, second, first)
    got = lax.ppermute(other, "dp", swap)
    total = (mine.astype(F32) + got.astype(F32)).astype(BF)
    step = 2
    while step < count:
        got = lax.ppermute(total, "dp", [(i, i ^ step) for i in range(count)])
        total = (total.astype(F32) + got.astype(F32)).astype(BF)
        step *= 2
    got = lax.ppermute(total, "dp", swap)
    return jnp.stack(
        [jnp.where(core == 0, total, got), jnp.where(core == 0, got, total)]
    ).astype(F32)


def on_device(
    tokens, w_qkv, w_attn_out, w_shared_in, w_shared_out, gain_attn, gain_ffn,
    w_expert_in, w_expert_out, route_ids, route_gates, seq_lengths, cotangent,
):
    row_count, model_width = tokens.shape
    groups = lax.axis_size("expert")
    local_experts = w_expert_in.shape[0]
    experts_total = local_experts * groups
    capacity = row_count * TOP * 5 // (4 * experts_total)

    qkv_full = lax.all_gather(w_qkv, BOTH, axis=0, tiled=True)
    out_full = lax.all_gather(w_attn_out, BOTH, axis=0, tiled=True)
    shared_in_full = lax.all_gather(w_shared_in, BOTH, axis=0, tiled=True)
    shared_out_full = lax.all_gather(w_shared_out, BOTH, axis=0, tiled=True)
    gains = lax.all_gather(jnp.stack([gain_attn, gain_ffn]), BOTH, axis=1, tiled=True)
    gain_first, gain_second = gains[0].astype(F32), gains[1].astype(F32)
    shared_width = shared_out_full.shape[0]
    score_scale = HEAD_DIM ** (-0.5)

    positions = jnp.arange(row_count)
    cosine, sine_table = rotary_tables(positions, HEAD_DIM)
    length = seq_lengths[0]
    live_rows = positions < length
    live_ids = jnp.where(live_rows[:, None], route_ids, -1).T
    counts = lax.psum(
        jnp.sum(
            (live_ids[:, :, None] == jnp.arange(experts_total)[None, None, :]).astype(jnp.int32),
            axis=(0, 1),
        ),
        BOTH,
    )
    routes = lax.all_gather(
        jnp.concatenate([live_ids.astype(F32), route_gates.T], axis=0), "expert", axis=0
    )
    mine = (
        lax.axis_index("expert") * local_experts + jnp.arange(local_experts)
    ).astype(F32)
    chosen = routes[:, None, :TOP, :] == mine[None, :, None, None]
    slot_gate = jnp.sum(jnp.where(chosen, routes[:, None, TOP:, :], 0.0), axis=2)
    named = jnp.any(chosen, axis=2)
    earlier = (positions[:, None] < positions[None, :]).astype(BF)
    rank = jnp.dot(
        named.astype(BF).reshape(groups * local_experts, row_count),
        earlier,
        preferred_element_type=F32,
    ).reshape(named.shape)
    slot_rank = jnp.where(named, rank.astype(jnp.int32), -1)
    grads_all = lax.all_gather(cotangent, "expert", axis=0)

    allowed = (positions[None, :] <= positions[:, None]) & (positions[None, :] < length)
    head_shape = (row_count, HEADS, HEAD_DIM)
    tokens_f = tokens.astype(F32)
    scale_first = norm_scale(tokens_f)
    normed_first = (tokens_f * scale_first * gain_first).astype(BF)
    projected = jnp.dot(normed_first, qkv_full, preferred_element_type=F32)
    queries = rotate(projected[:, :model_width].reshape(head_shape), cosine, sine_table).astype(BF)
    key_rows = rotate(
        projected[:, model_width : 2 * model_width].reshape(head_shape), cosine, sine_table
    ).astype(BF)
    value_rows = projected[:, 2 * model_width :].reshape(head_shape).astype(BF)
    scores = (
        jnp.einsum("qhd,khd->hqk", queries, key_rows, preferred_element_type=F32) * score_scale
    )
    scores = jnp.where(allowed[None], scores, -1e30)
    row_peak = jnp.max(scores, axis=-1, keepdims=True)
    exp_scores = jnp.exp(scores - row_peak)
    row_sum = jnp.sum(exp_scores, axis=-1, keepdims=True)
    log_total = row_peak + jnp.log(row_sum)
    attention_weights = (exp_scores / row_sum).astype(BF)
    attended = (
        jnp.einsum("hqk,khd->qhd", attention_weights, value_rows, preferred_element_type=F32)
        .reshape(row_count, model_width)
        .astype(BF)
    )
    residual = tokens_f + jnp.dot(attended, out_full, preferred_element_type=F32)
    scale_second = norm_scale(residual)
    normed_second = (residual * scale_second * gain_second).astype(BF)

    rows_all = lax.all_gather(normed_second, "expert", axis=0)
    part_back, part_out, x, hidden, result_grad, gate_up_grad = expert_rows(
        slot_rank, slot_gate, rows_all, grads_all, w_expert_in, w_expert_out, capacity
    )
    flat = lambda a: a.reshape(groups * row_count, model_width)
    routed_back = lax.psum_scatter(flat(part_back), "expert", scatter_dimension=0, tiled=True)
    routed_out = lax.psum_scatter(flat(part_out), "expert", scatter_dimension=0, tiled=True)
    grad_in = jnp.einsum("esrd,esrf->edf", x, gate_up_grad, preferred_element_type=F32)
    grad_down = jnp.einsum("esrf,esrd->efd", hidden, result_grad, preferred_element_type=F32)
    grad_in = sum_over_dp(grad_in.astype(BF))
    grad_down = sum_over_dp(grad_down.astype(BF))

    gradient = cotangent.astype(F32)
    shared_gate_up = jnp.dot(normed_second, shared_in_full, preferred_element_type=F32)
    shared_hidden = swish_product(shared_gate_up, shared_width).astype(BF)
    layer_sum = residual + jnp.dot(shared_hidden, shared_out_full, preferred_element_type=F32)
    grad_shared_out = contract_rows(shared_hidden, cotangent)
    grad_shared_hidden = times_transposed(cotangent, shared_out_full)
    grad_shared_gate_up = swish_back(grad_shared_hidden, shared_gate_up, shared_width).astype(BF)
    grad_shared_in = contract_rows(normed_second, grad_shared_gate_up)
    block_out = (layer_sum + routed_out.astype(F32)).astype(BF)

    scatter = lambda a: lax.psum_scatter(
        a.astype(BF), BOTH, scatter_dimension=0, tiled=True
    ).astype(F32)
    share_shared_in = scatter(grad_shared_in)
    share_shared_out = scatter(grad_shared_out)

    grad_normed_second = times_transposed(grad_shared_gate_up, shared_in_full) + routed_back.astype(
        F32
    )
    grad_residual_part, grad_gain_second = norm_back(
        grad_normed_second, residual, scale_second, gain_second
    )
    grad_residual = gradient + grad_residual_part
    grad_residual_low = grad_residual.astype(BF)
    share_out = scatter(contract_rows(attended, grad_residual_low))

    grad_attended = times_transposed(grad_residual_low, out_full).astype(BF).reshape(head_shape)
    scores = (
        jnp.einsum("qhd,khd->hqk", queries, key_rows, preferred_element_type=F32) * score_scale
    )
    scores = jnp.where(allowed[None], scores, -1e30)
    attention_probs = jnp.exp(scores - log_total)
    grad_weights = jnp.einsum("qhd,khd->hqk", grad_attended, value_rows, preferred_element_type=F32)
    row_delta = jnp.sum(grad_weights * attention_probs, axis=-1, keepdims=True)
    grad_scores = (attention_probs * (grad_weights - row_delta)).astype(BF)
    grad_values = jnp.einsum(
        "hqk,qhd->khd", attention_probs.astype(BF), grad_attended, preferred_element_type=F32
    )
    grad_queries = unrotate(
        jnp.einsum("hqk,khd->qhd", grad_scores, key_rows, preferred_element_type=F32) * score_scale,
        cosine,
        sine_table,
    )
    grad_keys = unrotate(
        jnp.einsum("hqk,qhd->khd", grad_scores, queries, preferred_element_type=F32) * score_scale,
        cosine,
        sine_table,
    )
    grad_projected = jnp.concatenate(
        [
            grad_queries.reshape(row_count, model_width),
            grad_keys.reshape(row_count, model_width),
            grad_values.reshape(row_count, model_width),
        ],
        axis=1,
    ).astype(BF)
    share_qkv = scatter(contract_rows(normed_first, grad_projected))
    grad_normed_first = times_transposed(grad_projected, qkv_full)
    grad_tokens_part, grad_gain_first = norm_back(
        grad_normed_first, tokens_f, scale_first, gain_first
    )
    grad_tokens = grad_residual + grad_tokens_part
    share_gain = lax.psum_scatter(
        jnp.stack([grad_gain_first, grad_gain_second]), BOTH, scatter_dimension=1, tiled=True
    )
    return (
        block_out, grad_tokens, share_qkv, share_out, share_shared_in, share_shared_out,
        share_gain[0], share_gain[1], grad_in, grad_down, counts,
    )


def solution(mesh):
    rows = P(BOTH, None)
    flat = P(BOTH)
    experts = P("expert", None, None)
    return jax.shard_map(
        on_device,
        mesh=mesh,
        in_specs=(
            rows, rows, rows, rows, rows, flat, flat, experts, experts, rows, rows, flat, rows,
        ),
        out_specs=(
            rows, rows, rows, rows, rows, rows, flat, flat, experts, experts, P(),
        ),
        check_vma=False,
    )
```

time: 2110 us -> 1430 us (0.68)
  waiting for transfers between devices: 1100 us -> 697 us
  local copies, waits for them, and re-layouts: 233 us -> 50.4 us
  matrix products: 249 us -> 136 us
  Pallas kernels: 0 us -> 91.9 us
  blocking collectives: 356 us -> 320 us
    all_to_all x4 -> x0, waiting for transfers between devices: 477 us -> none  [the longest x1 188 us: on_device(): lax.all_to_all(send_grad.reshape(groups, local_experts * capacity, model_...]
    unnamed x3 -> x2, blocking collectives: 316 us -> 176 us
    dot_general x14 -> x10, matrix products: 178 us -> 74.1 us  [the longest x1 26.8 us: on_device(): jnp.einsum('esrd,esrf->edf', x, gate_up_grad, preferred_element_type=F32)]
    all_gather x0 -> x2, blocking collectives: none -> 102 us  [the longest x1 69.9 us: on_device(): lax.all_gather(jnp.stack([gain_attn, gain_ffn]), BOTH, axis=1, tiled=True)]
    pallas_call x0 -> x1, Pallas kernels: none -> 91.9 us  [expert_rows(): pl.pallas_call(functools.partial(expert_body, capacity=capacity, hidden=h...]
    gather x4 -> x0, local copies, waits for them, and re-layouts: 83.1 us -> none  [the longest x1 24.7 us: on_device(): jnp.take(grad_rows, source_of, axis=0, mode='fill', fill_value=0)]
    ppermute x0 -> x6, waiting for transfers between devices: none -> 45.6 us  [the longest x2 45.6 us: sum_over_dp(): got = lax.ppermute(total, 'dp', [(i, i ^ step) for i in range(count)])]
    convert_element_type x4 -> x1, local copies, waits for them, and re-layouts: 36.9 us -> 2.58 us  [on_device(): times_transposed(grad_residual_low, out_full).astype(BF).reshape(head_shape)]
  transfers between devices with their start and end apart: 16 -> 21, of which waited for: 10 -> 9; matrix products, arithmetic and copies ran while one was open for 34% -> 28% of each run, Pallas kernels for 0% -> 6%
where the time goes in v1:
time: 1430 us; the launch traced here: 1420 us
  waiting for transfers between devices  697 us (49%)
  blocking collectives  320 us (22%)
  matrix products  136 us (10%)
  other arithmetic  93.3 us (7%)
  Pallas kernels  91.9 us (6%)
  local copies, waits for them, and re-layouts  50.4 us (4%)
  starting transfers between devices  16.8 us (1%)
  between operations  15.9 us (1%)
    reduce_scatter x3, waiting for transfers between devices, on_device(): lax.psum_scatter(a.astype(BF), BOTH, scatter_dimension=0, tiled=True)  225 us
    unnamed x2, blocking collectives  176 us
    all_gather x1, waiting for transfers between devices, on_device(): rows_all = lax.all_gather(normed_second, 'expert', axis=0)  151 us
    all_gather x1, waiting for transfers between devices, on_device(): grads_all = lax.all_gather(cotangent, 'expert', axis=0)  111 us
    reduce_scatter x1, waiting for transfers between devices, on_device(): lax.psum_scatter(flat(part_back), 'expert', scatter_dimension=0, tiled=True)  109 us
    pallas_call x1, Pallas kernels, expert_rows(): pl.pallas_call(functools.partial(expert_body, capacity=capacity, hidden=h...  91.9 us
    all_gather x1, blocking collectives, on_device(): lax.all_gather(jnp.stack([gain_attn, gain_ffn]), BOTH, axis=1, tiled=True)  69.9 us
    ppermute x2, waiting for transfers between devices, sum_over_dp(): got = lax.ppermute(total, 'dp', [(i, i ^ step) for i in range(count)])  45.6 us
  transfers between devices with their start and end apart: 21, of which 9 were waited for; matrix products, arithmetic and copies ran while one was open for 28% of the time, Pallas kernels for 6%

profile of v1, /device:TPU:0, one launch (start us, length us, event | category | flops | bytes accessed | tf_op | source)
XLA Modules:
  0.0 1420.5 jit_solution(15740431991527163082)
XLA Ops:
  10.1 69.9 %all-gather.3 = bf16[32,40,2]{1,2,0:T(2,128)(2,1)S(1)} all-gather(bf16[1,40,2]{1,2,0:T(2,128)(2,1)S(1)} %maximum_bitcast_fusion.1), channel_id=1, replica_groups=mesh['dp'=4,'expert'=8] {'dp','expert'}, dimensions={0}, use_global_device_ids=true | all-gather | bytes 5280 | tf_op jit(solution)/shard_map/all_gather | solution.py:182
  83.7 13.7 all-gather.13.cloned.1.call-done
  97.5 7.7 fusion.32
  106.4 2.7 fusion.46
  109.1 3.2 copy.90
  112.3 3.1 fusion.47
  115.4 3.0 copy.128
  118.4 2.0 copy.129
  120.4 3.2 copy.93
  123.6 3.1 fusion.48
  126.7 3.0 copy.130
  133.3 5.3 subtract_convert_fusion.3
  138.6 3.3 fusion.50
  143.6 2.3 copy-done
  145.9 3.5 fusion.21
  149.5 8.8 all-gather.15.cloned.1.call-done
  158.3 4.5 multiply_reduce_fusion.3
  167.5 32.0 %all-gather.5 = f32[8,12,512]{2,1,0:T(8,128)S(1)} all-gather(f32[1,12,512]{2,1,0:T(8,128)S(1)} %maximum_bitcast_fusion), channel_id=2, replica_groups=mesh['dp'=4,'expert'=8] {'expert'}, dimensions={0}, use_global_device_ids=true | all-gather | bytes 221184 | tf_op jit(solution)/shard_map/all_gather | solution.py:199
  201.3 111.1 %all-gather.21.cloned.1.call-done = bf16[4096,1280]{1,0:T(8,128)(2,1)} async-done(((bf16[512,1280]{1,0:T(8,128)(2,1)}), bf16[4096,1280]{1,0:T(8,128)(2,1)}) %all-gather.21.cloned.1.call-update) | async-done | bytes 10485776 | tf_op jit(solution)/shard_map/all_gather | solution.py:215
  312.4 151.1 %all-gather.19.cloned.1.call-done = bf16[4096,1280]{1,0:T(8,128)(2,1)} async-done(((bf16[512,1280]{1,0:T(8,128)(2,1)}), bf16[4096,1280]{1,0:T(8,128)(2,1)}) %all-gather.19.cloned.1.call-update) | async-done | bytes 10485776 | tf_op jit(solution)/shard_map/all_gather | solution.py:246
  463.5 91.9 %expert_rows.1 = (bf16[8,512,1280]{2,1,0:T(8,128)(2,1)}, bf16[8,512,1280]{2,1,0:T(8,128)(2,1)}, bf16[2,8,240,1280]{3,2,1,0:T(8,128)(2,1)}, bf16[2,8,240,896]{3,2...) custom-call(s32[8,2,512]{2,1,0:T(2,128)} %copy_select_fusion.rank_ref, ...), custom_call_target="tpu_custom_call" | custom-call | flops 74399997952 | bytes 78000000 | tf_op jit(solution)/shard_map/expert_rows/pallas_call | solution.py:125
  555.6 4.4 reshape.260
  560.0 28.0 %all-gather.17.cloned.1.call-done = bf16[1280,1792]{1,0:T(8,128)(2,1)} async-done(((bf16[40,1792]{1,0:T(8,128)(2,1)}), bf16[1280,1792]{1,0:T(8,128)(2,1)}) %all-gather.17.cloned.1.call-update) | async-done | bytes 4587536 | tf_op jit(solution)/shard_map/all_gather | solution.py:180
  588.0 5.0 fusion.51
  593.0 3.1 multiply_convert_fusion.3
  597.3 4.7 convolution_convert_fusion.1
  602.9 13.5 bitcast_convert_fusion.1
  619.4 26.8 %bitcast_convert_fusion = bf16[2,1280,1792]{2,1,0:T(8,128)(2,1)} fusion(bf16[2,8,240,1280]{3,2,1,0:T(8,128)(2,1)} %get-tuple-element.19, bf16[2,8,240,1792]{3,2,1,0:T(8,128)(2,1)} %get-tuple-element.20), kind=kOutput, calls=%fused_computation | convolution fusion | flops 17620664320 | bytes 32768000 | tf_op jit(solution)/shard_map/esrd,esrf->edf/dot_general | solution.py:253
  646.2 6.5 select_bitcast_fusion.2
  653.1 4.2 fusion.8
  658.5 109.3 %reduce-scatter.11.cloned.1.call-done = bf16[512,1280]{1,0:T(8,128)(2,1)} async-done(((bf16[4096,1280]{1,0:T(8,128)(2,1)}), bf16[512,1280]{1,0:T(8,128)(2,1)}) %reduce-scatter.11.cloned.1.call-update) | async-done | bytes 1310736 | tf_op jit(solution)/shard_map/reduce_scatter | solution.py:251
  767.8 6.2 multiply_reduce_fusion.1
  776.3 3.6 convolution_convert_fusion.2
  780.0 8.9 fusion.2
  790.4 3.0 convolution_convert_fusion.4
  793.4 2.6 copy.102
  795.9 11.1 multiply_reduce_fusion
  807.1 6.3 multiply_convert_fusion
  813.4 2.2 multiply_bitcast_fusion.1
  817.3 2.0 subtract_convert_fusion.1
  819.3 2.9 pad_maximum_fusion.6
  822.3 2.4 copy.108
  824.7 2.5 copy.112
  827.2 6.5 fusion.22
  834.7 9.6 convolution_convert_fusion
  844.4 45.6 %collective-permute-done.1 = bf16[1280,1792]{1,0:T(8,128)(2,1)} collective-permute-done((bf16[1280,1792]{1,0:T(8,128)(2,1)}, bf16[1280,1792]{1,0:T(8,128)(2,1)}, u32[]{:S(2)}, u32[]{:S(2)}) %collective-permute-start.1) | collective-permute-done | bytes 4587552 | tf_op jit(solution)/shard_map/ppermute | solution.py:159
  890.0 7.0 add_convert_fusion
  897.0 4.5 add_convert_fusion.1
  901.9 2.8 convolution_convert_fusion.3
  904.7 134.4 %fusion = bf16[32,1280]{1,0:T(8,128)(2,1)S(1)} fusion(bf16[896,1280]{1,0:T(8,128)(2,1)} %convolution_convert_fusion.3), kind=kCustom, calls=%all-reduce-scatter | all-reduce-scatter fusion | flops 1310721 | bytes 2375680
  1039.2 2.9 collective-permute-start.9
  1042.1 4.4 collective-permute-start.6
  1048.4 3.6 collective-permute-start.8
  1052.1 41.7 %psum.7 = s32[16]{0:T(128)} all-reduce(s32[16]{0:T(128)S(1)} %convert_reduce_fusion), channel_id=1, replica_groups=mesh['dp'=4,'expert'=8] {'dp','expert'}, use_global_device_ids=true, to_apply=%region_19.20 | all-reduce | flops 16 | bytes 128 | tf_op jit(solution)/shard_map/psum | solution.py:192
  1097.0 2.6 select_bitcast_fusion.4
  1099.6 4.2 maximum_convert_fusion.1
  1103.9 8.0 select_bitcast_fusion.1
  1111.9 11.6 maximum_convert_fusion
  1123.5 11.6 fusion.19
  1135.2 41.7 %all-reduce.1 = f32[2,1280]{1,0:T(2,128)S(1)} all-reduce(f32[2,1280]{1,0:T(2,128)S(1)} %pad_maximum_fusion.14), channel_id=11, replica_groups=mesh['dp'=4,'expert'=8] {'dp','expert'}, use_global_device_ids=true, to_apply=%region_17.18.clone | all-reduce | flops 2560 | bytes 20480
  1177.5 5.1 fusion.10
  1182.6 2.2 fusion.16
  1184.8 85.3 %reduce-scatter.15.cloned.1.call-done = bf16[40,1280]{1,0:T(8,128)(2,1)} async-done(((bf16[1280,1280]{1,0:T(8,128)(2,1)}), bf16[40,1280]{1,0:T(8,128)(2,1)}) %reduce-scatter.15.cloned.1.call-update) | async-done | bytes 102416 | tf_op jit(solution)/shard_map/reduce_scatter | solution.py:268
  1271.7 140.0 %reduce-scatter.13.cloned.1.call-done = bf16[40,3840]{1,0:T(8,128)(2,1)} async-done(((bf16[1280,3840]{1,0:T(8,128)(2,1)}), bf16[40,3840]{1,0:T(8,128)(2,1)}) %reduce-scatter.13.cloned.1.call-update) | async-done | bytes 307216 | tf_op jit(solution)/shard_map/reduce_scatter | solution.py:268
  (199 shorter events, 41.6 us)
Async XLA Ops:
  7.2 73.7 %copy-start.5 = (bf16[512,1280]{1,0:T(8,128)(2,1)S(1)}, bf16[512,1280]{1,0:T(8,128)(2,1)}, u32[]{:S(2)}) copy-start(bf16[512,1280]{1,0:T(8,128)(2,1)} %param.13) | copy-start | bytes 3932164
  7.2 90.3 %all-gather.13.cloned.1.call-start = ((), (), s32[]{:S(2)}) async-start(), calls=%async_computation.5 | async-start | bytes 10137600 | tf_op jit(solution)/shard_map/all_gather | solution.py:178
  7.9 150.3 %all-gather.15.cloned.1.call-start = ((), (), s32[]{:S(2)}) async-start(), calls=%async_computation.6 | async-start | bytes 3379200 | tf_op jit(solution)/shard_map/all_gather | solution.py:179
  8.7 303.8 %all-gather.21.cloned.1.call-start = ((), (), s32[]{:S(2)}) async-start(), calls=%async_computation.14 | async-start | bytes 11796480 | tf_op jit(solution)/shard_map/all_gather | solution.py:215
  9.4 454.1 %all-gather.19.cloned.1.call-start = ((), (), s32[]{:S(2)}) async-start(), calls=%async_computation.13 | async-start | bytes 11796480 | tf_op jit(solution)/shard_map/all_gather | solution.py:246
  80.9 24.3 %copy-start.40 = (f32[1280]{0:T(1024)}, f32[1280]{0:T(1024)S(1)}, u32[]{:S(2)}) copy-start(f32[1280]{0:T(1024)S(1)} %get-tuple-element.28) | copy-start | bytes 15364
  80.9 82.5 %copy-start.37 = (f32[1280]{0:T(1024)}, f32[1280]{0:T(1024)S(1)}, u32[]{:S(2)}) copy-start(f32[1280]{0:T(1024)S(1)} %get-tuple-element.27) | copy-start | bytes 15364
  81.8 23.4 %copy-start.47 = (f32[512]{0:T(512)}, f32[512]{0:T(512)S(1)}, u32[]{:S(2)}) copy-start(f32[512]{0:T(512)S(1)} %get-tuple-element.62) | copy-start | bytes 6148
  83.7 49.6 %copy-start.27 = (f32[512,64]{1,0:T(8,128)}, f32[512,64]{1,0:T(8,128)S(1)}, u32[]{:S(2)}) copy-start(f32[512,64]{1,0:T(8,128)S(1)} %get-tuple-element.60) | copy-start | bytes 393220
  133.3 10.3 copy-start.20
  138.6 3.4 copy-start.8
  138.6 3.4 copy-start.10
  138.6 3.4 copy-start.12
  138.6 3.4 copy-start.14
  142.0 3.9 copy-start
  142.1 3.9 copy-start.33
  164.2 3.2 copy-start.45
  165.7 389.9 %all-gather.23.cloned.1.call-start = ((), (), s32[]{:S(2)}) async-start(), calls=%async_computation.15 | async-start | bytes 2703360 | tf_op jit(solution)/shard_map/all_gather | solution.py:181
  166.2 421.7 %all-gather.17.cloned.1.call-start = ((), (), s32[]{:S(2)}) async-start(), calls=%async_computation.7 | async-start | bytes 4730880 | tf_op jit(solution)/shard_map/all_gather | solution.py:180
  166.8 601.0 %reduce-scatter.11.cloned.1.call-start = ((), (), s32[]{:S(2)}) async-start(), calls=%async_computation.9 | async-start | bytes 11796480 | tf_op jit(solution)/shard_map/reduce_scatter | solution.py:251
  555.5 32.5 %copy-start.21 = (bf16[512,1280]{1,0:T(8,128)(2,1)S(1)}, bf16[512,1280]{1,0:T(8,128)(2,1)}, u32[]{:S(2)}) copy-start(bf16[512,1280]{1,0:T(8,128)(2,1)} %multiply_convert_fusion.1) | copy-start | bytes 3932164
  555.5 539.8 %reduce-scatter.17.cloned.1.call-start = ((), (), s32[]{:S(2)}) async-start(), calls=%async_computation.12 | async-start | bytes 4730880 | tf_op jit(solution)/shard_map/reduce_scatter | solution.py:268
  560.0 33.0 %copy-start.22 = (bf16[512,1280]{1,0:T(8,128)(2,1)S(1)}, bf16[512,1280]{1,0:T(8,128)(2,1)}, u32[]{:S(2)}) copy-start(bf16[512,1280]{1,0:T(8,128)(2,1)} %param.25) | copy-start | bytes 3932164
  588.0 5.0 copy-start.29
  602.1 575.4 %reduce-scatter.9.cloned.1.call-start = ((), (), s32[]{:S(2)}) async-start(), calls=%async_computation.8 | async-start | bytes 11796480 | tf_op jit(solution)/shard_map/reduce_scatter | solution.py:252
  602.8 667.3 %reduce-scatter.15.cloned.1.call-start = ((), (), s32[]{:S(2)}) async-start(), calls=%async_computation.11 | async-start | bytes 3379200 | tf_op jit(solution)/shard_map/reduce_scatter | solution.py:268
  616.4 2.8 copy-start.3
  619.2 33.9 %collective-permute-start.3 = (bf16[896,1280]{1,0:T(8,128)(2,1)}, bf16[896,1280]{1,0:T(8,128)(2,1)}, u32[]{:S(2)}, u32[]{:S(2)}) collective-permute-start(bf16[896,1280]{1,0:T(8,128)(2,1)} %select_bitcast_fusion.5), channel_id=1, source_target_pairs={{0,8},{8,0},{16,24},{24,16},{1,9},{9,1},{17,25},{25,17},{2,10},{10... | collective-permute-start | bytes 6881288 | tf_op jit(solution)/shard_map/ppermute | solution.py:155
  646.2 6.8 copy-start.34
  646.2 6.8 copy-start.36
  646.2 6.8 copy-start.4
  652.8 127.2 %collective-permute-start = (bf16[1280,1792]{1,0:T(8,128)(2,1)}, bf16[1280,1792]{1,0:T(8,128)(2,1)}, u32[]{:S(2)}, u32[]{:S(2)}) collective-permute-start(bf16[1280,1792]{1,0:T(8,128)(2,1)} %select_bitcast_fusion.2), channel_id=1, source_target_pairs={{0,8},{8,0},{16,24},{24,16},{1,9},{9,1},{17,25},{25,17},{2,10},{10... | collective-permute-start | bytes 13762568 | tf_op jit(solution)/shard_map/ppermute | solution.py:155
  653.0 114.8 %copy-start.2 = (f32[512,1280]{1,0:T(8,128)S(1)}, f32[512,1280]{1,0:T(8,128)}, u32[]{:S(2)}) copy-start(f32[512,1280]{1,0:T(8,128)} %copy-done.1) | copy-start | bytes 7864324
  653.0 114.8 %copy-start.38 = (f32[1280]{0:T(1024)S(1)}, f32[1280]{0:T(1024)}, u32[]{:S(2)}) copy-start(f32[1280]{0:T(1024)} %copy-done.37) | copy-start | bytes 15364
  653.0 114.8 %copy-start.43 = (f32[512]{0:T(512)S(1)}, f32[512]{0:T(512)}, u32[]{:S(2)}) copy-start(f32[512]{0:T(512)} %copy-done.42) | copy-start | bytes 6148
  657.3 116.7 %copy-start.49 = (f32[512]{0:T(512)S(1)}, f32[512]{0:T(512)}, u32[]{:S(2)}) copy-start(f32[512]{0:T(512)} %get-tuple-element.63) | copy-start | bytes 6148
  657.3 239.8 %collective-permute-start.4 = (bf16[896,1280]{1,0:T(8,128)(2,1)}, bf16[896,1280]{1,0:T(8,128)(2,1)}, u32[]{:S(2)}, u32[]{:S(2)}) collective-permute-start(bf16[896,1280]{1,0:T(8,128)(2,1)} %fusion.8), channel_id=1, source_target_pairs={{0,16},{8,24},{16,0},{24,8},{1,17},{9,25},{17,1},{25,9},{2,18},{10... | collective-permute-start | bytes 6881288 | tf_op jit(solution)/shard_map/ppermute | solution.py:159
  767.8 6.3 copy-start.23
  779.9 631.8 %reduce-scatter.13.cloned.1.call-start = ((), (), s32[]{:S(2)}) async-start(), calls=%async_computation.10 | async-start | bytes 10137600 | tf_op jit(solution)/shard_map/reduce_scatter | solution.py:268
  780.0 10.4 copy-start.16
  780.0 10.4 copy-start.18
  788.9 101.1 %collective-permute-start.1 = (bf16[1280,1792]{1,0:T(8,128)(2,1)}, bf16[1280,1792]{1,0:T(8,128)(2,1)}, u32[]{:S(2)}, u32[]{:S(2)}) collective-permute-start(bf16[1280,1792]{1,0:T(8,128)(2,1)} %fusion.2), channel_id=1, source_target_pairs={{0,16},{8,24},{16,0},{24,8},{1,17},{9,25},{17,1},{25,9},{2,18},{10... | collective-permute-start | bytes 13762568 | tf_op jit(solution)/shard_map/ppermute | solution.py:159
  795.9 11.2 slice-start
  795.9 11.2 slice-start.1
  795.9 11.2 slice-start.2
  807.1 6.3 copy-start.13
  807.1 6.3 copy-start.15
  827.2 7.6 copy-start.6
  827.2 7.6 copy-start.31
  827.2 7.6 copy-start.41
  827.2 7.6 copy-start.48
  897.0 4.9 copy-start.24
  897.0 4.9 copy-start.50
  897.0 206.8 %collective-permute-start.2 = (bf16[1280,1792]{1,0:T(8,128)(2,1)}, bf16[1280,1792]{1,0:T(8,128)(2,1)}, u32[]{:S(2)}, u32[]{:S(2)}) collective-permute-start(bf16[1280,1792]{1,0:T(8,128)(2,1)} %add_convert_fusion), channel_id=1, source_target_pairs={{0,8},{8,0},{16,24},{24,16},{1,9},{9,1},{17,25},{25,17},{2,10},{10... | collective-permute-start | bytes 13762568 | tf_op jit(solution)/shard_map/ppermute | solution.py:162
  901.5 195.4 %collective-permute-start.5 = (bf16[896,1280]{1,0:T(8,128)(2,1)}, bf16[896,1280]{1,0:T(8,128)(2,1)}, u32[]{:S(2)}, u32[]{:S(2)}) collective-permute-start(bf16[896,1280]{1,0:T(8,128)(2,1)} %add_convert_fusion.1), channel_id=1, source_target_pairs={{0,8},{8,0},{16,24},{24,16},{1,9},{9,1},{17,25},{25,17},{2,10},{10... | collective-permute-start | bytes 6881288 | tf_op jit(solution)/shard_map/ppermute | solution.py:162
  901.9 150.1 %copy-start.39 = (s32[6,512]{1,0:T(8,128)S(1)}, s32[6,512]{1,0:T(8,128)}, u32[]{:S(2)}) copy-start(s32[6,512]{1,0:T(8,128)} %get-tuple-element.30) | copy-start | bytes 36868
  1039.2 9.3 collective-permute-start.9
  1042.1 51.7 %collective-permute-start.6 = (bf16[32,1280]{1,0:T(8,128)(2,1)S(1)}, bf16[32,1280]{1,0:T(8,128)(2,1)S(1)}, u32[]{:S(2)}, u32[]{:S(2)}) collective-permute-start(bf16[32,1280]{1,0:T(8,128)(2,1)S(1)} %fusion), channel_id=1, source_target_pairs={{0,1},{1,2},{2,3},{3,4},{4,5},{5,6},{6,7},{7,8},{8,9},{9,10},{10,1... | collective-permute-start | bytes 245768
  1046.5 47.4 %collective-permute-start.7 = (bf16[32,1280]{1,0:T(8,128)(2,1)S(1)}, bf16[32,1280]{1,0:T(8,128)(2,1)S(1)}, u32[]{:S(2)}, u32[]{:S(2)}) collective-permute-start(bf16[32,1280]{1,0:T(8,128)(2,1)S(1)} %fusion), channel_id=1, source_target_pairs={{0,2},{1,3},{2,4},{3,5},{4,6},{5,7},{6,8},{7,9},{8,10},{9,11},{10,... | collective-permute-start | bytes 245768
  1048.4 45.4 %collective-permute-start.8 = (bf16[32,1280]{1,0:T(8,128)(2,1)S(1)}, bf16[32,1280]{1,0:T(8,128)(2,1)S(1)}, u32[]{:S(2)}, u32[]{:S(2)}) collective-permute-start(bf16[32,1280]{1,0:T(8,128)(2,1)S(1)} %fusion), channel_id=1, source_target_pairs={{0,3},{1,4},{2,5},{3,6},{4,7},{5,8},{6,9},{7,10},{8,11},{9,12},{10... | collective-permute-start | bytes 245768
  1177.5 5.1 copy-start.46
  1177.5 5.1 copy-start.7
  1177.5 5.1 copy-start.19
  1177.5 5.1 copy-start.26
  (13 other events, 22.1 us)
Sparse Core Ops, SparseCore 0:
  10.9 86.4 all-gather.12
  100.3 57.9 all-gather.14
  160.5 151.9 all-gather.20
  314.5 149.0 all-gather.18
  466.3 56.2 all-gather.22
  525.3 62.5 all-gather.16
  591.6 176.1 reduce-scatter.10
  770.1 145.2 reduce-scatter.16
  919.0 208.4 reduce-scatter.8
  1129.6 140.5 reduce-scatter.14
  1277.1 134.5 reduce-scatter.12

commit v2 on v1

v2 whole, which is shorter than its diff:
```python
import functools

import jax
import jax.numpy as jnp
from jax import lax
from jax.experimental import pallas as pl
from jax.experimental.pallas import tpu as pltpu
from jax.sharding import PartitionSpec as P

HEADS = 10
HEAD_DIM = 128
TOP = 6
PAIR = 2 * HEAD_DIM
ROUTE_ROWS = 16
norm_eps = 1e-06

BF = jnp.bfloat16
F32 = jnp.float32
BOTH = ("dp", "expert")
together = lax.optimization_barrier


def dot(left, right, left_dim=1, right_dim=0):
    return lax.dot_general(
        left, right, (((left_dim,), (right_dim,)), ((), ())), preferred_element_type=F32
    )


def add(left, right):
    return (left.astype(F32) + right.astype(F32)).astype(BF)


def norm_scale(activation):
    return lax.rsqrt(jnp.mean(activation * activation, axis=-1, keepdims=True) + norm_eps)


def full_block(*shape):
    return pl.BlockSpec(
        shape, lambda *i: (0,) * len(shape), pipeline_mode=pl.Buffered(1)
    )


def shaped(*shape, dtype=BF):
    return jax.ShapeDtypeStruct(shape, dtype)


def kernel_cost(flops, moved):
    return pl.CostEstimate(flops=flops, bytes_accessed=moved, transcendentals=0)


def rotary_tables(row_count):
    half = HEAD_DIM // 2
    frequencies = 10000.0 ** (-(2.0 * jnp.arange(half, dtype=F32)) / HEAD_DIM)
    angles = jnp.arange(row_count).astype(F32)[:, None] * frequencies[None, :]
    cosine, sine = jnp.cos(angles), jnp.sin(angles)
    return (
        jnp.concatenate([cosine, cosine], axis=1),
        jnp.concatenate([-sine, sine], axis=1),
    )


def turn(head, cosine, sine):
    return head * cosine + pltpu.roll(head, HEAD_DIM // 2, 1) * sine


def turn_back(head, cosine, sine):
    return head * cosine - pltpu.roll(head, HEAD_DIM // 2, 1) * sine


def allowed_keys(start, stop, length):
    shape = (stop - start, stop)
    row = lax.broadcasted_iota(jnp.int32, shape, 0) + start
    column = lax.broadcasted_iota(jnp.int32, shape, 1)
    return (column <= row) & (column < length)


def attend_body(
    length_ref, wq_ref, wk_ref, wv_ref, wo_ref, gains_in_ref, cos_ref, sin_ref, tokens_ref,
    q_ref, k_ref, v_ref, att_ref, lse_ref, normed_ref, gains_ref, residual_ref, normed_second_ref,
    total_ref,
):
    step = pl.program_id(0)
    row_count = tokens_ref.shape[0]

    @pl.when(step == 0)
    def _():
        shape = (gains_ref.shape[0], HEAD_DIM)
        pick = lax.broadcasted_iota(jnp.int32, shape, 0) == lax.broadcasted_iota(
            jnp.int32, shape, 1
        )
        gains = dot(jnp.where(pick, 1.0, 0.0).astype(BF), gains_in_ref[...], 1, 1)
        gains_ref[...] = gains
        value = tokens_ref[...].astype(F32)
        normed_ref[...] = (value * norm_scale(value) * gains[0:1]).astype(BF)
        total_ref[...] = value

    normed = normed_ref[...]
    length = length_ref[0]
    cosine, sine = cos_ref[...], sin_ref[...]
    queries, keys = dot(normed, wq_ref[...]), dot(normed, wk_ref[...])
    v_ref[...] = dot(normed, wv_ref[...]).astype(BF)
    for head in range(2):
        here = slice(head * HEAD_DIM, (head + 1) * HEAD_DIM)
        q = turn(queries[:, here], cosine, sine).astype(BF)
        k = turn(keys[:, here], cosine, sine).astype(BF)
        q_ref[:, here] = q
        k_ref[:, here] = k
        for start in range(0, row_count, row_count // 2):
            stop = start + row_count // 2
            scores = dot(q[start:stop], k[:stop], 1, 1) * HEAD_DIM ** (-0.5)
            scores = jnp.where(allowed_keys(start, stop, length), scores, -1e30)
            peak = jnp.max(scores, axis=1, keepdims=True)
            weights = jnp.exp(scores - peak)
            whole = jnp.sum(weights, axis=1, keepdims=True)
            lse_ref[0, start:stop, head : head + 1] = peak + jnp.log(whole)
            att_ref[start:stop, here] = dot(
                (weights * (1.0 / whole)).astype(BF), v_ref[:stop, here]
            ).astype(BF)

    total_ref[...] += dot(att_ref[...], wo_ref[...])

    @pl.when(step == pl.num_programs(0) - 1)
    def _():
        residual = total_ref[...]
        residual_ref[...] = residual
        normed_second_ref[...] = (residual * norm_scale(residual) * gains_ref[1:2]).astype(BF)


def attend(length, weights, cosine, sine, tokens):
    rows, width = tokens.shape
    steps = width // PAIR
    part = lambda offset: pl.BlockSpec((width, PAIR), lambda i: (0, i + offset))
    pair = pl.BlockSpec((rows, PAIR), lambda i: (0, i))
    whole = full_block(rows, width)
    return pl.pallas_call(
        attend_body,
        grid=(steps,),
        in_specs=[
            pl.BlockSpec(memory_space=pltpu.SMEM),
            part(0),
            part(steps),
            part(2 * steps),
            pl.BlockSpec((PAIR, width), lambda i: (i, 3)),
            pl.BlockSpec((width, HEAD_DIM), lambda i: (0, 4 * HEADS), pipeline_mode=pl.Buffered(1)),
            full_block(rows, HEAD_DIM),
            full_block(rows, HEAD_DIM),
            whole,
        ],
        out_specs=[pair] * 4
        + [
            pl.BlockSpec((1, rows, 2), lambda i: (i, 0, 0)),
            whole,
            full_block(8, width),
            whole,
            whole,
        ],
        out_shape=[shaped(rows, width)] * 4
        + [
            shaped(steps, rows, 2, dtype=F32), shaped(rows, width), shaped(8, width, dtype=F32),
            shaped(rows, width, dtype=F32), shaped(rows, width),
        ],
        scratch_shapes=[pltpu.VMEM((rows, width), F32)],
        compiler_params=pltpu.CompilerParams(vmem_limit_bytes=48 * 2**20),
        cost_estimate=kernel_cost(10_000_000_000, 25_000_000),
        name="attend",
    )(length, weights, weights, weights, weights, weights, cosine, sine, tokens)


def middle_body(
    pre_ref, own_ref, one_ref, two_ref, residual_ref, cot_ref, gain_ref, wo_ref,
    gr_ref, grb_ref, datt_ref, prod_ref,
):
    @pl.when(pl.program_id(0) == 0)
    def _():
        value = residual_ref[...]
        scale = norm_scale(value)
        grad = pre_ref[...] + (
            own_ref[...].astype(F32) + one_ref[...].astype(F32) + two_ref[...].astype(F32)
        )
        weighted = grad * gain_ref[1:2]
        out = cot_ref[...].astype(F32) + (
            scale * weighted
            - value * (scale * scale * scale) * jnp.mean(weighted * value, axis=1, keepdims=True)
        )
        gr_ref[...] = out
        grb_ref[...] = out.astype(BF)
        prod_ref[...] = (grad * value * scale).astype(BF)

    datt_ref[...] = dot(grb_ref[...], wo_ref[...], 1, 1).astype(BF)


def middle(pre, own, one, two, residual, cot, gain, weights):
    rows, width = residual.shape
    steps = width // PAIR
    pair = pl.BlockSpec((rows, PAIR), lambda i: (0, i))
    whole = full_block(rows, width)
    return pl.pallas_call(
        middle_body,
        grid=(steps,),
        in_specs=[whole] * 6
        + [full_block(8, width), pl.BlockSpec((PAIR, width), lambda i: (i, 3))],
        out_specs=[whole, whole, pair, whole],
        out_shape=[
            shaped(rows, width, dtype=F32), shaped(rows, width), shaped(rows, width),
            shaped(rows, width),
        ],
        compiler_params=pltpu.CompilerParams(vmem_limit_bytes=48 * 2**20),
        cost_estimate=kernel_cost(4_000_000_000, 25_000_000),
        name="middle",
    )(pre, own, one, two, residual, cot, gain, weights)


def attend_back_body(
    length_ref, normed_ref, wq_ref, wk_ref, wv_ref, cos_ref, sin_ref, tokens_ref, gain_ref,
    q_ref, k_ref, v_ref, datt_ref, lse_ref, gr_ref, grb_ref, att_ref, prod_ref,
    mine_ref, other_ref, gtok_ref, mine_late_ref, other_late_ref,
    gq_ref, gk_ref, gv_ref, total_ref, *, chips,
):
    step = pl.program_id(0)
    normed = normed_ref[...]
    row_count, width = normed.shape
    length, core = length_ref[0], length_ref[1]
    cosine, sine = cos_ref[...], sin_ref[...]
    scale = HEAD_DIM ** (-0.5)
    unit = width // (2 * chips)

    def store(refs, columns, block):
        block = block.astype(BF)
        for mine in range(2):

            @pl.when(core == mine)
            def _(mine=mine):
                for n in range(2 * chips):
                    ref = refs[0] if n % 2 == mine else refs[1]
                    ref[n // 2 * unit : (n // 2 + 1) * unit, columns] = block[
                        n * unit : (n + 1) * unit
                    ]

    half = row_count // 2
    for head in range(2):
        here = slice(head * HEAD_DIM, (head + 1) * HEAD_DIM)
        grad_keys, grad_values = [], []
        for start in (0, half):
            stop = start + half
            q, k = q_ref[start:stop, here], k_ref[:stop, here]
            grad = datt_ref[start:stop, here]
            scores = dot(q, k, 1, 1) * scale
            scores = jnp.where(allowed_keys(start, stop, length), scores, -1e30)
            probs = jnp.exp(scores - lse_ref[0, start:stop, head : head + 1])
            grad_probs = dot(grad, v_ref[:stop, here], 1, 1)
            delta = jnp.sum(grad_probs * probs, axis=1, keepdims=True)
            grad_scores = (probs * (grad_probs - delta)).astype(BF)
            grad_values.append(dot(probs.astype(BF), grad, 0, 0))
            gq_ref[start:stop, here] = turn_back(
                dot(grad_scores, k) * scale, cosine[start:stop], sine[start:stop]
            ).astype(BF)
            grad_keys.append(dot(grad_scores, q, 0, 0) * scale)
        for out_ref, (first, second), turned in (
            (gk_ref, grad_keys, True),
            (gv_ref, grad_values, False),
        ):
            whole = jnp.concatenate([first + second[:half], second[half:]], axis=0)
            if turned:
                whole = turn_back(whole, cosine, sine)
            out_ref[:, here] = whole.astype(BF)

    @pl.when(step == 0)
    def _():
        total_ref[...] = jnp.zeros_like(total_ref)

    offset = pl.multiple_of(step * 3 * PAIR, PAIR)
    refs = (mine_ref, other_ref)
    for n, (grad_ref, w_ref) in enumerate(((gq_ref, wq_ref), (gk_ref, wk_ref), (gv_ref, wv_ref))):
        grad = grad_ref[...]
        store(refs, pl.ds(offset + n * PAIR, PAIR), dot(normed, grad, 0, 0))
        total_ref[...] += dot(grad, w_ref[...], 1, 1)

    @pl.when(step == pl.num_programs(0) - 1)
    def _():
        value = tokens_ref[...].astype(F32)
        r = norm_scale(value)
        grad = total_ref[...]
        weighted = grad * gain_ref[0:1]
        gtok_ref[...] = gr_ref[...] + (
            r * weighted
            - value * (r * r * r) * jnp.mean(weighted * value, axis=1, keepdims=True)
        )
        lane = lax.broadcasted_iota(jnp.int32, (row_count, HEAD_DIM), 1)
        first = jnp.where(lane == 0, 1.0, 0.0).astype(BF)
        second = jnp.where(lane == 1, 1.0, 0.0).astype(BF)
        refs = (mine_late_ref, other_late_ref)
        store(
            refs,
            slice(width, width + HEAD_DIM),
            dot((grad * value * r).astype(BF), first, 0, 0) + dot(prod_ref[...], second, 0, 0),
        )
        store(refs, slice(0, width), dot(att_ref[...], grb_ref[...], 0, 0))


def attend_back(
    length, normed, weights, cosine, sine, tokens, gain, q, k, v, datt, lse, gr, grb, att, prod, chips
):
    rows, width = tokens.shape
    steps = width // PAIR
    part = lambda offset: pl.BlockSpec((width, PAIR), lambda i: (0, i + offset))
    pair = pl.BlockSpec((rows, PAIR), lambda i: (0, i))
    whole = full_block(rows, width)
    return pl.pallas_call(
        functools.partial(attend_back_body, chips=chips),
        grid=(steps,),
        in_specs=[
            pl.BlockSpec(memory_space=pltpu.SMEM),
            whole,
            part(0),
            part(steps),
            part(2 * steps),
            full_block(rows, HEAD_DIM),
            full_block(rows, HEAD_DIM),
            whole,
            full_block(8, width),
            pair, pair, pair, pair,
            pl.BlockSpec((1, rows, 2), lambda i: (i, 0, 0)),
            whole, whole, whole, whole,
        ],
        out_specs=[full_block(width // 2, 3 * width)] * 2
        + [whole]
        + [full_block(width // 2, width + HEAD_DIM)] * 2,
        out_shape=[shaped(width // 2, 3 * width)] * 2
        + [shaped(rows, width, dtype=F32)]
        + [shaped(width // 2, width + HEAD_DIM)] * 2,
        scratch_shapes=[pltpu.VMEM((rows, PAIR), BF)] * 3 + [pltpu.VMEM((rows, width), F32)],
        compiler_params=pltpu.CompilerParams(vmem_limit_bytes=56 * 2**20),
        cost_estimate=kernel_cost(14_000_000_000, 40_000_000),
        name="attend_back",
    )(
        length, normed, weights, weights, weights, cosine, sine, tokens, gain,
        q, k, v, datt, lse, gr, grb, att, prod,
    )


def expert_body(mine_ref, *refs, count, capacity, hidden):
    rows_refs, grads_refs, route_refs = [refs[n * count : (n + 1) * count] for n in range(3)]
    win_hbm, wout_hbm = refs[3 * count : 3 * count + 2]
    win_ref, wout_ref, sems = refs[-3:]
    refs = refs[:-3]
    pdx_refs, pout_refs = refs[-2 * count - 4 : -count - 4], refs[-count - 4 : -4]
    x_ref, h_ref, gr_ref, dgu_ref = refs[-4:]
    step = pl.program_id(0)
    experts = win_ref.shape[0]
    copies = [
        [
            pltpu.make_async_copy(hbm.at[e], ref.at[e], sems.at[e, n])
            for n, (hbm, ref) in enumerate(((win_hbm, win_ref), (wout_hbm, wout_ref)))
        ]
        for e in range(experts)
    ]

    @pl.when(step == 0)
    def _():
        for copy in sum(copies, []):
            copy.start()

    def arrived(copy):
        @pl.when(step == 0)
        def _():
            copy.wait()

    rows, grads, routes = [g[0][...] for g in (rows_refs, grads_refs, route_refs)]
    for n in range(1, count):
        rows = jnp.where(step == n, rows_refs[n][...], rows)
        grads = jnp.where(step == n, grads_refs[n][...], grads)
        routes = jnp.where(step == n, route_refs[n][...], routes)
    row_count = rows.shape[0]
    routes = routes.astype(F32)
    ids = routes[:TOP, :row_count]
    gates = (
        routes[:TOP, row_count : 2 * row_count]
        + routes[TOP : 2 * TOP, :row_count]
        + routes[TOP : 2 * TOP, row_count : 2 * row_count]
    )
    square = (row_count, row_count)
    earlier = lax.broadcasted_iota(jnp.int32, square, 0) < lax.broadcasted_iota(
        jnp.int32, square, 1
    )
    earlier = jnp.where(earlier, 1.0, 0.0).astype(BF)
    slot = lax.broadcasted_iota(jnp.int32, (capacity, row_count), 0)
    picks, back_rows, results = [], [], []
    for e in range(experts):
        chosen = ids == (mine_ref[0] + e).astype(F32)
        named = jnp.sum(jnp.where(chosen, 1.0, 0.0), axis=0, keepdims=True)
        gate = jnp.sum(jnp.where(chosen, gates, 0.0), axis=0, keepdims=True)
        rank = dot(jnp.broadcast_to(named, (16, row_count)).astype(BF), earlier)[0:1]
        mask = slot == jnp.where(named > 0.5, rank, -1.0).astype(jnp.int32)
        pick = jnp.where(mask, 1.0, 0.0).astype(BF)
        gate_col = jnp.sum(jnp.where(mask, gate, 0.0), axis=1, keepdims=True)
        x = dot(pick, rows).astype(BF)
        x_ref[e, 0] = x
        gr = (dot(pick, grads) * gate_col).astype(BF)
        gr_ref[e, 0] = gr
        arrived(copies[e][0])
        gate_up = dot(x, win_ref[e])
        a, b = gate_up[:, :hidden], gate_up[:, hidden:]
        s = jax.nn.sigmoid(a)
        swish = a * s
        h = (swish * b).astype(BF)
        h_ref[e, 0] = h
        arrived(copies[e][1])
        gh = dot(gr, wout_ref[e], 1, 1)
        dgu_ref[e, 0, :, :hidden] = (gh * b * s * (1.0 + a * (1.0 - s))).astype(BF)
        dgu_ref[e, 0, :, hidden:] = (gh * swish).astype(BF)
        back_rows.append(dot(dgu_ref[e, 0], win_ref[e], 1, 1).astype(BF))
        results.append((dot(h, wout_ref[e]) * gate_col).astype(BF))
        picks.append(pick)
    picks = jnp.concatenate(picks, axis=0)
    back = dot(picks, jnp.concatenate(back_rows, axis=0), 0, 0).astype(BF)
    out = dot(picks, jnp.concatenate(results, axis=0), 0, 0).astype(BF)
    for n in range(count):

        @pl.when(step == n)
        def _(n=n):
            pdx_refs[n][...] = back
            pout_refs[n][...] = out


def expert_rows(first, mine, groups, rows, grads, w_in, w_out, capacity, so_far):
    count = len(rows)
    row_count, width = rows[0].shape
    experts, hidden, _ = w_out.shape
    whole = full_block(row_count, width)
    routes = pl.BlockSpec(
        (ROUTE_ROWS, width),
        lambda i, mine: (row_count // ROUTE_ROWS, 0),
        pipeline_mode=pl.Buffered(1),
    )
    slots = lambda w: pl.BlockSpec((experts, 1, capacity, w), lambda i, mine: (0, first + i, 0, 0))
    widths = (width, hidden, width, 2 * hidden)
    so_far = [] if so_far is None else list(so_far)
    out = pl.pallas_call(
        functools.partial(expert_body, count=count, capacity=capacity, hidden=hidden),
        grid_spec=pltpu.PrefetchScalarGridSpec(
            num_scalar_prefetch=1,
            grid=(count,),
            in_specs=[whole] * (2 * count)
            + [routes] * count
            + [pl.BlockSpec(memory_space=pl.ANY)] * (2 + len(so_far)),
            out_specs=[whole] * (2 * count)
            + [slots(w) for w in widths],
            scratch_shapes=[
                pltpu.VMEM(w_in.shape, BF),
                pltpu.VMEM(w_out.shape, BF),
                pltpu.SemaphoreType.DMA((experts, 2)),
            ],
        ),
        out_shape=[shaped(row_count, width)] * (2 * count)
        + [shaped(experts, groups, capacity, w) for w in widths],
        input_output_aliases={3 + 3 * count + n: 2 * count + n for n in range(len(so_far))},
        compiler_params=pltpu.CompilerParams(vmem_limit_bytes=60 * 2**20),
        cost_estimate=kernel_cost(count * 9_300_000_000, count * 8_000_000 + 14_000_000),
        name="expert_rows",
    )(mine, *rows, *grads, *grads, w_in, w_out, *so_far)
    return list(out[:count]), list(out[count : 2 * count]), list(out[2 * count :])


def expert_grads_body(core_ref, left_ref, right_ref, mine_ref, other_ref):
    merge = lambda ref: ref[0].reshape(-1, ref.shape[-1])
    grads = dot(merge(left_ref), merge(right_ref), 0, 0).astype(BF)

    @pl.when(pl.program_id(0) == 0)
    def _():
        mine_ref[...] = grads

    @pl.when(pl.program_id(0) == 1)
    def _():
        other_ref[...] = grads


def expert_grads(core, left, right, columns):
    experts, groups, capacity, width = left.shape
    steps = right.shape[3] // columns
    take = lambda w, pick: pl.BlockSpec((1, groups, capacity, w), pick)
    block = lambda pick: pl.BlockSpec((width, columns), pick)
    return pl.pallas_call(
        expert_grads_body,
        grid_spec=pltpu.PrefetchScalarGridSpec(
            num_scalar_prefetch=1,
            grid=(experts, steps),
            in_specs=[
                take(width, lambda e, i, core: ((e + core[0]) % 2, 0, 0, 0)),
                take(columns, lambda e, i, core: ((e + core[0]) % 2, 0, 0, i)),
            ],
            out_specs=[
                block(lambda e, i, core: (0, jnp.where(e == 0, i, steps - 1))),
                block(lambda e, i, core: (0, jnp.where(e == 0, 0, i))),
            ],
        ),
        out_shape=[shaped(width, right.shape[3])] * 2,
        compiler_params=pltpu.CompilerParams(vmem_limit_bytes=60 * 2**20),
        cost_estimate=kernel_cost(
            2 * experts * groups * capacity * width * right.shape[3], 40_000_000
        ),
        name="expert_grads",
    )(core, left, right)


def both_experts_body(core_ref, mine_ref, other_ref, out_ref):
    out_ref[core_ref[0]] = mine_ref[...].astype(F32)
    out_ref[1 - core_ref[0]] = other_ref[...].astype(F32)


def both_experts(core, mine, other):
    rows, width = mine.shape
    step = rows // 7 if rows % 112 == 0 else rows // 8
    block = pl.BlockSpec((step, width), lambda i, core: (i, 0))
    return pl.pallas_call(
        both_experts_body,
        grid_spec=pltpu.PrefetchScalarGridSpec(
            num_scalar_prefetch=1,
            grid=(rows // step,),
            in_specs=[block, block],
            out_specs=pl.BlockSpec((2, step, width), lambda i, core: (0, i, 0)),
        ),
        out_shape=shaped(2, rows, width, dtype=F32),
        cost_estimate=kernel_cost(rows * width, 12 * rows * width),
        name="both_experts",
    )(core, mine, other)


def shared_body(
    normed_ref, cot_ref, residual_ref, win_ref, wout_ref,
    pre_ref, sum_ref, gin_ref, gout_ref, grad_ref, *, hidden,
):
    normed, cot = normed_ref[...], cot_ref[...]
    gate_up = dot(normed, win_ref[...])
    a, b = gate_up[:, :hidden], gate_up[:, hidden:]
    s = jax.nn.sigmoid(a)
    swish = a * s
    h = (swish * b).astype(BF)
    gh = dot(cot, wout_ref[...], 1, 1)
    grad_ref[:, :hidden] = (gh * b * s * (1.0 + a * (1.0 - s))).astype(BF)
    grad_ref[:, hidden:] = (gh * swish).astype(BF)
    pre_ref[...] = dot(grad_ref[...], win_ref[...], 1, 1)
    sum_ref[...] = residual_ref[...] + dot(h, wout_ref[...])
    gin_ref[...] = dot(normed, grad_ref[...], 0, 0).astype(BF)
    gout_ref[...] = dot(h, cot, 0, 0).astype(BF)


def shared_expert(normed, cot, residual, w_in, w_out):
    rows, width = normed.shape
    hidden = w_out.shape[0]
    whole = full_block(rows, width)
    return pl.pallas_call(
        functools.partial(shared_body, hidden=hidden),
        grid=(1,),
        in_specs=[
            whole, whole, whole, full_block(width, 2 * hidden), full_block(hidden, width),
        ],
        out_specs=[whole, whole, full_block(width, 2 * hidden), full_block(hidden, width)],
        out_shape=[
            shaped(rows, width, dtype=F32), shaped(rows, width, dtype=F32),
            shaped(width, 2 * hidden), shaped(hidden, width),
        ],
        scratch_shapes=[pltpu.VMEM((rows, 2 * hidden), BF)],
        compiler_params=pltpu.CompilerParams(vmem_limit_bytes=56 * 2**20),
        cost_estimate=kernel_cost(14_000_000_000, 25_000_000),
        name="shared_expert",
    )(normed, cot, residual, w_in, w_out)


LINE = 4


def across(array):
    return lax.ppermute(array, "expert", [(i, i ^ 1) for i in range(2 * LINE)])


def along(array, hops):
    return lax.ppermute(
        array, "expert", [(2 * a + side, 2 * b + side) for a, b in hops for side in (0, 1)]
    )


def by_place(place, options):
    result = options[-1]
    for n in range(len(options) - 2, -1, -1):
        result = jnp.where(place == n, options[n], result)
    return result


class Flow:
    def __init__(self, steps):
        self.steps, self.result = steps, None
        self.waiting = next(steps)

    def feed(self, arrived):
        try:
            self.waiting = self.steps.send(arrived)
        except StopIteration as stop:
            self.waiting, self.result = (), stop.value


def advance(flows, done=()):
    arrived, done = together((tuple(f.waiting for f in flows), done))
    for flow, block in zip(flows, arrived):
        flow.feed(block)
    return done


def finish(flow):
    while flow.result is None:
        advance([flow])
    return flow.result


def gather_steps(own, place, slots):
    slots.append(own)
    y0, d1, u1 = yield (
        across(own),
        along(own, [(1, 0), (2, 1), (3, 2)]),
        along(own, [(0, 1), (1, 2), (2, 3)]),
    )
    s1 = jnp.where(place <= 1, d1, u1)
    slots += [y0, s1]
    y1, d2, u2 = yield (
        across(s1),
        along(d1, [(1, 0), (2, 1)]),
        along(u1, [(1, 2), (2, 3)]),
    )
    s2 = by_place(place, [d2, u1, d1, u2])
    slots += [y1, s2]
    y2, ud3 = yield (across(s2), along(jnp.where(place == 2, u2, d2), [(2, 3), (1, 0)]))
    s3 = by_place(place, [ud3, d2, u2, ud3])
    slots += [y2, s3]
    (y3,) = yield (across(s3),)
    slots.append(y3)
    return slots


def reduce_steps(place, parts):
    own, y0, s1, y1, s2, y2, s3, y3 = parts
    (r3,) = yield (across(y3),)
    s3 = add(s3, r3)
    r2, t3 = yield (across(y2), along(s3, [(0, 1), (3, 2)]))
    s2, s3 = add(s2, r2), add(s3, t3)
    r1, up, down = yield (
        across(y1),
        along(jnp.where(place == 0, s2, s3), [(0, 1), (1, 2)]),
        along(jnp.where(place == 3, s2, s3), [(3, 2), (2, 1)]),
    )
    s1 = add(s1, r1)
    m1 = add(s1, jnp.where(place == 1, up, down))
    m2 = add(s2, jnp.where(place == 1, down, up))
    r0, up, down = yield (
        across(y0),
        along(by_place(place, [s1, m1, m2]), [(0, 1), (1, 2), (2, 3)]),
        along(by_place(place, [m2, m2, m1, s1]), [(3, 2), (2, 1), (1, 0)]),
    )
    return add(own, r0), up, down


def pick_half(array, bit, dim):
    return lax.dynamic_index_in_dim(array, bit, dim, keepdims=False)


def split_core(count):
    return [(i, i ^ 1) for i in range(count)]


def home_steps(mine, other, split=True):
    count = lax.axis_size("dp")
    chip = lax.axis_index("dp") // 2
    place, side = lax.axis_index("expert") // 2, lax.axis_index("expert") % 2
    columns = mine.shape[-1]
    (got,) = yield (lax.ppermute(other, "dp", split_core(count)),)
    total = add(mine, got)

    def over_side(part):
        (got,) = yield (across(pick_half(part, 1 - side, 2)),)
        return add(pick_half(part, side, 2), got)

    def over_chips(part):
        while part.shape[0] > 1:
            half = part.shape[0] // 2
            bit = chip // half % 2
            part = part.reshape((2, half) + part.shape[1:])
            (got,) = yield (
                lax.ppermute(
                    pick_half(part, 1 - bit, 0), "dp", [(i, i ^ (2 * half)) for i in range(count)]
                ),
            )
            part = add(pick_half(part, bit, 0), got)
        return part

    if not split:
        part = yield from over_chips(total)
        part = part[0]
        arrived = yield tuple(
            along(
                pick_half(part, (place + hop) % LINE, 0),
                [(n, (n + hop) % LINE) for n in range(LINE)],
            )
            for hop in range(1, LINE)
        )
        part = pick_half(part, place, 0).astype(F32)
        for block in arrived:
            part = part + block.astype(F32)
        (got,) = yield (across(pick_half(part, 1 - side, 0).astype(BF)),)
        return pick_half(part, side, 0) + got.astype(F32)

    cut = columns // 256 * 128
    parts = [total[..., :cut], total[..., cut:]]
    for kinds in ((over_side, over_chips), (over_chips, over_side)):
        flows = [Flow(kind(part)) for kind, part in zip(kinds, parts)]
        while any(f.result is None for f in flows):
            open_flows = [f for f in flows if f.result is None]
            arrived = yield tuple(f.waiting for f in open_flows)
            for flow, block in zip(open_flows, arrived):
                flow.feed(block)
        parts = [f.result for f in flows]
    part = jnp.concatenate([p[0] for p in parts], axis=-1)
    result = pick_half(part, place, 0).astype(F32)
    arrived = yield tuple(
        along(
            pick_half(part, (place + hop) % LINE, 0), [(n, (n + hop) % LINE) for n in range(LINE)]
        )
        for hop in range(1, LINE)
    )
    for block in arrived:
        result = result + block.astype(F32)
    return result


def dp_sum_steps(mine, other, core, pieces):
    count = lax.axis_size("dp")
    (got,) = yield (lax.ppermute(other, "dp", split_core(count)),)
    unit = mine.shape[0] // pieces
    done = []
    for n in range(pieces):
        piece = add(mine[n * unit : (n + 1) * unit], got[n * unit : (n + 1) * unit])
        step = 2
        while step < count:
            (there,) = yield (lax.ppermute(piece, "dp", [(i, i ^ step) for i in range(count)]),)
            piece = add(piece, there)
            step *= 2
        done.append(piece)
    total = jnp.concatenate(done, axis=0)
    (got,) = yield (lax.ppermute(total, "dp", split_core(count)),)
    return both_experts(core, total, got)


def on_device(
    tokens, w_qkv, w_attn_out, w_shared_in, w_shared_out, gain_attn, gain_ffn,
    w_expert_in, w_expert_out, route_ids, route_gates, seq_lengths, cotangent,
):
    rows, width = tokens.shape
    groups = lax.axis_size("expert")
    devices = groups * lax.axis_size("dp")
    experts = w_expert_in.shape[0]
    experts_total = experts * groups
    capacity = rows * TOP * 5 // (4 * experts_total)
    share, share_out = w_qkv.shape[0], w_shared_out.shape[0]
    shared_width = share_out * devices
    place, side = lax.axis_index("expert") // 2, lax.axis_index("expert") % 2

    gain_columns = jnp.pad(
        jnp.stack([gain_attn, gain_ffn], axis=1), ((0, 0), (0, HEAD_DIM - 2))
    )
    attn_full = lax.all_gather(
        jnp.concatenate([w_qkv, w_attn_out, gain_columns], axis=1), BOTH, axis=0, tiled=True
    )
    live = jnp.arange(rows) < seq_lengths[0]
    ids = jnp.where(live[:, None], route_ids, -1).astype(F32).T
    high = lax.reduce_precision(route_gates.T, 8, 7)
    middle_bits = lax.reduce_precision(route_gates.T - high, 8, 7)
    low = route_gates.T - high - middle_bits
    routes = jnp.concatenate(
        [jnp.concatenate([ids, high], axis=1), jnp.concatenate([middle_bits, low], axis=1)], axis=0
    )
    routes = jnp.pad(
        routes, ((0, ROUTE_ROWS - 2 * TOP), (0, width - 2 * rows))
    ).astype(BF)
    grads = []
    grads_flow = Flow(
        gather_steps(jnp.concatenate([cotangent, routes], axis=0), place, grads)
    )
    mine = lax.axis_index("expert")[None] * experts
    cosine, sine = rotary_tables(rows)
    advance([grads_flow])
    attn_full, w_shared_in, w_shared_out = together((attn_full, w_shared_in, w_shared_out))
    shared_full = lax.all_gather(
        jnp.concatenate(
            [w_shared_in, jnp.pad(w_shared_out, ((0, share - share_out), (0, 0)))], axis=1
        ),
        BOTH,
        axis=0,
        tiled=True,
    )
    advance([grads_flow])

    q, k, v, att, lse, normed_first, gains, residual, normed_second = advance(
        [grads_flow], attend(seq_lengths, attn_full, cosine, sine, tokens)
    )

    arrived, back, out, kept = [], [], [], [None]
    rows_flow = Flow(gather_steps(normed_second, place, arrived))

    def through():
        first = len(back)
        new_back, new_out, kept[0] = expert_rows(
            first, mine, groups, arrived[first:], grads[first : len(arrived)],
            w_expert_in, w_expert_out, capacity, kept[0],
        )
        back.extend(new_back)
        out.extend(new_out)

    through()
    while rows_flow.result is None:
        more = [f for f in (grads_flow,) if f.result is None]
        back[:], out[:], kept[0] = advance([rows_flow] + more, (back, out, kept[0]))
        through()
    x, hidden, result_grad, gate_up_grad = kept[0]

    back_flow = Flow(reduce_steps(place, back))
    core = lax.axis_index("dp")[None] % 2
    grad_in = expert_grads(core, x, gate_up_grad, shared_width)
    grad_down = expert_grads(core, hidden, result_grad, width)
    grad_in, grad_down, out, shared_full = advance(
        [back_flow], (grad_in, grad_down, out, shared_full)
    )

    out_flow = Flow(reduce_steps(place, out))
    in_flow = Flow(dp_sum_steps(*grad_in, core, 4))
    down_flow = Flow(dp_sum_steps(*grad_down, core, 2))
    pre, layer_sum, grad_shared_in, grad_shared_out = shared_expert(
        normed_second,
        cotangent,
        residual,
        shared_full,
        shared_full[:, 2 * shared_width :]
        .reshape(devices, share, width)[:, :share_out]
        .reshape(shared_width, width),
    )
    pre, layer_sum, grad_shared_in, grad_shared_out = advance(
        [back_flow, in_flow, down_flow], (pre, layer_sum, grad_shared_in, grad_shared_out)
    )

    def of_core(which):
        part = lambda array: pick_half(
            array.reshape(devices // groups // 2, 2, LINE, 2, -1, array.shape[1]), which, 1
        )
        below = ((0, 0),) * 3 + ((0, share - share_out), (0, 0))
        return jnp.concatenate(
            [part(grad_shared_in), jnp.pad(part(grad_shared_out), below)], axis=-1
        )

    shared_flow = Flow(home_steps(of_core(core[0]), of_core(1 - core[0]), split=False))
    advance([back_flow, out_flow, in_flow, down_flow])
    advance([back_flow, out_flow, in_flow, down_flow, shared_flow])
    own, up, down = back_flow.result

    gr, grb, datt, prod = middle(pre, own, up, down, residual, cotangent, gains, attn_full)
    mine_last, other_last, grad_tokens, mine_late, other_late = attend_back(
        jnp.concatenate([seq_lengths, core.astype(jnp.int32)]), normed_first, attn_full,
        cosine, sine, tokens, gains, q, k, v, datt, lse, gr, grb, att, prod, devices // groups // 2,
    )
    mine_last, other_last, grad_tokens, mine_late, other_late = advance(
        [out_flow, in_flow, down_flow, shared_flow],
        (mine_last, other_last, grad_tokens, mine_late, other_late),
    )
    blocks = lambda array: array.reshape(
        devices // groups // 2, LINE, 2, share, array.shape[1]
    )
    last_flow = Flow(home_steps(blocks(mine_last), blocks(other_last)))
    late_flow = Flow(home_steps(blocks(mine_late), blocks(other_late), split=False))
    for flow in (last_flow, late_flow, out_flow, in_flow, down_flow, shared_flow):
        finish(flow)
    late = late_flow.result
    last, shares = last_flow.result, shared_flow.result
    block_out = layer_sum
    for part in out_flow.result:
        block_out = block_out + part.astype(F32)
    block_out = block_out.astype(BF)
    share_in, share_down = shares[:, : 2 * shared_width], shares[:share_out, 2 * shared_width :]
    share_qkv = (
        last[:, : 3 * width]
        .reshape(share, width // PAIR, 3, PAIR)
        .transpose(0, 2, 1, 3)
        .reshape(share, 3 * width)
    )

    all_ids = jnp.stack([g[rows : rows + TOP, :rows] for g in grads])
    counts = jnp.sum(
        (all_ids[None] == jnp.arange(experts_total, dtype=BF)[:, None, None, None]).astype(F32),
        axis=(1, 2, 3),
    )
    counts = jnp.broadcast_to(counts[:, None], (experts_total, HEAD_DIM))
    step = 1
    while step < devices // groups:
        counts = counts + lax.ppermute(
            counts, "dp", [(i, i ^ step) for i in range(devices // groups)]
        )
        step *= 2
    return (
        block_out, grad_tokens, share_qkv, late[:, :width], share_in, share_down,
        late[:, width], late[:, width + 1], in_flow.result, down_flow.result,
        counts[:, 0].astype(jnp.int32),
    )


def solution(mesh):
    rows = P(BOTH, None)
    flat = P(BOTH)
    experts = P("expert", None, None)
    return jax.shard_map(
        on_device,
        mesh=mesh,
        in_specs=(
            rows, rows, rows, rows, rows, flat, flat, experts, experts, rows, rows, flat, rows,
        ),
        out_specs=(
            rows, rows, rows, rows, rows, rows, flat, flat, experts, experts, P(),
        ),
        check_vma=False,
    )
```

time: 1430 us -> 919 us (0.64)
  waiting for transfers between devices: 697 us -> 363 us
  blocking collectives: 320 us -> 0 us
  Pallas kernels: 91.9 us -> 295 us
  matrix products: 136 us -> 0 us
  starting transfers between devices: 16.8 us -> 114 us
    reduce_scatter x5 -> x0, waiting for transfers between devices: 335 us -> none  [the longest x3 225 us: on_device(): lax.psum_scatter(a.astype(BF), BOTH, scatter_dimension=0, tiled=True)]
    ppermute x6 -> x68, waiting for transfers between devices: 45.6 us -> 295 us  [the longest x29 139 us: along(): lax.ppermute(array, 'expert', [(2 * a + side, 2 * b + side) for a, b in h...]
    all_gather x6 -> x2, waiting for transfers between devices: 313 us -> 68.2 us  [the longest x1 68.2 us: on_device(): lax.all_gather(jnp.concatenate([w_qkv, w_attn_out, gain_columns], axis=1)...]
    pallas_call x1 -> x13, Pallas kernels: 91.9 us -> 295 us  [the longest x5 133 us: expert_rows(): pl.pallas_call(functools.partial(expert_body, count=count, capacity=capac...]
    unnamed x2 -> x0, blocking collectives: 176 us -> none
    dot_general x21 -> x0, matrix products: 136 us -> none  [the longest x1 26.8 us: on_device(): jnp.einsum('esrd,esrf->edf', x, gate_up_grad, preferred_element_type=F32)]
    ppermute x6 -> x68, starting transfers between devices: 3.6 us -> 114 us  [the longest x29 79.8 us: along(): lax.ppermute(array, 'expert', [(2 * a + side, 2 * b + side) for a, b in h...]
    all_gather x2 -> x0, blocking collectives: 102 us -> none  [the longest x1 69.9 us: on_device(): lax.all_gather(jnp.stack([gain_attn, gain_ffn]), BOTH, axis=1, tiled=True)]
  transfers between devices with their start and end apart: 21 -> 70, of which waited for: 9 -> 24; matrix products, arithmetic and copies ran while one was open for 28% -> 12% of each run, Pallas kernels for 6% -> 32%
where the time goes in v2:
time: 919 us; the launch traced here: 910 us
  waiting for transfers between devices  363 us (39%)
  Pallas kernels  295 us (32%)
  starting transfers between devices  114 us (12%)
  other arithmetic  84.1 us (9%)
  local copies, waits for them, and re-layouts  37.6 us (4%)
  between operations  16.2 us (2%)
    ppermute x29, waiting for transfers between devices, along(): lax.ppermute(array, 'expert', [(2 * a + side, 2 * b + side) for a, b in h...  139 us
    pallas_call x5, Pallas kernels, expert_rows(): pl.pallas_call(functools.partial(expert_body, count=count, capacity=capac...  133 us
    ppermute x20, waiting for transfers between devices, across(): return lax.ppermute(array, 'expert', [(i, i ^ 1) for i in range(2 * LINE)])  110 us
    ppermute x29, starting transfers between devices, along(): lax.ppermute(array, 'expert', [(2 * a + side, 2 * b + side) for a, b in h...  79.8 us
    all_gather x1, waiting for transfers between devices, on_device(): lax.all_gather(jnp.concatenate([w_qkv, w_attn_out, gain_columns], axis=1)...  68.2 us
    pallas_call x2, Pallas kernels, expert_grads(): pl.pallas_call(expert_grads_body, grid_spec=pltpu.PrefetchScalarGridSpec(...  45.1 us
    pallas_call x1, Pallas kernels, attend_back(): pl.pallas_call(functools.partial(attend_back_body, chips=chips), grid=(st...  44.5 us
    convert_element_type x18, other arithmetic, add(): return (left.astype(F32) + right.astype(F32)).astype(BF)  37.5 us
  transfers between devices with their start and end apart: 70, of which 24 were waited for; matrix products, arithmetic and copies ran while one was open for 12% of the time, Pallas kernels for 32%

profile of v2, /device:TPU:0, one launch (start us, length us, event | category | flops | bytes accessed | tf_op | source)
XLA Modules:
  0.0 910.4 jit_solution(1728874096058950192)
XLA Ops:
  13.3 3.0 collective-permute-start
  17.6 4.6 collective-permute-start.2
  22.3 27.0 %collective-permute-done.refs_2_.refs_4_ = bf16[528,1280]{1,0:T(8,128)(2,1)} collective-permute-done((bf16[528,1280]{1,0:T(8,128)(2,1)}, bf16[528,1280]{1,0:T(8,128)(2,1)}, u32[]{:S(2)}, u32[]{:S(2)}) %collective-permute-start) | collective-permute-done | bytes 1351712 | tf_op jit(solution)/shard_map/ppermute | solution.py:573
  49.3 25.1 %collective-permute-done.1 = bf16[528,1280]{1,0:T(8,128)(2,1)S(1)} collective-permute-done((bf16[528,1280]{1,0:T(8,128)(2,1)}, bf16[528,1280]{1,0:T(8,128)(2,1)S(1)}, u32[]{:S(2)}, u32[]{:S(2)}) %collective-permute-start.1) | collective-permute-done | bytes 1351712 | tf_op jit(solution)/shard_map/ppermute | solution.py:577
  78.6 68.2 %all-gather.3.cloned.1.call-done.wq_ref.wk_ref.wv_ref.wo_ref.gains_in_ref = bf16[1280,5248]{1,0:T(8,128)(2,1)} async-done(((bf16[40,5248]{1,0:T(8,128)(2,1)}), bf16[1280,5248]{1,0:T(8,128)(2,1)}) %all-gather.3.cloned.1.call-update) | async-done | bytes 13434896 | tf_op jit(solution)/shard_map/all_gather | solution.py:767
  153.5 24.3 %attend.1 = (bf16[512,1280]{1,0:T(8,128)(2,1)S(1)}, bf16[512,1280]{1,0:T(8,128)(2,1)S(1)}, bf16[512,1280]{1,0:T(8,128)(2,1)S(1)}, bf16[512,1280]{1,0:T(8,128)(2,...) custom-call(s32[1]{0:T(128)} %copy.84.length_ref, ...), custom_call_target="tpu_custom_call" | custom-call | flops 10000000000 | bytes 25000000 | tf_op jit(solution)/shard_map/attend/pallas_call | solution.py:135
  177.8 5.5 collective-permute-done.6.refs_2_.refs_4_
  183.3 17.2 %collective-permute-done.7 = bf16[528,1280]{1,0:T(8,128)(2,1)S(1)} collective-permute-done((bf16[528,1280]{1,0:T(8,128)(2,1)S(1)}, bf16[528,1280]{1,0:T(8,128)(2,1)S(1)}, u32[]{:S(2)}, u32[]{:S(2)}) %collective-permute-start.7) | collective-permute-done | bytes 1351712 | tf_op jit(solution)/shard_map/ppermute | solution.py:577
  203.6 2.8 collective-permute-start.10
  208.6 17.8 %expert_rows.5 = (bf16[512,1280]{1,0:T(8,128)(2,1)}, bf16[512,1280]{1,0:T(8,128)(2,1)}, bf16[2,8,240,1280]{3,2,1,0:T(8,128)(2,1)}, bf16[2,8,240,896]{3,2,1,0:T(8...) custom-call(s32[1]{0:T(128)} %bitcast.5.mine_ref, ...), custom_call_target="tpu_custom_call" | custom-call | flops 9299999744 | bytes 22000000 | tf_op jit(solution)/shard_map/expert_rows/pallas_call | solution.py:438
  226.4 28.5 %collective-permute-done.10 = bf16[512,1280]{1,0:T(8,128)(2,1)S(1)} collective-permute-done((bf16[512,1280]{1,0:T(8,128)(2,1)}, bf16[512,1280]{1,0:T(8,128)(2,1)S(1)}, u32[]{:S(2)}, u32[]{:S(2)}) %collective-permute-start.10) | collective-permute-done | bytes 1310752 | tf_op jit(solution)/shard_map/ppermute | solution.py:577
  254.9 20.6 %collective-permute-done.8.refs_0_ = bf16[512,1280]{1,0:T(8,128)(2,1)} collective-permute-done((bf16[512,1280]{1,0:T(8,128)(2,1)}, bf16[512,1280]{1,0:T(8,128)(2,1)}, u32[]{:S(2)}, u32[]{:S(2)}) %collective-permute-start.8) | collective-permute-done | bytes 1310752 | tf_op jit(solution)/shard_map/ppermute | solution.py:573
  278.6 2.6 broadcast_select_fusion.5.refs_1_
  282.8 32.3 %expert_rows.6 = (bf16[512,1280]{1,0:T(8,128)(2,1)}, bf16[512,1280]{1,0:T(8,128)(2,1)}, bf16[512,1280]{1,0:T(8,128)(2,1)}, bf16[512,1280]{1,0:T(8,128)(2,1)}, bf...) custom-call(s32[1]{0:T(128)} %bitcast.5.mine_ref, ...), custom_call_target="tpu_custom_call", output_to_operand_aliasing={{4}: (9, {}), {5}: (10, {}), {6}: (11, {}), {7}: (12, {})} | custom-call | flops 18599999488 | bytes 30000000 | tf_op jit(solution)/shard_map/expert_rows/pallas_call | solution.py:438
  315.2 3.0 broadcast_select_fusion.4
  320.2 32.4 %expert_rows.7 = (bf16[512,1280]{1,0:T(8,128)(2,1)}, bf16[512,1280]{1,0:T(8,128)(2,1)}, bf16[512,1280]{1,0:T(8,128)(2,1)}, bf16[512,1280]{1,0:T(8,128)(2,1)}, bf...) custom-call(s32[1]{0:T(128)} %bitcast.5.mine_ref, ...), custom_call_target="tpu_custom_call", output_to_operand_aliasing={{4}: (9, {}), {5}: (10, {}), {6}: (11, {}), {7}: (12, {})} | custom-call | flops 18599999488 | bytes 30000000 | tf_op jit(solution)/shard_map/expert_rows/pallas_call | solution.py:438
  352.6 3.4 collective-permute-done.16
  357.3 32.9 %expert_rows.8 = (bf16[512,1280]{1,0:T(8,128)(2,1)}, bf16[512,1280]{1,0:T(8,128)(2,1)}, bf16[512,1280]{1,0:T(8,128)(2,1)}, bf16[512,1280]{1,0:T(8,128)(2,1)}, bf...) custom-call(s32[1]{0:T(128)} %bitcast.5.mine_ref, ...), custom_call_target="tpu_custom_call", output_to_operand_aliasing={{4}: (9, {}), {5}: (10, {}), {6}: (11, {}), {7}: (12, {})} | custom-call | flops 18599999488 | bytes 30000000 | tf_op jit(solution)/shard_map/expert_rows/pallas_call | solution.py:438
  391.3 17.7 %expert_rows.9 = (bf16[512,1280]{1,0:T(8,128)(2,1)}, bf16[512,1280]{1,0:T(8,128)(2,1)}, bf16[2,8,240,1280]{3,2,1,0:T(8,128)(2,1)}, bf16[2,8,240,896]{3,2,1,0:T(8...) custom-call(s32[1]{0:T(128)} %bitcast.5.mine_ref, ...), custom_call_target="tpu_custom_call", output_to_operand_aliasing={{2}: (6, {}), {3}: (7, {}), {4}: (8, {}), {5}: (9, {})} | custom-call | flops 9299999744 | bytes 22000000 | tf_op jit(solution)/shard_map/expert_rows/pallas_call | solution.py:438
  410.1 16.1 %expert_grads.3 = (bf16[896,1280]{1,0:T(8,128)(2,1)}, bf16[896,1280]{1,0:T(8,128)(2,1)}) custom-call(s32[1]{0:T(128)} %select_n.320.core_ref, bf16[2,8,240,896]{3,2,1,0:T(8,128)(2,1)} %get-tuple-element.314.left_ref, bf16[2,8,240,1280]{3,2,1,0:T(8,128)(2,1)} %get-tuple-element.315.right_ref), custom_call_target="tpu_custom_call" | custom-call | flops 8808038400 | bytes 40000000 | tf_op jit(solution)/shard_map/expert_grads/pallas_call | solution.py:482
  426.2 29.1 %expert_grads.2 = (bf16[1280,1792]{1,0:T(8,128)(2,1)}, bf16[1280,1792]{1,0:T(8,128)(2,1)}) custom-call(s32[1]{0:T(128)} %select_n.320.core_ref, bf16[2,8,240,1280]{3,2,1,0:T(8,128)(2,1)} %get-tuple-element.310.left_ref, bf16[2,8,240,1792]{3,2,1,0:T(8,128)(2,1)} %get-tuple-element.311.right_ref), custom_call_target="tpu_custom_call" | custom-call | flops 17616076800 | bytes 40000000 | tf_op jit(solution)/shard_map/expert_grads/pallas_call | solution.py:482
  469.2 4.2 reshape.145.wout_ref
  473.8 9.2 %collective-permute-start.20 = (bf16[512,1280]{1,0:T(8,128)(2,1)S(1)}, bf16[512,1280]{1,0:T(8,128)(2,1)S(1)}, u32[]{:S(2)}, u32[]{:S(2)}) collective-permute-start(bf16[512,1280]{1,0:T(8,128)(2,1)S(1)} %add_convert_fusion.16), channel_id=1, source_target_pairs={{0,2},{1,3},{6,4},{7,5},{8,10},{9,11},{14,12},{15,13},{16,18},{17,... | collective-permute-start | bytes 3932168 | tf_op jit(solution)/shard_map/ppermute | solution.py:577
  483.0 18.2 %shared_expert.1 = (f32[512,1280]{1,0:T(8,128)}, f32[512,1280]{1,0:T(8,128)}, bf16[1280,1792]{1,0:T(8,128)(2,1)}, bf16[896,1280]{1,0:T(8,128)(2,1)}) custom-call(bf16[512,1280]{1,0:T(8,128)(2,1)} %get-tuple-element.228.refs_0_.normed_ref, bf16[512,1280]{1,0:T(8,128)(2,1)} %cot_ref.3, f32[512,1280]{1,0:T(8,128)} %get-tuple-element.331.residual_ref, ...), custom_call_target="tpu_custom_call" | custom-call | flops 14000000000 | bytes 25000000 | tf_op jit(solution)/shard_map/shared_expert/pallas_call | solution.py:551
  502.2 8.0 collective-permute-done.20
  511.3 3.1 broadcast_select_fusion.3
  516.0 6.2 add_convert_fusion.19
  523.0 3.5 add_convert_fusion.26
  526.5 2.5 dynamic-slice_bitcast_fusion
  529.0 4.1 reshape.147
  535.1 5.5 collective-permute-start.27
  540.6 18.9 %collective-permute-done.29 = bf16[512,1280]{1,0:T(8,128)(2,1)} collective-permute-done((bf16[512,1280]{1,0:T(8,128)(2,1)}, bf16[512,1280]{1,0:T(8,128)(2,1)}, u32[]{:S(2)}, u32[]{:S(2)}) %collective-permute-start.29) | collective-permute-done | bytes 1310752 | tf_op jit(solution)/shard_map/ppermute | solution.py:573
  566.6 8.8 collective-permute-done.31
  576.3 20.9 %collective-permute-done.30 = bf16[320,1792]{1,0:T(8,128)(2,1)} collective-permute-done((bf16[320,1792]{1,0:T(8,128)(2,1)}, bf16[320,1792]{1,0:T(8,128)(2,1)}, u32[]{:S(2)}, u32[]{:S(2)}) %collective-permute-start.30) | collective-permute-done | bytes 1146912 | tf_op jit(solution)/shard_map/ppermute | solution.py:741
  602.2 3.1 select_select_fusion.1
  605.4 4.5 collective-permute-start.35
  609.9 19.1 %collective-permute-done.34 = bf16[512,1280]{1,0:T(8,128)(2,1)S(1)} collective-permute-done((bf16[512,1280]{1,0:T(8,128)(2,1)}, bf16[512,1280]{1,0:T(8,128)(2,1)S(1)}, u32[]{:S(2)}, u32[]{:S(2)}) %collective-permute-start.34) | collective-permute-done | bytes 1310752 | tf_op jit(solution)/shard_map/ppermute | solution.py:573
  629.0 4.5 collective-permute-start.32
  634.8 2.9 add_convert_fusion.18
  637.7 2.9 add_convert_fusion.22
  642.6 4.8 collective-permute-done.36
  649.3 13.3 %collective-permute-done.32.one_ref = bf16[512,1280]{1,0:T(8,128)(2,1)S(1)} collective-permute-done((bf16[512,1280]{1,0:T(8,128)(2,1)S(1)}, bf16[512,1280]{1,0:T(8,128)(2,1)S(1)}, u32[]{:S(2)}, u32[]{:S(2)}) %collective-permute-start.32) | collective-permute-done | bytes 1310752 | tf_op jit(solution)/shard_map/ppermute | solution.py:577
  664.1 2.7 add_convert_fusion
  674.9 5.5 collective-permute-start.39
  680.7 11.6 %middle.1 = (f32[512,1280]{1,0:T(8,128)}, bf16[512,1280]{1,0:T(8,128)(2,1)S(1)}, bf16[512,1280]{1,0:T(8,128)(2,1)S(1)}, bf16[512,1280]{1,0:T(8,128)(2,1)S(1)}) custom-call(f32[512,1280]{1,0:T(8,128)} %get-tuple-element.372.pre_ref, bf16[512,1280]{1,0:T(8,128)(2,1)S(1)} %add_convert_fusion.7.own_ref, bf16[512,1280]{1,0:T(8,128)(2,1)} %copy-done.39, ...), custom_call_target="tpu_custom_call" | custom-call | flops 4000000000 | bytes 25000000 | tf_op jit(solution)/shard_map/middle/pallas_call | solution.py:197
  698.5 44.5 %attend_back.1 = (bf16[640,3840]{1,0:T(8,128)(2,1)}, bf16[640,3840]{1,0:T(8,128)(2,1)}, f32[512,1280]{1,0:T(8,128)}, bf16[640,1408]{1,0:T(8,128)(2,1)}, bf16[640,1408]{1,0:T(8,128)(2,1)}) custom-call(s32[2]{0:T(128)} %pad_add_fusion.length_ref, bf16[512,1280]{1,0:T(8,128)(2,1)} %get-tuple-element.367.normed_ref, ...), custom_call_target="tpu_custom_call" | custom-call | flops 14000000000 | bytes 40000000 | tf_op jit(solution)/shard_map/attend_back/pallas_call | solution.py:308
  743.1 2.4 add_convert_fusion.1
  746.4 3.4 collective-permute-start.62
  749.9 2.6 copy.54
  752.9 4.6 select_select_fusion
  759.4 2.4 collective-permute-done.60
  762.9 19.0 %collective-permute-done.61 = bf16[2,40,3072]{2,1,0:T(8,128)(2,1)S(1)} collective-permute-done((bf16[2,40,3072]{2,1,0:T(8,128)(2,1)S(1)}, bf16[2,40,3072]{2,1,0:T(8,128)(2,1)S(1)}, u32[]{:S(2)}, u32[]{:S(2)}) %collective-permute-start.61) | collective-permute-done | bytes 491552 | tf_op jit(solution)/shard_map/ppermute | solution.py:577
  781.9 10.4 %collective-permute-start.44 = (bf16[512,1280]{1,0:T(8,128)(2,1)}, bf16[512,1280]{1,0:T(8,128)(2,1)}, u32[]{:S(2)}, u32[]{:S(2)}) collective-permute-start(bf16[512,1280]{1,0:T(8,128)(2,1)} %get-tuple-element.428), channel_id=1, source_target_pairs={{0,2},{1,3},{2,4},{3,5},{4,6},{5,7},{8,10},{9,11},{10,12},{11,13},... | collective-permute-start | bytes 3932168 | tf_op jit(solution)/shard_map/ppermute | solution.py:577
  798.6 7.5 both_experts.3
  807.4 7.8 collective-permute-done.55
  819.1 5.2 fusion
  824.9 2.9 collective-permute-start.58
  828.8 16.9 %collective-permute-done.45 = bf16[512,1280]{1,0:T(8,128)(2,1)S(1)} collective-permute-done((bf16[512,1280]{1,0:T(8,128)(2,1)S(1)}, bf16[512,1280]{1,0:T(8,128)(2,1)S(1)}, u32[]{:S(2)}, u32[]{:S(2)}) %collective-permute-start.45) | collective-permute-done | bytes 1310752 | tf_op jit(solution)/shard_map/ppermute | solution.py:577
  849.3 5.2 collective-permute-done.57
  855.6 15.5 %collective-permute-done.47 = bf16[2,4,40,1920]{3,2,1,0:T(8,128)(2,1)S(1)} collective-permute-done((bf16[2,4,40,1920]{3,2,1,0:T(8,128)(2,1)S(1)}, bf16[2,4,40,1920]{3,2,1,0:T(8,128)(2,1)S(1)}, u32[]{:S(2)}, u32[]{:S(2)}) %collective-permute-start.47) | collective-permute-done | bytes 1228832 | tf_op jit(solution)/shard_map/ppermute | solution.py:573
  874.6 3.7 add_convert_fusion.2
  878.3 3.4 collective-permute-done.50
  886.0 2.8 collective-permute-start.53
  890.2 11.1 %both_experts.2 = f32[2,1280,1792]{2,1,0:T(8,128)} custom-call(s32[1]{0:T(128)} %select_n.320.core_ref, bf16[1280,1792]{1,0:T(8,128)(2,1)} %pad_maximum_fusion.mine_ref, bf16[1280,1792]{1,0:T(8,128)(2,1)} %collective-permute-done.65.other_ref), custom_call_target="tpu_custom_call" | custom-call | flops 2293760 | bytes 27525120 | tf_op jit(solution)/shard_map/both_experts/pallas_call | solution.py:514
  (297 shorter events, 121.2 us)
Async XLA Ops:
  7.2 139.7 %all-gather.3.cloned.1.call-start = ((), (), s32[]{:S(2)}) async-start(), calls=%async_computation | async-start | bytes 13854720 | tf_op jit(solution)/shard_map/all_gather | solution.py:767
  9.9 445.3 %all-gather.5.cloned.1.call-start = ((), (), s32[]{:S(2)}) async-start(), calls=%async_computation.1 | async-start | bytes 8110080 | tf_op jit(solution)/shard_map/all_gather | solution.py:789
  13.3 35.9 %collective-permute-start = (bf16[528,1280]{1,0:T(8,128)(2,1)}, bf16[528,1280]{1,0:T(8,128)(2,1)}, u32[]{:S(2)}, u32[]{:S(2)}) collective-permute-start(bf16[528,1280]{1,0:T(8,128)(2,1)} %pad_maximum_fusion.2.refs_1_.refs_2_), channel_id=1, source_target_pairs={{0,1},{1,0},{2,3},{3,2},{4,5},{5,4},{6,7},{7,6},{8,9},{9,8},{10,11... | collective-permute-start | bytes 4055048 | tf_op jit(solution)/shard_map/ppermute | solution.py:573
  16.3 58.1 %collective-permute-start.1 = (bf16[528,1280]{1,0:T(8,128)(2,1)}, bf16[528,1280]{1,0:T(8,128)(2,1)S(1)}, u32[]{:S(2)}, u32[]{:S(2)}) collective-permute-start(bf16[528,1280]{1,0:T(8,128)(2,1)} %pad_maximum_fusion.2.refs_1_.refs_2_), channel_id=1, source_target_pairs={{2,0},{3,1},{4,2},{5,3},{6,4},{7,5},{10,8},{11,9},{12,10},{13,11},... | collective-permute-start | bytes 4055048 | tf_op jit(solution)/shard_map/ppermute | solution.py:577
  17.6 56.8 %collective-permute-start.2 = (bf16[528,1280]{1,0:T(8,128)(2,1)}, bf16[528,1280]{1,0:T(8,128)(2,1)S(1)}, u32[]{:S(2)}, u32[]{:S(2)}) collective-permute-start(bf16[528,1280]{1,0:T(8,128)(2,1)} %pad_maximum_fusion.2.refs_1_.refs_2_), channel_id=1, source_target_pairs={{0,2},{1,3},{2,4},{3,5},{4,6},{5,7},{8,10},{9,11},{10,12},{11,13},... | collective-permute-start | bytes 4055048 | tf_op jit(solution)/shard_map/ppermute | solution.py:577
  75.6 72.0 %collective-permute-start.3 = (bf16[528,1280]{1,0:T(8,128)(2,1)}, bf16[528,1280]{1,0:T(8,128)(2,1)}, u32[]{:S(2)}, u32[]{:S(2)}) collective-permute-start(bf16[528,1280]{1,0:T(8,128)(2,1)} %broadcast_select_fusion.1.refs_3_.refs_5_), channel_id=1, source_target_pairs={{0,1},{1,0},{2,3},{3,2},{4,5},{5,4},{6,7},{7,6},{8,9},{9,8},{10,11... | collective-permute-start | bytes 4055048 | tf_op jit(solution)/shard_map/ppermute | solution.py:573
  75.6 72.0 %collective-permute-start.4 = (bf16[528,1280]{1,0:T(8,128)(2,1)S(1)}, bf16[528,1280]{1,0:T(8,128)(2,1)}, u32[]{:S(2)}, u32[]{:S(2)}) collective-permute-start(bf16[528,1280]{1,0:T(8,128)(2,1)S(1)} %collective-permute-done.1), channel_id=1, source_target_pairs={{2,0},{3,1},{4,2},{5,3},{10,8},{11,9},{12,10},{13,11},{18,16},{19,... | collective-permute-start | bytes 4055048 | tf_op jit(solution)/shard_map/ppermute | solution.py:577
  76.9 70.7 %collective-permute-start.5 = (bf16[528,1280]{1,0:T(8,128)(2,1)S(1)}, bf16[528,1280]{1,0:T(8,128)(2,1)}, u32[]{:S(2)}, u32[]{:S(2)}) collective-permute-start(bf16[528,1280]{1,0:T(8,128)(2,1)S(1)} %collective-permute-done.2), channel_id=1, source_target_pairs={{2,4},{3,5},{4,6},{5,7},{10,12},{11,13},{12,14},{13,15},{18,20},{1... | collective-permute-start | bytes 4055048 | tf_op jit(solution)/shard_map/ppermute | solution.py:577
  149.7 33.6 %collective-permute-start.6 = (bf16[528,1280]{1,0:T(8,128)(2,1)S(1)}, bf16[528,1280]{1,0:T(8,128)(2,1)S(1)}, u32[]{:S(2)}, u32[]{:S(2)}) collective-permute-start(bf16[528,1280]{1,0:T(8,128)(2,1)S(1)} %get-tuple-element.438.refs_3_.refs_5_), channel_id=1, source_target_pairs={{0,1},{1,0},{2,3},{3,2},{4,5},{5,4},{6,7},{7,6},{8,9},{9,8},{10,11... | collective-permute-start | bytes 4055048 | tf_op jit(solution)/shard_map/ppermute | solution.py:573
  151.0 49.5 %collective-permute-start.7 = (bf16[528,1280]{1,0:T(8,128)(2,1)S(1)}, bf16[528,1280]{1,0:T(8,128)(2,1)S(1)}, u32[]{:S(2)}, u32[]{:S(2)}) collective-permute-start(bf16[528,1280]{1,0:T(8,128)(2,1)S(1)} %get-tuple-element.437), channel_id=1, source_target_pairs={{4,6},{5,7},{2,0},{3,1},{12,14},{13,15},{10,8},{11,9},{20,22},{21,... | collective-permute-start | bytes 4055048 | tf_op jit(solution)/shard_map/ppermute | solution.py:577
  201.8 73.6 %collective-permute-start.11 = (bf16[528,1280]{1,0:T(8,128)(2,1)}, bf16[528,1280]{1,0:T(8,128)(2,1)S(1)}, u32[]{:S(2)}, u32[]{:S(2)}) collective-permute-start(bf16[528,1280]{1,0:T(8,128)(2,1)} %select_select_fusion.2.refs_3_.refs_5_), channel_id=1, source_target_pairs={{0,1},{1,0},{2,3},{3,2},{4,5},{5,4},{6,7},{7,6},{8,9},{9,8},{10,11... | collective-permute-start | bytes 4055048 | tf_op jit(solution)/shard_map/ppermute | solution.py:573
  203.6 51.3 %collective-permute-start.10 = (bf16[512,1280]{1,0:T(8,128)(2,1)}, bf16[512,1280]{1,0:T(8,128)(2,1)S(1)}, u32[]{:S(2)}, u32[]{:S(2)}) collective-permute-start(bf16[512,1280]{1,0:T(8,128)(2,1)} %get-tuple-element.228.refs_0_.normed_ref), channel_id=1, source_target_pairs={{0,2},{1,3},{2,4},{3,5},{4,6},{5,7},{8,10},{9,11},{10,12},{11,13},... | collective-permute-start | bytes 3932168 | tf_op jit(solution)/shard_map/ppermute | solution.py:577
  206.5 69.0 %collective-permute-start.8 = (bf16[512,1280]{1,0:T(8,128)(2,1)}, bf16[512,1280]{1,0:T(8,128)(2,1)}, u32[]{:S(2)}, u32[]{:S(2)}) collective-permute-start(bf16[512,1280]{1,0:T(8,128)(2,1)} %get-tuple-element.228.refs_0_.normed_ref), channel_id=1, source_target_pairs={{0,1},{1,0},{2,3},{3,2},{4,5},{5,4},{6,7},{7,6},{8,9},{9,8},{10,11... | collective-permute-start | bytes 3932168 | tf_op jit(solution)/shard_map/ppermute | solution.py:573
  206.8 68.6 %collective-permute-start.9 = (bf16[512,1280]{1,0:T(8,128)(2,1)}, bf16[512,1280]{1,0:T(8,128)(2,1)}, u32[]{:S(2)}, u32[]{:S(2)}) collective-permute-start(bf16[512,1280]{1,0:T(8,128)(2,1)} %get-tuple-element.228.refs_0_.normed_ref), channel_id=1, source_target_pairs={{2,0},{3,1},{4,2},{5,3},{6,4},{7,5},{10,8},{11,9},{12,10},{13,11},... | collective-permute-start | bytes 3932168 | tf_op jit(solution)/shard_map/ppermute | solution.py:577
  275.4 39.7 %collective-permute-start.13 = (bf16[512,1280]{1,0:T(8,128)(2,1)}, bf16[512,1280]{1,0:T(8,128)(2,1)}, u32[]{:S(2)}, u32[]{:S(2)}) collective-permute-start(bf16[512,1280]{1,0:T(8,128)(2,1)} %collective-permute-done.9), channel_id=1, source_target_pairs={{2,0},{3,1},{4,2},{5,3},{10,8},{11,9},{12,10},{13,11},{18,16},{19,... | collective-permute-start | bytes 3932168 | tf_op jit(solution)/shard_map/ppermute | solution.py:577
  276.7 38.5 %collective-permute-start.14 = (bf16[512,1280]{1,0:T(8,128)(2,1)S(1)}, bf16[512,1280]{1,0:T(8,128)(2,1)}, u32[]{:S(2)}, u32[]{:S(2)}) collective-permute-start(bf16[512,1280]{1,0:T(8,128)(2,1)S(1)} %collective-permute-done.10), channel_id=1, source_target_pairs={{2,4},{3,5},{4,6},{5,7},{10,12},{11,13},{12,14},{13,15},{18,20},{1... | collective-permute-start | bytes 3932168 | tf_op jit(solution)/shard_map/ppermute | solution.py:577
  281.2 34.0 %collective-permute-start.12 = (bf16[512,1280]{1,0:T(8,128)(2,1)}, bf16[512,1280]{1,0:T(8,128)(2,1)}, u32[]{:S(2)}, u32[]{:S(2)}) collective-permute-start(bf16[512,1280]{1,0:T(8,128)(2,1)} %broadcast_select_fusion.5.refs_1_), channel_id=1, source_target_pairs={{0,1},{1,0},{2,3},{3,2},{4,5},{5,4},{6,7},{7,6},{8,9},{9,8},{10,11... | collective-permute-start | bytes 3932168 | tf_op jit(solution)/shard_map/ppermute | solution.py:573
  318.2 34.3 %collective-permute-start.15 = (bf16[512,1280]{1,0:T(8,128)(2,1)}, bf16[512,1280]{1,0:T(8,128)(2,1)}, u32[]{:S(2)}, u32[]{:S(2)}) collective-permute-start(bf16[512,1280]{1,0:T(8,128)(2,1)} %get-tuple-element.442.refs_1_), channel_id=1, source_target_pairs={{0,1},{1,0},{2,3},{3,2},{4,5},{5,4},{6,7},{7,6},{8,9},{9,8},{10,11... | collective-permute-start | bytes 3932168 | tf_op jit(solution)/shard_map/ppermute | solution.py:573
  318.7 37.3 %collective-permute-start.16 = (bf16[512,1280]{1,0:T(8,128)(2,1)S(1)}, bf16[512,1280]{1,0:T(8,128)(2,1)S(1)}, u32[]{:S(2)}, u32[]{:S(2)}) collective-permute-start(bf16[512,1280]{1,0:T(8,128)(2,1)S(1)} %get-tuple-element.441), channel_id=1, source_target_pairs={{4,6},{5,7},{2,0},{3,1},{12,14},{13,15},{10,8},{11,9},{20,22},{21,... | collective-permute-start | bytes 3932168 | tf_op jit(solution)/shard_map/ppermute | solution.py:577
  356.2 34.0 %collective-permute-start.17 = (bf16[512,1280]{1,0:T(8,128)(2,1)S(1)}, bf16[512,1280]{1,0:T(8,128)(2,1)S(1)}, u32[]{:S(2)}, u32[]{:S(2)}) collective-permute-start(bf16[512,1280]{1,0:T(8,128)(2,1)S(1)} %select_select_fusion.6.refs_1_), channel_id=1, source_target_pairs={{0,1},{1,0},{2,3},{3,2},{4,5},{5,4},{6,7},{7,6},{8,9},{9,8},{10,11... | collective-permute-start | bytes 3932168 | tf_op jit(solution)/shard_map/ppermute | solution.py:573
  409.0 46.2 %collective-permute-start.19 = (bf16[512,1280]{1,0:T(8,128)(2,1)}, bf16[512,1280]{1,0:T(8,128)(2,1)S(1)}, u32[]{:S(2)}, u32[]{:S(2)}) collective-permute-start(bf16[512,1280]{1,0:T(8,128)(2,1)} %get-tuple-element.309), channel_id=1, source_target_pairs={{0,1},{1,0},{2,3},{3,2},{4,5},{5,4},{6,7},{7,6},{8,9},{9,8},{10,11... | collective-permute-start | bytes 3932168 | tf_op jit(solution)/shard_map/ppermute | solution.py:573
  455.3 56.0 %collective-permute-start.21 = (bf16[1280,1792]{1,0:T(8,128)(2,1)}, bf16[1280,1792]{1,0:T(8,128)(2,1)}, u32[]{:S(2)}, u32[]{:S(2)}) collective-permute-start(bf16[1280,1792]{1,0:T(8,128)(2,1)} %get-tuple-element.329), channel_id=1, source_target_pairs={{0,8},{8,0},{16,24},{24,16},{1,9},{9,1},{17,25},{25,17},{2,10},{10... | collective-permute-start | bytes 13762568 | tf_op jit(solution)/shard_map/ppermute | solution.py:734
  459.6 51.7 %collective-permute-start.22 = (bf16[896,1280]{1,0:T(8,128)(2,1)}, bf16[896,1280]{1,0:T(8,128)(2,1)}, u32[]{:S(2)}, u32[]{:S(2)}) collective-permute-start(bf16[896,1280]{1,0:T(8,128)(2,1)} %get-tuple-element.330), channel_id=1, source_target_pairs={{0,8},{8,0},{16,24},{24,16},{1,9},{9,1},{17,25},{25,17},{2,10},{10... | collective-permute-start | bytes 6881288 | tf_op jit(solution)/shard_map/ppermute | solution.py:734
  463.3 71.1 %collective-permute-start.67 = (f32[16,128]{0,1:T(8,128)S(1)}, f32[16,128]{0,1:T(8,128)S(1)}, u32[]{:S(2)}, u32[]{:S(2)}) collective-permute-start(f32[16,128]{0,1:T(8,128)S(1)} %broadcast_add_fusion), channel_id=1, source_target_pairs={{0,16},{8,24},{16,0},{24,8},{1,17},{9,25},{17,1},{25,9},{2,18},{10... | collective-permute-start | bytes 24584 | tf_op jit(solution)/shard_map/ppermute | solution.py:898
  464.5 36.7 %collective-permute-start.18 = (bf16[512,1280]{1,0:T(8,128)(2,1)}, bf16[512,1280]{1,0:T(8,128)(2,1)}, u32[]{:S(2)}, u32[]{:S(2)}) collective-permute-start(bf16[512,1280]{1,0:T(8,128)(2,1)} %get-tuple-element.301), channel_id=1, source_target_pairs={{0,1},{1,0},{2,3},{3,2},{4,5},{5,4},{6,7},{7,6},{8,9},{9,8},{10,11... | collective-permute-start | bytes 3932168 | tf_op jit(solution)/shard_map/ppermute | solution.py:573
  473.8 36.4 %collective-permute-start.20 = (bf16[512,1280]{1,0:T(8,128)(2,1)S(1)}, bf16[512,1280]{1,0:T(8,128)(2,1)S(1)}, u32[]{:S(2)}, u32[]{:S(2)}) collective-permute-start(bf16[512,1280]{1,0:T(8,128)(2,1)S(1)} %add_convert_fusion.16), channel_id=1, source_target_pairs={{0,2},{1,3},{6,4},{7,5},{8,10},{9,11},{14,12},{15,13},{16,18},{17,... | collective-permute-start | bytes 3932168 | tf_op jit(solution)/shard_map/ppermute | solution.py:577
  501.2 34.0 %collective-permute-start.26 = (bf16[512,1280]{1,0:T(8,128)(2,1)}, bf16[512,1280]{1,0:T(8,128)(2,1)S(1)}, u32[]{:S(2)}, u32[]{:S(2)}) collective-permute-start(bf16[512,1280]{1,0:T(8,128)(2,1)} %get-tuple-element.345), channel_id=1, source_target_pairs={{0,1},{1,0},{2,3},{3,2},{4,5},{5,4},{6,7},{7,6},{8,9},{9,8},{10,11... | collective-permute-start | bytes 3932168 | tf_op jit(solution)/shard_map/ppermute | solution.py:573
  510.2 49.3 %collective-permute-start.29 = (bf16[512,1280]{1,0:T(8,128)(2,1)}, bf16[512,1280]{1,0:T(8,128)(2,1)}, u32[]{:S(2)}, u32[]{:S(2)}) collective-permute-start(bf16[512,1280]{1,0:T(8,128)(2,1)} %get-tuple-element.349), channel_id=1, source_target_pairs={{0,1},{1,0},{2,3},{3,2},{4,5},{5,4},{6,7},{7,6},{8,9},{9,8},{10,11... | collective-permute-start | bytes 3932168 | tf_op jit(solution)/shard_map/ppermute | solution.py:573
  522.2 43.3 %collective-permute-start.64 = (bf16[320,1792]{1,0:T(8,128)(2,1)}, bf16[320,1792]{1,0:T(8,128)(2,1)}, u32[]{:S(2)}, u32[]{:S(2)}) collective-permute-start(bf16[320,1792]{1,0:T(8,128)(2,1)} %get-tuple-element.423), channel_id=1, source_target_pairs={{0,16},{8,24},{16,0},{24,8},{1,17},{9,25},{17,1},{25,9},{2,18},{10... | collective-permute-start | bytes 3440648 | tf_op jit(solution)/shard_map/ppermute | solution.py:741
  533.1 42.3 %collective-permute-start.31 = (bf16[448,1280]{1,0:T(8,128)(2,1)}, bf16[448,1280]{1,0:T(8,128)(2,1)}, u32[]{:S(2)}, u32[]{:S(2)}) collective-permute-start(bf16[448,1280]{1,0:T(8,128)(2,1)} %get-tuple-element.436), channel_id=1, source_target_pairs={{0,16},{8,24},{16,0},{24,8},{1,17},{9,25},{17,1},{25,9},{2,18},{10... | collective-permute-start | bytes 3440648 | tf_op jit(solution)/shard_map/ppermute | solution.py:741
  534.4 62.8 %collective-permute-start.30 = (bf16[320,1792]{1,0:T(8,128)(2,1)}, bf16[320,1792]{1,0:T(8,128)(2,1)}, u32[]{:S(2)}, u32[]{:S(2)}) collective-permute-start(bf16[320,1792]{1,0:T(8,128)(2,1)} %get-tuple-element.426), channel_id=1, source_target_pairs={{0,16},{8,24},{16,0},{24,8},{1,17},{9,25},{17,1},{25,9},{2,18},{10... | collective-permute-start | bytes 3440648 | tf_op jit(solution)/shard_map/ppermute | solution.py:741
  535.1 63.0 %collective-permute-start.27 = (bf16[512,1280]{1,0:T(8,128)(2,1)}, bf16[512,1280]{1,0:T(8,128)(2,1)}, u32[]{:S(2)}, u32[]{:S(2)}) collective-permute-start(bf16[512,1280]{1,0:T(8,128)(2,1)} %broadcast_select_fusion.7), channel_id=1, source_target_pairs={{0,2},{1,3},{2,4},{3,5},{8,10},{9,11},{10,12},{11,13},{16,18},{17,... | collective-permute-start | bytes 3932168 | tf_op jit(solution)/shard_map/ppermute | solution.py:577
  559.5 39.4 %collective-permute-start.28 = (bf16[512,1280]{1,0:T(8,128)(2,1)}, bf16[512,1280]{1,0:T(8,128)(2,1)}, u32[]{:S(2)}, u32[]{:S(2)}) collective-permute-start(bf16[512,1280]{1,0:T(8,128)(2,1)} %get-tuple-element.421), channel_id=1, source_target_pairs={{6,4},{7,5},{4,2},{5,3},{14,12},{15,13},{12,10},{13,11},{22,20},{2... | collective-permute-start | bytes 3932168 | tf_op jit(solution)/shard_map/ppermute | solution.py:577
  565.4 97.2 %collective-permute-start.38 = (bf16[2,4,2,40,3072]{4,3,2,1,0:T(8,128)(2,1)}, bf16[2,4,2,40,3072]{4,3,2,1,0:T(8,128)(2,1)}, u32[]{:S(2)}, u32[]{:S(2)}) collective-permute-start(bf16[2,4,2,40,3072]{4,3,2,1,0:T(8,128)(2,1)} %fusion.3), channel_id=1, source_target_pairs={{0,8},{8,0},{16,24},{24,16},{1,9},{9,1},{17,25},{25,17},{2,10},{10... | collective-permute-start | bytes 11796488 | tf_op jit(solution)/shard_map/ppermute | solution.py:673
  575.3 30.0 %collective-permute-start.25 = (bf16[512,1280]{1,0:T(8,128)(2,1)}, bf16[512,1280]{1,0:T(8,128)(2,1)S(1)}, u32[]{:S(2)}, u32[]{:S(2)}) collective-permute-start(bf16[512,1280]{1,0:T(8,128)(2,1)} %get-tuple-element.343), channel_id=1, source_target_pairs={{0,1},{1,0},{2,3},{3,2},{4,5},{5,4},{6,7},{7,6},{8,9},{9,8},{10,11... | collective-permute-start | bytes 3932168 | tf_op jit(solution)/shard_map/ppermute | solution.py:573
  597.2 31.8 %collective-permute-start.34 = (bf16[512,1280]{1,0:T(8,128)(2,1)}, bf16[512,1280]{1,0:T(8,128)(2,1)S(1)}, u32[]{:S(2)}, u32[]{:S(2)}) collective-permute-start(bf16[512,1280]{1,0:T(8,128)(2,1)} %get-tuple-element.357), channel_id=1, source_target_pairs={{0,1},{1,0},{2,3},{3,2},{4,5},{5,4},{6,7},{7,6},{8,9},{9,8},{10,11... | collective-permute-start | bytes 3932168 | tf_op jit(solution)/shard_map/ppermute | solution.py:573
  598.2 35.3 %collective-permute-start.37 = (bf16[448,1280]{1,0:T(8,128)(2,1)}, bf16[448,1280]{1,0:T(8,128)(2,1)S(1)}, u32[]{:S(2)}, u32[]{:S(2)}) collective-permute-start(bf16[448,1280]{1,0:T(8,128)(2,1)} %get-tuple-element.435), channel_id=1, source_target_pairs={{0,16},{8,24},{16,0},{24,8},{1,17},{9,25},{17,1},{25,9},{2,18},{10... | collective-permute-start | bytes 3440648 | tf_op jit(solution)/shard_map/ppermute | solution.py:741
  598.9 48.5 %collective-permute-start.36 = (bf16[320,1792]{1,0:T(8,128)(2,1)}, bf16[320,1792]{1,0:T(8,128)(2,1)S(1)}, u32[]{:S(2)}, u32[]{:S(2)}) collective-permute-start(bf16[320,1792]{1,0:T(8,128)(2,1)} %get-tuple-element.425), channel_id=1, source_target_pairs={{0,16},{8,24},{16,0},{24,8},{1,17},{9,25},{17,1},{25,9},{2,18},{10... | collective-permute-start | bytes 3440648 | tf_op jit(solution)/shard_map/ppermute | solution.py:741
  605.4 43.2 %collective-permute-start.35 = (bf16[512,1280]{1,0:T(8,128)(2,1)S(1)}, bf16[512,1280]{1,0:T(8,128)(2,1)S(1)}, u32[]{:S(2)}, u32[]{:S(2)}) collective-permute-start(bf16[512,1280]{1,0:T(8,128)(2,1)S(1)} %add_convert_fusion.10), channel_id=1, source_target_pairs={{0,2},{1,3},{6,4},{7,5},{8,10},{9,11},{14,12},{15,13},{16,18},{17,... | collective-permute-start | bytes 3932168 | tf_op jit(solution)/shard_map/ppermute | solution.py:577
  629.0 33.6 %collective-permute-start.32 = (bf16[512,1280]{1,0:T(8,128)(2,1)S(1)}, bf16[512,1280]{1,0:T(8,128)(2,1)S(1)}, u32[]{:S(2)}, u32[]{:S(2)}) collective-permute-start(bf16[512,1280]{1,0:T(8,128)(2,1)S(1)} %get-tuple-element.430), channel_id=1, source_target_pairs={{0,2},{1,3},{2,4},{3,5},{4,6},{5,7},{8,10},{9,11},{10,12},{11,13},... | collective-permute-start | bytes 3932168 | tf_op jit(solution)/shard_map/ppermute | solution.py:577
  633.5 29.1 %collective-permute-start.33 = (bf16[512,1280]{1,0:T(8,128)(2,1)S(1)}, bf16[512,1280]{1,0:T(8,128)(2,1)S(1)}, u32[]{:S(2)}, u32[]{:S(2)}) collective-permute-start(bf16[512,1280]{1,0:T(8,128)(2,1)S(1)} %get-tuple-element.429), channel_id=1, source_target_pairs={{6,4},{7,5},{4,2},{5,3},{2,0},{3,1},{14,12},{15,13},{12,10},{13,11... | collective-permute-start | bytes 3932168 | tf_op jit(solution)/shard_map/ppermute | solution.py:577
  647.4 48.3 %collective-permute-start.24 = (bf16[512,1280]{1,0:T(8,128)(2,1)}, bf16[512,1280]{1,0:T(8,128)(2,1)S(1)}, u32[]{:S(2)}, u32[]{:S(2)}) collective-permute-start(bf16[512,1280]{1,0:T(8,128)(2,1)} %get-tuple-element.341), channel_id=1, source_target_pairs={{0,1},{1,0},{2,3},{3,2},{4,5},{5,4},{6,7},{7,6},{8,9},{9,8},{10,11... | collective-permute-start | bytes 3932168 | tf_op jit(solution)/shard_map/ppermute | solution.py:573
  648.6 94.5 %collective-permute-start.41 = (bf16[320,1792]{1,0:T(8,128)(2,1)}, bf16[320,1792]{1,0:T(8,128)(2,1)}, u32[]{:S(2)}, u32[]{:S(2)}) collective-permute-start(bf16[320,1792]{1,0:T(8,128)(2,1)} %get-tuple-element.424), channel_id=1, source_target_pairs={{0,16},{8,24},{16,0},{24,8},{1,17},{9,25},{17,1},{25,9},{2,18},{10... | collective-permute-start | bytes 3440648 | tf_op jit(solution)/shard_map/ppermute | solution.py:741
  668.2 74.9 %collective-permute-start.43 = (bf16[1,4,2,40,3072]{4,3,2,1,0:T(8,128)(2,1)}, bf16[1,4,2,40,3072]{4,3,2,1,0:T(8,128)(2,1)}, u32[]{:S(2)}, u32[]{:S(2)}) collective-permute-start(bf16[1,4,2,40,3072]{4,3,2,1,0:T(8,128)(2,1)} %constant_dynamic-slice_fusion.3), channel_id=1, source_target_pairs={{0,16},{8,24},{16,0},{24,8},{1,17},{9,25},{17,1},{25,9},{2,18},{10... | collective-permute-start | bytes 5898248 | tf_op jit(solution)/shard_map/ppermute | solution.py:686
  671.0 72.0 %collective-permute-start.42 = (bf16[896,1280]{1,0:T(8,128)(2,1)}, bf16[896,1280]{1,0:T(8,128)(2,1)}, u32[]{:S(2)}, u32[]{:S(2)}) collective-permute-start(bf16[896,1280]{1,0:T(8,128)(2,1)} %pad_maximum_fusion.1.mine_ref), channel_id=1, source_target_pairs={{0,8},{8,0},{16,24},{24,16},{1,9},{9,1},{17,25},{25,17},{2,10},{10... | collective-permute-start | bytes 6881288 | tf_op jit(solution)/shard_map/ppermute | solution.py:746
  674.9 68.2 %collective-permute-start.39 = (bf16[512,1280]{1,0:T(8,128)(2,1)}, bf16[512,1280]{1,0:T(8,128)(2,1)}, u32[]{:S(2)}, u32[]{:S(2)}) collective-permute-start(bf16[512,1280]{1,0:T(8,128)(2,1)} %broadcast_select_fusion.6), channel_id=1, source_target_pairs={{0,2},{1,3},{2,4},{3,5},{8,10},{9,11},{10,12},{11,13},{16,18},{17,... | collective-permute-start | bytes 3932168 | tf_op jit(solution)/shard_map/ppermute | solution.py:577
  696.8 46.3 %collective-permute-start.40 = (bf16[512,1280]{1,0:T(8,128)(2,1)}, bf16[512,1280]{1,0:T(8,128)(2,1)}, u32[]{:S(2)}, u32[]{:S(2)}) collective-permute-start(bf16[512,1280]{1,0:T(8,128)(2,1)} %get-tuple-element.419), channel_id=1, source_target_pairs={{6,4},{7,5},{4,2},{5,3},{14,12},{15,13},{12,10},{13,11},{22,20},{2... | collective-permute-start | bytes 3932168 | tf_op jit(solution)/shard_map/ppermute | solution.py:577
  745.7 16.1 %collective-permute-start.60 = (bf16[2,40,3072]{2,1,0:T(8,128)(2,1)S(1)}, bf16[2,40,3072]{2,1,0:T(8,128)(2,1)S(1)}, u32[]{:S(2)}, u32[]{:S(2)}) collective-permute-start(bf16[2,40,3072]{2,1,0:T(8,128)(2,1)S(1)} %get-tuple-element.445), channel_id=1, source_target_pairs={{0,2},{1,3},{2,4},{3,5},{4,6},{5,7},{6,0},{7,1},{8,10},{9,11},{10,... | collective-permute-start | bytes 1474568 | tf_op jit(solution)/shard_map/ppermute | solution.py:577
  745.8 36.1 %collective-permute-start.61 = (bf16[2,40,3072]{2,1,0:T(8,128)(2,1)S(1)}, bf16[2,40,3072]{2,1,0:T(8,128)(2,1)S(1)}, u32[]{:S(2)}, u32[]{:S(2)}) collective-permute-start(bf16[2,40,3072]{2,1,0:T(8,128)(2,1)S(1)} %get-tuple-element.444), channel_id=1, source_target_pairs={{0,4},{1,5},{2,6},{3,7},{4,0},{5,1},{6,2},{7,3},{8,12},{9,13},{10,... | collective-permute-start | bytes 1474568 | tf_op jit(solution)/shard_map/ppermute | solution.py:577
  746.4 45.9 %collective-permute-start.62 = (bf16[2,40,3072]{2,1,0:T(8,128)(2,1)S(1)}, bf16[2,40,3072]{2,1,0:T(8,128)(2,1)S(1)}, u32[]{:S(2)}, u32[]{:S(2)}) collective-permute-start(bf16[2,40,3072]{2,1,0:T(8,128)(2,1)S(1)} %get-tuple-element.443), channel_id=1, source_target_pairs={{0,6},{1,7},{2,0},{3,1},{4,2},{5,3},{6,4},{7,5},{8,14},{9,15},{10,... | collective-permute-start | bytes 1474568 | tf_op jit(solution)/shard_map/ppermute | solution.py:577
  749.8 42.7 %collective-permute-start.54 = (bf16[2,4,2,40,1408]{4,3,2,1,0:T(8,128)(2,1)S(1)}, bf16[2,4,2,40,1408]{4,3,2,1,0:T(8,128)(2,1)S(1)}, u32[]{:S(2)}, u32[]{:S(2)}) collective-permute-start(bf16[2,4,2,40,1408]{4,3,2,1,0:T(8,128)(2,1)S(1)} %bitcast.121), channel_id=1, source_target_pairs={{0,8},{8,0},{16,24},{24,16},{1,9},{9,1},{17,25},{25,17},{2,10},{10... | collective-permute-start | bytes 5406728 | tf_op jit(solution)/shard_map/ppermute | solution.py:673
  752.4 64.5 %collective-permute-start.46 = (bf16[2,4,2,40,3840]{4,3,1,2,0:T(8,128)(2,1)}, bf16[2,4,2,40,3840]{4,3,1,2,0:T(8,128)(2,1)}, u32[]{:S(2)}, u32[]{:S(2)}) collective-permute-start(bf16[2,4,2,40,3840]{4,3,1,2,0:T(8,128)(2,1)} %copy.54), channel_id=1, source_target_pairs={{0,8},{8,0},{16,24},{24,16},{1,9},{9,1},{17,25},{25,17},{2,10},{10... | collective-permute-start | bytes 14745608 | tf_op jit(solution)/shard_map/ppermute | solution.py:673
  761.8 63.1 %collective-permute-start.23 = (bf16[512,1280]{1,0:T(8,128)(2,1)}, bf16[512,1280]{1,0:T(8,128)(2,1)}, u32[]{:S(2)}, u32[]{:S(2)}) collective-permute-start(bf16[512,1280]{1,0:T(8,128)(2,1)} %get-tuple-element.339), channel_id=1, source_target_pairs={{0,1},{1,0},{2,3},{3,2},{4,5},{5,4},{6,7},{7,6},{8,9},{9,8},{10,11... | collective-permute-start | bytes 3932168 | tf_op jit(solution)/shard_map/ppermute | solution.py:573
  781.9 45.9 %collective-permute-start.44 = (bf16[512,1280]{1,0:T(8,128)(2,1)}, bf16[512,1280]{1,0:T(8,128)(2,1)}, u32[]{:S(2)}, u32[]{:S(2)}) collective-permute-start(bf16[512,1280]{1,0:T(8,128)(2,1)} %get-tuple-element.428), channel_id=1, source_target_pairs={{0,2},{1,3},{2,4},{3,5},{4,6},{5,7},{8,10},{9,11},{10,12},{11,13},... | collective-permute-start | bytes 3932168 | tf_op jit(solution)/shard_map/ppermute | solution.py:577
  794.1 21.1 %collective-permute-start.55 = (bf16[1,4,2,40,1408]{4,3,2,1,0:T(8,128)(2,1)}, bf16[1,4,2,40,1408]{4,3,2,1,0:T(8,128)(2,1)}, u32[]{:S(2)}, u32[]{:S(2)}) collective-permute-start(bf16[1,4,2,40,1408]{4,3,2,1,0:T(8,128)(2,1)} %constant_dynamic-slice_fusion), channel_id=1, source_target_pairs={{0,16},{8,24},{16,0},{24,8},{1,17},{9,25},{17,1},{25,9},{2,18},{10... | collective-permute-start | bytes 2703368 | tf_op jit(solution)/shard_map/ppermute | solution.py:686
  806.1 39.7 %collective-permute-start.45 = (bf16[512,1280]{1,0:T(8,128)(2,1)S(1)}, bf16[512,1280]{1,0:T(8,128)(2,1)S(1)}, u32[]{:S(2)}, u32[]{:S(2)}) collective-permute-start(bf16[512,1280]{1,0:T(8,128)(2,1)S(1)} %copy-done.31), channel_id=1, source_target_pairs={{6,4},{7,5},{4,2},{5,3},{2,0},{3,1},{14,12},{15,13},{12,10},{13,11... | collective-permute-start | bytes 3932168 | tf_op jit(solution)/shard_map/ppermute | solution.py:577
  816.7 32.5 %collective-permute-start.56 = (bf16[2,40,1408]{2,1,0:T(8,128)(2,1)S(1)}, bf16[2,40,1408]{2,1,0:T(8,128)(2,1)S(1)}, u32[]{:S(2)}, u32[]{:S(2)}) collective-permute-start(bf16[2,40,1408]{2,1,0:T(8,128)(2,1)S(1)} %get-tuple-element.451), channel_id=1, source_target_pairs={{0,2},{1,3},{2,4},{3,5},{4,6},{5,7},{6,0},{7,1},{8,10},{9,11},{10,... | collective-permute-start | bytes 675848 | tf_op jit(solution)/shard_map/ppermute | solution.py:577
  817.0 37.5 %collective-permute-start.57 = (bf16[2,40,1408]{2,1,0:T(8,128)(2,1)S(1)}, bf16[2,40,1408]{2,1,0:T(8,128)(2,1)S(1)}, u32[]{:S(2)}, u32[]{:S(2)}) collective-permute-start(bf16[2,40,1408]{2,1,0:T(8,128)(2,1)S(1)} %get-tuple-element.450), channel_id=1, source_target_pairs={{0,4},{1,5},{2,6},{3,7},{4,0},{5,1},{6,2},{7,3},{8,12},{9,13},{10,... | collective-permute-start | bytes 675848 | tf_op jit(solution)/shard_map/ppermute | solution.py:577
  824.9 29.5 %collective-permute-start.58 = (bf16[2,40,1408]{2,1,0:T(8,128)(2,1)S(1)}, bf16[2,40,1408]{2,1,0:T(8,128)(2,1)S(1)}, u32[]{:S(2)}, u32[]{:S(2)}) collective-permute-start(bf16[2,40,1408]{2,1,0:T(8,128)(2,1)S(1)} %get-tuple-element.449), channel_id=1, source_target_pairs={{0,6},{1,7},{2,0},{3,1},{4,2},{5,3},{6,4},{7,5},{8,14},{9,15},{10,... | collective-permute-start | bytes 675848 | tf_op jit(solution)/shard_map/ppermute | solution.py:577
  827.8 27.8 %collective-permute-start.48 = (bf16[1,4,2,40,1920]{4,3,1,2,0:T(8,128)(2,1)S(1)}, bf16[1,4,2,40,1920]{4,3,1,2,0:T(8,128)(2,1)S(1)}, u32[]{:S(2)}, u32[]{:S(2)}) collective-permute-start(bf16[1,4,2,40,1920]{4,3,1,2,0:T(8,128)(2,1)S(1)} %constant_dynamic-slice_fusion.2), channel_id=1, source_target_pairs={{0,16},{8,24},{16,0},{24,8},{1,17},{9,25},{17,1},{25,9},{2,18},{10... | collective-permute-start | bytes 3686408 | tf_op jit(solution)/shard_map/ppermute | solution.py:686
  845.8 25.3 %collective-permute-start.47 = (bf16[2,4,40,1920]{3,2,1,0:T(8,128)(2,1)S(1)}, bf16[2,4,40,1920]{3,2,1,0:T(8,128)(2,1)S(1)}, u32[]{:S(2)}, u32[]{:S(2)}) collective-permute-start(bf16[2,4,40,1920]{3,2,1,0:T(8,128)(2,1)S(1)} %dynamic-slice_bitcast_fusion.4), channel_id=1, source_target_pairs={{0,1},{1,0},{2,3},{3,2},{4,5},{5,4},{6,7},{7,6},{8,9},{9,8},{10,11... | collective-permute-start | bytes 3686408 | tf_op jit(solution)/shard_map/ppermute | solution.py:573
  849.2 41.1 %collective-permute-start.65 = (bf16[1280,1792]{1,0:T(8,128)(2,1)S(1)}, bf16[1280,1792]{1,0:T(8,128)(2,1)}, u32[]{:S(2)}, u32[]{:S(2)}) collective-permute-start(bf16[1280,1792]{1,0:T(8,128)(2,1)S(1)} %bitcast.110), channel_id=1, source_target_pairs={{0,8},{8,0},{16,24},{24,16},{1,9},{9,1},{17,25},{25,17},{2,10},{10... | collective-permute-start | bytes 13762568 | tf_op jit(solution)/shard_map/ppermute | solution.py:746
  854.6 23.7 %collective-permute-start.59 = (bf16[40,1408]{1,0:T(8,128)(2,1)S(1)}, bf16[40,1408]{1,0:T(8,128)(2,1)S(1)}, u32[]{:S(2)}, u32[]{:S(2)}) collective-permute-start(bf16[40,1408]{1,0:T(8,128)(2,1)S(1)} %fusion.29), channel_id=1, source_target_pairs={{0,1},{1,0},{2,3},{3,2},{4,5},{5,4},{6,7},{7,6},{8,9},{9,8},{10,11... | collective-permute-start | bytes 337928 | tf_op jit(solution)/shard_map/ppermute | solution.py:573
  883.5 17.8 %collective-permute-start.51 = (bf16[40,3840]{1,0:T(8,128)(2,1)S(1)}, bf16[40,3840]{1,0:T(8,128)(2,1)S(1)}, u32[]{:S(2)}, u32[]{:S(2)}) collective-permute-start(bf16[40,3840]{1,0:T(8,128)(2,1)S(1)} %get-tuple-element.447), channel_id=1, source_target_pairs={{0,2},{1,3},{2,4},{3,5},{4,6},{5,7},{6,0},{7,1},{8,10},{9,11},{10,... | collective-permute-start | bytes 921608 | tf_op jit(solution)/shard_map/ppermute | solution.py:577
  (61 other events, 1378.5 us)
Sparse Core Ops, SparseCore 0:
  11.4 135.3 all-gather.2
  149.8 101.8 all-gather.4

commit v3 on v2

--- a/solution.py
+++ b/solution.py
@@ -214,7 +214,7 @@
     length_ref, normed_ref, wq_ref, wk_ref, wv_ref, cos_ref, sin_ref, tokens_ref, gain_ref,
     q_ref, k_ref, v_ref, datt_ref, lse_ref, gr_ref, grb_ref, att_ref, prod_ref,
     mine_ref, other_ref, gtok_ref, mine_late_ref, other_late_ref,
-    gq_ref, gk_ref, gv_ref, total_ref, *, chips,
+    g3_ref, total_ref, turned_ref, *, chips,
 ):
     step = pl.program_id(0)
     normed = normed_ref[...]
@@ -225,16 +225,15 @@
     unit = width // (2 * chips)
 
     def store(refs, columns, block):
-        block = block.astype(BF)
         for mine in range(2):
 
             @pl.when(core == mine)
             def _(mine=mine):
                 for n in range(2 * chips):
                     ref = refs[0] if n % 2 == mine else refs[1]
-                    ref[n // 2 * unit : (n // 2 + 1) * unit, columns] = block[
-                        n * unit : (n + 1) * unit
-                    ]
+                    ref[n // 2 * unit : (n // 2 + 1) * unit, columns] = block(
+                        slice(n * unit, (n + 1) * unit)
+                    ).astype(BF)
 
     half = row_count // 2
     for head in range(2):
@@ -251,29 +250,29 @@
             delta = jnp.sum(grad_probs * probs, axis=1, keepdims=True)
             grad_scores = (probs * (grad_probs - delta)).astype(BF)
             grad_values.append(dot(probs.astype(BF), grad, 0, 0))
-            gq_ref[start:stop, here] = turn_back(
+            g3_ref[start:stop, here] = turn_back(
                 dot(grad_scores, k) * scale, cosine[start:stop], sine[start:stop]
             ).astype(BF)
             grad_keys.append(dot(grad_scores, q, 0, 0) * scale)
-        for out_ref, (first, second), turned in (
-            (gk_ref, grad_keys, True),
-            (gv_ref, grad_values, False),
-        ):
+        for n, (first, second) in enumerate((grad_keys, grad_values)):
             whole = jnp.concatenate([first + second[:half], second[half:]], axis=0)
-            if turned:
+            if n == 0:
                 whole = turn_back(whole, cosine, sine)
-            out_ref[:, here] = whole.astype(BF)
+            there = (n + 1) * PAIR + head * HEAD_DIM
+            g3_ref[:, there : there + HEAD_DIM] = whole.astype(BF)
 
     @pl.when(step == 0)
     def _():
         total_ref[...] = jnp.zeros_like(total_ref)
-
-    offset = pl.multiple_of(step * 3 * PAIR, PAIR)
+        turned_ref[...] = normed.astype(F32).T.astype(BF)
+
     refs = (mine_ref, other_ref)
-    for n, (grad_ref, w_ref) in enumerate(((gq_ref, wq_ref), (gk_ref, wk_ref), (gv_ref, wv_ref))):
-        grad = grad_ref[...]
-        store(refs, pl.ds(offset + n * PAIR, PAIR), dot(normed, grad, 0, 0))
-        total_ref[...] += dot(grad, w_ref[...], 1, 1)
+    columns = pl.ds(pl.multiple_of(step * 3 * PAIR, PAIR), 3 * PAIR)
+    store(refs, columns, lambda some: dot(turned_ref[some], g3_ref[...]))
+    total = total_ref[...]
+    for n, w_ref in enumerate((wq_ref, wk_ref, wv_ref)):
+        total = total + dot(g3_ref[:, n * PAIR : (n + 1) * PAIR], w_ref[...], 1, 1)
+    total_ref[...] = total
 
     @pl.when(step == pl.num_programs(0) - 1)
     def _():
@@ -289,12 +288,12 @@
         first = jnp.where(lane == 0, 1.0, 0.0).astype(BF)
         second = jnp.where(lane == 1, 1.0, 0.0).astype(BF)
         refs = (mine_late_ref, other_late_ref)
-        store(
-            refs,
-            slice(width, width + HEAD_DIM),
-            dot((grad * value * r).astype(BF), first, 0, 0) + dot(prod_ref[...], second, 0, 0),
+        gain_grads = dot((grad * value * r).astype(BF), first, 0, 0) + dot(
+            prod_ref[...], second, 0, 0
         )
-        store(refs, slice(0, width), dot(att_ref[...], grb_ref[...], 0, 0))
+        store(refs, slice(width, width + HEAD_DIM), lambda some: gain_grads[some])
+        turned_ref[...] = att_ref[...].astype(F32).T.astype(BF)
+        store(refs, slice(0, width), lambda some: dot(turned_ref[some], grb_ref[...]))
 
 
 def attend_back(
@@ -328,7 +327,11 @@
         out_shape=[shaped(width // 2, 3 * width)] * 2
         + [shaped(rows, width, dtype=F32)]
         + [shaped(width // 2, width + HEAD_DIM)] * 2,
-        scratch_shapes=[pltpu.VMEM((rows, PAIR), BF)] * 3 + [pltpu.VMEM((rows, width), F32)],
+        scratch_shapes=[
+            pltpu.VMEM((rows, 3 * PAIR), BF),
+            pltpu.VMEM((rows, width), F32),
+            pltpu.VMEM((width, rows), BF),
+        ],
         compiler_params=pltpu.CompilerParams(vmem_limit_bytes=56 * 2**20),
         cost_estimate=kernel_cost(14_000_000_000, 40_000_000),
         name="attend_back",
@@ -635,24 +638,57 @@
     return slots
 
 
+def outer_sums(place, s2, r2, s3, t3):
+    s2, s3 = s2 + r2, s3 + t3
+    return jnp.where(place == 0, s2, s3), jnp.where(place == LINE - 1, s2, s3), s2
+
+
+def inner_sums(place, s1, r1, s2, up, down):
+    s1 = s1 + r1
+    m1 = s1 + jnp.where(place == 1, up, down)
+    m2 = s2 + jnp.where(place == 1, down, up)
+    return by_place(place, [s1, m1, m2]), by_place(place, [m2, m2, m1, s1])
+
+
+def by_rows(function, place, results, *arrays):
+    rows, width = arrays[0].shape
+    block = pl.BlockSpec((rows // 4, width), lambda i, place: (i, 0))
+
+    def body(place_ref, *refs):
+        values = [ref[...].astype(F32) for ref in refs[:-results]]
+        for ref, value in zip(refs[-results:], function(place_ref[0], *values)):
+            ref[...] = value.astype(BF)
+
+    return pl.pallas_call(
+        body,
+        grid_spec=pltpu.PrefetchScalarGridSpec(
+            num_scalar_prefetch=1,
+            grid=(4,),
+            in_specs=[block] * len(arrays),
+            out_specs=[block] * results,
+        ),
+        out_shape=[shaped(rows, width)] * results,
+        cost_estimate=kernel_cost(
+            8 * rows * width, 2 * rows * width * (len(arrays) + results)
+        ),
+        name=function.__name__,
+    )(place[None], *arrays)
+
+
 def reduce_steps(place, parts):
     own, y0, s1, y1, s2, y2, s3, y3 = parts
     (r3,) = yield (across(y3),)
     s3 = add(s3, r3)
     r2, t3 = yield (across(y2), along(s3, [(0, 1), (3, 2)]))
-    s2, s3 = add(s2, r2), add(s3, t3)
+    up, down, s2 = by_rows(outer_sums, place, 3, s2, r2, s3, t3)
     r1, up, down = yield (
-        across(y1),
-        along(jnp.where(place == 0, s2, s3), [(0, 1), (1, 2)]),
-        along(jnp.where(place == 3, s2, s3), [(3, 2), (2, 1)]),
-    )
-    s1 = add(s1, r1)
-    m1 = add(s1, jnp.where(place == 1, up, down))
-    m2 = add(s2, jnp.where(place == 1, down, up))
+        across(y1), along(up, [(0, 1), (1, 2)]), along(down, [(3, 2), (2, 1)])
+    )
+    up, down = by_rows(inner_sums, place, 2, s1, r1, s2, up, down)
     r0, up, down = yield (
         across(y0),
-        along(by_place(place, [s1, m1, m2]), [(0, 1), (1, 2), (2, 3)]),
-        along(by_place(place, [m2, m2, m1, s1]), [(3, 2), (2, 1), (1, 0)]),
+        along(up, [(0, 1), (1, 2), (2, 3)]),
+        along(down, [(3, 2), (2, 1), (1, 0)]),
     )
     return add(own, r0), up, down
 
@@ -690,25 +726,13 @@
             part = add(pick_half(part, bit, 0), got)
         return part
 
-    if not split:
-        part = yield from over_chips(total)
-        part = part[0]
-        arrived = yield tuple(
-            along(
-                pick_half(part, (place + hop) % LINE, 0),
-                [(n, (n + hop) % LINE) for n in range(LINE)],
-            )
-            for hop in range(1, LINE)
-        )
-        part = pick_half(part, place, 0).astype(F32)
-        for block in arrived:
-            part = part + block.astype(F32)
-        (got,) = yield (across(pick_half(part, 1 - side, 0).astype(BF)),)
-        return pick_half(part, side, 0) + got.astype(F32)
-
-    cut = columns // 256 * 128
-    parts = [total[..., :cut], total[..., cut:]]
-    for kinds in ((over_side, over_chips), (over_chips, over_side)):
+    if split:
+        cut = columns // 256 * 128
+        parts = [total[..., :cut], total[..., cut:]]
+        rounds = ((over_side, over_chips), (over_chips, over_side))
+    else:
+        parts, rounds = [total], ((over_chips,), (over_side,))
+    for kinds in rounds:
         flows = [Flow(kind(part)) for kind, part in zip(kinds, parts)]
         while any(f.result is None for f in flows):
             open_flows = [f for f in flows if f.result is None]
@@ -761,14 +785,20 @@
     shared_width = share_out * devices
     place, side = lax.axis_index("expert") // 2, lax.axis_index("expert") % 2
 
-    gain_columns = jnp.pad(
-        jnp.stack([gain_attn, gain_ffn], axis=1), ((0, 0), (0, HEAD_DIM - 2))
-    )
+    live = jnp.arange(rows) < seq_lengths[0]
+    ids = jnp.where(live[:, None], route_ids, -1).astype(F32).T
+    own_counts = jnp.sum(
+        (ids[None] == jnp.arange(experts_total, dtype=F32)[:, None, None]).astype(jnp.int32),
+        axis=(1, 2),
+    )
+    count_rows = jnp.pad(
+        jnp.stack([own_counts % 256, own_counts // 256]), ((0, share - 2), (0, 0))
+    ).astype(BF)
+    extra = jnp.concatenate([gain_attn[:, None], gain_ffn[:, None], count_rows], axis=1)
+    gain_columns = jnp.pad(extra, ((0, 0), (0, HEAD_DIM - extra.shape[1])))
     attn_full = lax.all_gather(
         jnp.concatenate([w_qkv, w_attn_out, gain_columns], axis=1), BOTH, axis=0, tiled=True
     )
-    live = jnp.arange(rows) < seq_lengths[0]
-    ids = jnp.where(live[:, None], route_ids, -1).astype(F32).T
     high = lax.reduce_precision(route_gates.T, 8, 7)
     middle_bits = lax.reduce_precision(route_gates.T - high, 8, 7)
     low = route_gates.T - high - middle_bits
@@ -785,20 +815,11 @@
     mine = lax.axis_index("expert")[None] * experts
     cosine, sine = rotary_tables(rows)
     advance([grads_flow])
-    attn_full, w_shared_in, w_shared_out = together((attn_full, w_shared_in, w_shared_out))
-    shared_full = lax.all_gather(
-        jnp.concatenate(
-            [w_shared_in, jnp.pad(w_shared_out, ((0, share - share_out), (0, 0)))], axis=1
-        ),
-        BOTH,
-        axis=0,
-        tiled=True,
-    )
     advance([grads_flow])
 
-    q, k, v, att, lse, normed_first, gains, residual, normed_second = advance(
-        [grads_flow], attend(seq_lengths, attn_full, cosine, sine, tokens)
-    )
+    attended = attend(seq_lengths, attn_full, cosine, sine, tokens)
+    q, k, v, att, lse, normed_first, gains, residual, normed_second = attended
+    advance([grads_flow], normed_second)
 
     arrived, back, out, kept = [], [], [], [None]
     rows_flow = Flow(gather_steps(normed_second, place, arrived))
@@ -812,35 +833,40 @@
         back.extend(new_back)
         out.extend(new_out)
 
+    shares_in = jnp.concatenate(
+        [w_shared_in, jnp.pad(w_shared_out, ((0, share - share_out), (0, 0)))], axis=1
+    )
+    shared_full = None
     through()
     while rows_flow.result is None:
         more = [f for f in (grads_flow,) if f.result is None]
-        back[:], out[:], kept[0] = advance([rows_flow] + more, (back, out, kept[0]))
+        back[:], out[:], kept[0], shares_in = advance(
+            [rows_flow] + more, (back, out, kept[0], shares_in)
+        )
         through()
+        if shared_full is None and len(arrived) > 5:
+            shared_full = lax.all_gather(shares_in, BOTH, axis=0, tiled=True)
     x, hidden, result_grad, gate_up_grad = kept[0]
 
     back_flow = Flow(reduce_steps(place, back))
     core = lax.axis_index("dp")[None] % 2
+    grad_down = expert_grads(core, hidden, result_grad, width)
+    grad_down, x, out = advance([back_flow], (grad_down, x, out))
+    down_flow = Flow(dp_sum_steps(*grad_down, core, 1))
     grad_in = expert_grads(core, x, gate_up_grad, shared_width)
-    grad_down = expert_grads(core, hidden, result_grad, width)
-    grad_in, grad_down, out, shared_full = advance(
-        [back_flow], (grad_in, grad_down, out, shared_full)
-    )
-
-    out_flow = Flow(reduce_steps(place, out))
-    in_flow = Flow(dp_sum_steps(*grad_in, core, 4))
-    down_flow = Flow(dp_sum_steps(*grad_down, core, 2))
-    pre, layer_sum, grad_shared_in, grad_shared_out = shared_expert(
-        normed_second,
-        cotangent,
-        residual,
-        shared_full,
+    shared_out_full = (
         shared_full[:, 2 * shared_width :]
         .reshape(devices, share, width)[:, :share_out]
-        .reshape(shared_width, width),
-    )
+        .reshape(shared_width, width)
+    )
+    out_flow = Flow(reduce_steps(place, out))
+    grad_in, shared_full, shared_out_full = advance(
+        [back_flow, down_flow], (grad_in, shared_full, shared_out_full)
+    )
+    in_flow = Flow(dp_sum_steps(*grad_in, core, 2))
     pre, layer_sum, grad_shared_in, grad_shared_out = advance(
-        [back_flow, in_flow, down_flow], (pre, layer_sum, grad_shared_in, grad_shared_out)
+        [back_flow, in_flow, down_flow, out_flow],
+        shared_expert(normed_second, cotangent, residual, shared_full, shared_out_full),
     )
 
     def of_core(which):
@@ -853,8 +879,7 @@
         )
 
     shared_flow = Flow(home_steps(of_core(core[0]), of_core(1 - core[0]), split=False))
-    advance([back_flow, out_flow, in_flow, down_flow])
-    advance([back_flow, out_flow, in_flow, down_flow, shared_flow])
+    advance([back_flow, in_flow])
     own, up, down = back_flow.result
 
     gr, grb, datt, prod = middle(pre, own, up, down, residual, cotangent, gains, attn_full)
@@ -887,22 +912,13 @@
         .reshape(share, 3 * width)
     )
 
-    all_ids = jnp.stack([g[rows : rows + TOP, :rows] for g in grads])
-    counts = jnp.sum(
-        (all_ids[None] == jnp.arange(experts_total, dtype=BF)[:, None, None, None]).astype(F32),
-        axis=(1, 2, 3),
-    )
-    counts = jnp.broadcast_to(counts[:, None], (experts_total, HEAD_DIM))
-    step = 1
-    while step < devices // groups:
-        counts = counts + lax.ppermute(
-            counts, "dp", [(i, i ^ step) for i in range(devices // groups)]
-        )
-        step *= 2
+    digits = attn_full[:, 4 * width + 2 : 4 * width + 2 + experts_total].astype(F32)
+    digits = jnp.sum(digits.reshape(devices, share, experts_total)[:, :2], axis=0)
+    counts = (digits[0] + 256.0 * digits[1]).astype(jnp.int32)
     return (
         block_out, grad_tokens, share_qkv, late[:, :width], share_in, share_down,
         late[:, width], late[:, width + 1], in_flow.result, down_flow.result,
-        counts[:, 0].astype(jnp.int32),
+        counts,
     )
 
 

time: 919 us -> 836 us (0.910)
  waiting for transfers between devices: 363 us -> 267 us
  Pallas kernels: 295 us -> 311 us
  other arithmetic: 84.1 us -> 69.3 us
    ppermute x20, waiting for transfers between devices: 110 us -> 172 us  [across(): return lax.ppermute(array, 'expert', [(i, i ^ 1) for i in range(2 * LINE)])]
    ppermute x29, waiting for transfers between devices: 139 us -> 77.6 us  [along(): lax.ppermute(array, 'expert', [(2 * a + side, 2 * b + side) for a, b in h...]
    all_gather x1, waiting for transfers between devices: 68.2 us -> 7.16 us  [on_device(): lax.all_gather(jnp.concatenate([w_qkv, w_attn_out, gain_columns], axis=1)...]
    ppermute x6 -> x3, waiting for transfers between devices: 34.5 us -> 0.01 us  [dp_sum_steps(): lax.ppermute(piece, 'dp', [(i, i ^ step) for i in range(count)])]
    pallas_call x0 -> x4, Pallas kernels: none -> 20.5 us  [by_rows(): pl.pallas_call(body, grid_spec=pltpu.PrefetchScalarGridSpec(num_scalar_pr...]
    dynamic_slice x0 -> x6, local copies, waits for them, and re-layouts: none -> 9.42 us  [pick_half(): return lax.dynamic_index_in_dim(array, bit, dim, keepdims=False)]
    convert_element_type x18 -> x17, other arithmetic: 37.5 us -> 40.8 us  [add(): return (left.astype(F32) + right.astype(F32)).astype(BF)]
  transfers between devices with their start and end apart: 70 -> 65, of which waited for: 24 -> 28; matrix products, arithmetic and copies ran while one was open for 12% -> 11% of each run, Pallas kernels for 32% -> 38%
where the time goes in v3:
time: 836 us; the launch traced here: 822 us
  Pallas kernels  311 us (37%)
  waiting for transfers between devices  267 us (32%)
  starting transfers between devices  112 us (13%)
  other arithmetic  69.3 us (8%)
  local copies, waits for them, and re-layouts  46.3 us (6%)
  between operations  16.1 us (2%)
    ppermute x20, waiting for transfers between devices, across(): return lax.ppermute(array, 'expert', [(i, i ^ 1) for i in range(2 * LINE)])  172 us
    pallas_call x5, Pallas kernels, expert_rows(): pl.pallas_call(functools.partial(expert_body, count=count, capacity=capac...  133 us
    ppermute x29, waiting for transfers between devices, along(): lax.ppermute(array, 'expert', [(2 * a + side, 2 * b + side) for a, b in h...  77.6 us
    ppermute x29, starting transfers between devices, along(): lax.ppermute(array, 'expert', [(2 * a + side, 2 * b + side) for a, b in h...  75.5 us
    pallas_call x2, Pallas kernels, expert_grads(): pl.pallas_call(expert_grads_body, grid_spec=pltpu.PrefetchScalarGridSpec(...  46 us
    convert_element_type x17, other arithmetic, add(): return (left.astype(F32) + right.astype(F32)).astype(BF)  40.8 us
    pallas_call x1, Pallas kernels, attend_back(): pl.pallas_call(functools.partial(attend_back_body, chips=chips), grid=(st...  39.1 us
    ppermute x20, starting transfers between devices, across(): return lax.ppermute(array, 'expert', [(i, i ^ 1) for i in range(2 * LINE)])  27.6 us
  transfers between devices with their start and end apart: 65, of which 28 were waited for; matrix products, arithmetic and copies ran while one was open for 11% of the time, Pallas kernels for 38%

profile of v3, /device:TPU:0, one launch (start us, length us, event | category | flops | bytes accessed | tf_op | source)
XLA Modules:
  0.0 822.4 jit_solution(1787300235329555409)
XLA Ops:
  14.3 3.0 collective-permute-start.3
  18.6 4.6 collective-permute-start.5
  23.2 27.0 %collective-permute-done.3.refs_2_.refs_4_ = bf16[528,1280]{1,0:T(8,128)(2,1)} collective-permute-done((bf16[528,1280]{1,0:T(8,128)(2,1)}, bf16[528,1280]{1,0:T(8,128)(2,1)}, u32[]{:S(2)}, u32[]{:S(2)}) %collective-permute-start.3) | collective-permute-done | bytes 1351712 | tf_op jit(solution)/shard_map/ppermute | solution.py:576
  50.2 25.1 %collective-permute-done.4 = bf16[528,1280]{1,0:T(8,128)(2,1)S(1)} collective-permute-done((bf16[528,1280]{1,0:T(8,128)(2,1)}, bf16[528,1280]{1,0:T(8,128)(2,1)S(1)}, u32[]{:S(2)}, u32[]{:S(2)}) %collective-permute-start.4) | collective-permute-done | bytes 1351712 | tf_op jit(solution)/shard_map/ppermute | solution.py:580
  79.6 44.1 %collective-permute-done.6.refs_2_.refs_4_ = bf16[528,1280]{1,0:T(8,128)(2,1)} collective-permute-done((bf16[528,1280]{1,0:T(8,128)(2,1)}, bf16[528,1280]{1,0:T(8,128)(2,1)}, u32[]{:S(2)}, u32[]{:S(2)}) %collective-permute-start.6) | collective-permute-done | bytes 1351712 | tf_op jit(solution)/shard_map/ppermute | solution.py:576
  123.8 7.2 collective-permute-done.7
  131.0 3.7 broadcast_select_fusion
  136.0 3.5 collective-permute-start.9
  140.7 7.2 all-gather.3.cloned.1.call-done.wq_ref.wk_ref.wv_ref.wo_ref.gains_in_ref
  147.8 24.1 %attend.1 = (bf16[512,1280]{1,0:T(8,128)(2,1)S(1)}, bf16[512,1280]{1,0:T(8,128)(2,1)S(1)}, bf16[512,1280]{1,0:T(8,128)(2,1)S(1)}, bf16[512,1280]{1,0:T(8,128)(2,...) custom-call(s32[1]{0:T(128)} %copy.117.length_ref, ...), custom_call_target="tpu_custom_call" | custom-call | flops 10000000000 | bytes 25000000 | tf_op jit(solution)/shard_map/attend/pallas_call | solution.py:135
  172.0 8.2 collective-permute-done.10
  182.6 2.8 collective-permute-start.11
  186.8 7.6 collective-permute-start.2
  195.2 17.7 %expert_rows.5 = (bf16[512,1280]{1,0:T(8,128)(2,1)}, bf16[512,1280]{1,0:T(8,128)(2,1)}, bf16[2,8,240,1280]{3,2,1,0:T(8,128)(2,1)}, bf16[2,8,240,896]{3,2,1,0:T(8...) custom-call(s32[1]{0:T(128)} %bitcast.6.mine_ref, ...), custom_call_target="tpu_custom_call" | custom-call | flops 9299999744 | bytes 22000000 | tf_op jit(solution)/shard_map/expert_rows/pallas_call | solution.py:441
  212.9 27.3 %collective-permute-done.refs_0_ = bf16[512,1280]{1,0:T(8,128)(2,1)} collective-permute-done((bf16[512,1280]{1,0:T(8,128)(2,1)}, bf16[512,1280]{1,0:T(8,128)(2,1)}, u32[]{:S(2)}, u32[]{:S(2)}) %collective-permute-start) | collective-permute-done | bytes 1310752 | tf_op jit(solution)/shard_map/ppermute | solution.py:576
  246.4 32.3 %expert_rows.6 = (bf16[512,1280]{1,0:T(8,128)(2,1)}, bf16[512,1280]{1,0:T(8,128)(2,1)}, bf16[512,1280]{1,0:T(8,128)(2,1)}, bf16[512,1280]{1,0:T(8,128)(2,1)}, bf...) custom-call(s32[1]{0:T(128)} %bitcast.6.mine_ref, ...), custom_call_target="tpu_custom_call", output_to_operand_aliasing={{4}: (9, {}), {5}: (10, {}), {6}: (11, {}), {7}: (12, {})} | custom-call | flops 18599999488 | bytes 30000000 | tf_op jit(solution)/shard_map/expert_rows/pallas_call | solution.py:441
  278.8 3.9 broadcast_select_fusion.2
  284.5 32.4 %expert_rows.7 = (bf16[512,1280]{1,0:T(8,128)(2,1)}, bf16[512,1280]{1,0:T(8,128)(2,1)}, bf16[512,1280]{1,0:T(8,128)(2,1)}, bf16[512,1280]{1,0:T(8,128)(2,1)}, bf...) custom-call(s32[1]{0:T(128)} %bitcast.6.mine_ref, ...), custom_call_target="tpu_custom_call", output_to_operand_aliasing={{4}: (9, {}), {5}: (10, {}), {6}: (11, {}), {7}: (12, {})} | custom-call | flops 18599999488 | bytes 30000000 | tf_op jit(solution)/shard_map/expert_rows/pallas_call | solution.py:441
  317.0 2.8 collective-permute-done.16
  321.6 32.9 %expert_rows.8 = (bf16[512,1280]{1,0:T(8,128)(2,1)}, bf16[512,1280]{1,0:T(8,128)(2,1)}, bf16[512,1280]{1,0:T(8,128)(2,1)}, bf16[512,1280]{1,0:T(8,128)(2,1)}, bf...) custom-call(s32[1]{0:T(128)} %bitcast.6.mine_ref, ...), custom_call_target="tpu_custom_call", output_to_operand_aliasing={{4}: (9, {}), {5}: (10, {}), {6}: (11, {}), {7}: (12, {})} | custom-call | flops 18599999488 | bytes 30000000 | tf_op jit(solution)/shard_map/expert_rows/pallas_call | solution.py:441
  355.6 17.9 %expert_rows.9 = (bf16[512,1280]{1,0:T(8,128)(2,1)}, bf16[512,1280]{1,0:T(8,128)(2,1)}, bf16[2,8,240,1280]{3,2,1,0:T(8,128)(2,1)}, bf16[2,8,240,896]{3,2,1,0:T(8...) custom-call(s32[1]{0:T(128)} %bitcast.6.mine_ref, ...), custom_call_target="tpu_custom_call", output_to_operand_aliasing={{2}: (6, {}), {3}: (7, {}), {4}: (8, {}), {5}: (9, {})} | custom-call | flops 9299999744 | bytes 22000000 | tf_op jit(solution)/shard_map/expert_rows/pallas_call | solution.py:441
  374.4 17.0 %expert_grads.2 = (bf16[896,1280]{1,0:T(8,128)(2,1)}, bf16[896,1280]{1,0:T(8,128)(2,1)}) custom-call(s32[1]{0:T(128)} %select_n.273.core_ref, bf16[2,8,240,896]{3,2,1,0:T(8,128)(2,1)} %get-tuple-element.305.left_ref, bf16[2,8,240,1280]{3,2,1,0:T(8,128)(2,1)} %get-tuple-element.306.right_ref), custom_call_target="tpu_custom_call" | custom-call | flops 8808038400 | bytes 40000000 | tf_op jit(solution)/shard_map/expert_grads/pallas_call | solution.py:485
  391.4 20.4 %collective-permute-done.20 = bf16[512,1280]{1,0:T(8,128)(2,1)S(1)} collective-permute-done((bf16[512,1280]{1,0:T(8,128)(2,1)}, bf16[512,1280]{1,0:T(8,128)(2,1)S(1)}, u32[]{:S(2)}, u32[]{:S(2)}) %collective-permute-start.20) | collective-permute-done | bytes 1310752 | tf_op jit(solution)/shard_map/ppermute | solution.py:576
  414.4 13.4 %collective-permute-start.21 = (bf16[512,1280]{1,0:T(8,128)(2,1)}, bf16[512,1280]{1,0:T(8,128)(2,1)}, u32[]{:S(2)}, u32[]{:S(2)}) collective-permute-start(bf16[512,1280]{1,0:T(8,128)(2,1)} %add_convert_fusion.12.refs_2_), channel_id=1, source_target_pairs={{0,2},{1,3},{6,4},{7,5},{8,10},{9,11},{14,12},{15,13},{16,18},{17,... | collective-permute-start | bytes 3932168 | tf_op jit(solution)/shard_map/ppermute | solution.py:580
  427.9 29.0 %expert_grads.3 = (bf16[1280,1792]{1,0:T(8,128)(2,1)}, bf16[1280,1792]{1,0:T(8,128)(2,1)}) custom-call(s32[1]{0:T(128)} %select_n.273.core_ref, bf16[2,8,240,1280]{3,2,1,0:T(8,128)(2,1)} %get-tuple-element.320.left_ref, bf16[2,8,240,1792]{3,2,1,0:T(8,128)(2,1)} %get-tuple-element.321.right_ref), custom_call_target="tpu_custom_call" | custom-call | flops 17616076800 | bytes 40000000 | tf_op jit(solution)/shard_map/expert_grads/pallas_call | solution.py:485
  460.6 4.1 reshape.249.wout_ref
  466.3 2.9 add_convert_fusion.6
  473.1 5.0 outer_sums.2
  480.5 16.3 %collective-permute-done.18.refs_1_ = bf16[512,1280]{1,0:T(8,128)(2,1)} collective-permute-done((bf16[512,1280]{1,0:T(8,128)(2,1)}, bf16[512,1280]{1,0:T(8,128)(2,1)}, u32[]{:S(2)}, u32[]{:S(2)}) %collective-permute-start.18) | collective-permute-done | bytes 1310752 | tf_op jit(solution)/shard_map/ppermute | solution.py:576
  498.9 18.3 %shared_expert.1 = (f32[512,1280]{1,0:T(8,128)}, f32[512,1280]{1,0:T(8,128)}, bf16[1280,1792]{1,0:T(8,128)(2,1)}, bf16[896,1280]{1,0:T(8,128)(2,1)}) custom-call(bf16[512,1280]{1,0:T(8,128)(2,1)} %get-tuple-element.214.refs_0_.normed_ref, bf16[512,1280]{1,0:T(8,128)(2,1)} %cot_ref.3, f32[512,1280]{1,0:T(8,128)} %get-tuple-element.332.residual_ref, ...), custom_call_target="tpu_custom_call" | custom-call | flops 14000000000 | bytes 25000000 | tf_op jit(solution)/shard_map/shared_expert/pallas_call | solution.py:554
  517.2 7.2 collective-permute-done.27
  524.5 4.7 add_convert_fusion.3
  535.9 2.7 constant_dynamic-slice_fusion.2
  543.0 5.2 inner_sums.2
  548.2 4.6 collective-permute-start.36
  561.8 2.9 add_convert_fusion.4.mine_ref
  564.7 8.4 %collective-permute-done.35 = bf16[512,1280]{1,0:T(8,128)(2,1)} collective-permute-done((bf16[512,1280]{1,0:T(8,128)(2,1)}, bf16[512,1280]{1,0:T(8,128)(2,1)}, u32[]{:S(2)}, u32[]{:S(2)}) %collective-permute-start.35) | collective-permute-done | bytes 1310752 | tf_op jit(solution)/shard_map/ppermute | solution.py:576
  574.5 6.9 collective-permute-done.36.one_ref
  581.4 5.0 collective-permute-done.37.two_ref
  586.4 4.7 collective-permute-start.31
  592.9 11.5 %middle.1 = (f32[512,1280]{1,0:T(8,128)}, bf16[512,1280]{1,0:T(8,128)(2,1)S(1)}, bf16[512,1280]{1,0:T(8,128)(2,1)S(1)}, bf16[512,1280]{1,0:T(8,128)(2,1)S(1)}) custom-call(f32[512,1280]{1,0:T(8,128)} %get-tuple-element.358.pre_ref, bf16[512,1280]{1,0:T(8,128)(2,1)S(1)} %add_convert_fusion.10.own_ref, bf16[512,1280]{1,0:T(8,128)(2,1)} %copy-done.31, ...), custom_call_target="tpu_custom_call" | custom-call | flops 4000000000 | bytes 25000000 | tf_op jit(solution)/shard_map/middle/pallas_call | solution.py:197
  607.6 39.1 %attend_back.1 = (bf16[640,3840]{1,0:T(8,128)(2,1)}, bf16[640,3840]{1,0:T(8,128)(2,1)}, f32[512,1280]{1,0:T(8,128)}, bf16[640,1408]{1,0:T(8,128)(2,1)}, bf16[640,1408]{1,0:T(8,128)(2,1)}) custom-call(s32[2]{0:T(128)} %pad_add_fusion.length_ref, bf16[512,1280]{1,0:T(8,128)(2,1)} %get-tuple-element.353.normed_ref, ...), custom_call_target="tpu_custom_call" | custom-call | flops 14000000000 | bytes 40000000 | tf_op jit(solution)/shard_map/attend_back/pallas_call | solution.py:307
  647.6 2.9 copy.80
  650.5 5.0 outer_sums.3
  657.6 4.1 add_convert_fusion
  666.3 4.3 add_convert_fusion.2
  670.5 2.6 copy.77
  673.1 3.6 collective-permute-done.29.refs_1_
  676.7 3.7 add_convert_fusion.1
  680.4 5.6 collective-permute-done.39.refs_3_
  688.3 5.3 inner_sums.3
  693.6 5.3 collective-permute-start.41
  703.4 6.6 collective-permute-done.57
  720.4 7.4 both_experts.3
  727.7 3.7 collective-permute-done.42
  735.2 6.7 collective-permute-done.58
  746.0 5.0 fusion
  754.9 3.6 add_convert_fusion.8
  761.1 9.6 %collective-permute-done.60 = bf16[40,3072]{1,0:T(8,128)(2,1)S(1)} collective-permute-done((bf16[40,3072]{1,0:T(8,128)(2,1)S(1)}, bf16[40,3072]{1,0:T(8,128)(2,1)S(1)}, u32[]{:S(2)}, u32[]{:S(2)}) %collective-permute-start.60) | collective-permute-done | bytes 245792 | tf_op jit(solution)/shard_map/ppermute | solution.py:580
  772.0 3.4 collective-permute-start.55
  783.8 8.1 collective-permute-done.47
  794.2 2.7 collective-permute-start.49
  798.9 11.1 %both_experts.2 = f32[2,1280,1792]{2,1,0:T(8,128)} custom-call(s32[1]{0:T(128)} %select_n.273.core_ref, bf16[1280,1792]{1,0:T(8,128)(2,1)} %pad_maximum_fusion.mine_ref, bf16[1280,1792]{1,0:T(8,128)(2,1)} %collective-permute-done.62.other_ref), custom_call_target="tpu_custom_call" | custom-call | flops 2293760 | bytes 27525120 | tf_op jit(solution)/shard_map/both_experts/pallas_call | solution.py:517
  810.0 3.4 collective-permute-done.49
  (259 shorter events, 128.0 us)
Async XLA Ops:
  7.2 140.6 %all-gather.3.cloned.1.call-start = ((), (), s32[]{:S(2)}) async-start(), calls=%async_computation | async-start | bytes 13854720 | tf_op jit(solution)/shard_map/all_gather | solution.py:799
  12.3 444.6 %all-gather.5.cloned.1.call-start = ((), (), s32[]{:S(2)}) async-start(), calls=%async_computation.1 | async-start | bytes 8110080 | tf_op jit(solution)/shard_map/all_gather | solution.py:848
  14.3 35.9 %collective-permute-start.3 = (bf16[528,1280]{1,0:T(8,128)(2,1)}, bf16[528,1280]{1,0:T(8,128)(2,1)}, u32[]{:S(2)}, u32[]{:S(2)}) collective-permute-start(bf16[528,1280]{1,0:T(8,128)(2,1)} %pad_maximum_fusion.1.refs_1_.refs_2_), channel_id=1, source_target_pairs={{0,1},{1,0},{2,3},{3,2},{4,5},{5,4},{6,7},{7,6},{8,9},{9,8},{10,11... | collective-permute-start | bytes 4055048 | tf_op jit(solution)/shard_map/ppermute | solution.py:576
  17.3 58.0 %collective-permute-start.4 = (bf16[528,1280]{1,0:T(8,128)(2,1)}, bf16[528,1280]{1,0:T(8,128)(2,1)S(1)}, u32[]{:S(2)}, u32[]{:S(2)}) collective-permute-start(bf16[528,1280]{1,0:T(8,128)(2,1)} %pad_maximum_fusion.1.refs_1_.refs_2_), channel_id=1, source_target_pairs={{2,0},{3,1},{4,2},{5,3},{6,4},{7,5},{10,8},{11,9},{12,10},{13,11},... | collective-permute-start | bytes 4055048 | tf_op jit(solution)/shard_map/ppermute | solution.py:580
  18.6 56.7 %collective-permute-start.5 = (bf16[528,1280]{1,0:T(8,128)(2,1)}, bf16[528,1280]{1,0:T(8,128)(2,1)S(1)}, u32[]{:S(2)}, u32[]{:S(2)}) collective-permute-start(bf16[528,1280]{1,0:T(8,128)(2,1)} %pad_maximum_fusion.1.refs_1_.refs_2_), channel_id=1, source_target_pairs={{0,2},{1,3},{2,4},{3,5},{4,6},{5,7},{8,10},{9,11},{10,12},{11,13},... | collective-permute-start | bytes 4055048 | tf_op jit(solution)/shard_map/ppermute | solution.py:580
  76.6 47.2 %collective-permute-start.6 = (bf16[528,1280]{1,0:T(8,128)(2,1)}, bf16[528,1280]{1,0:T(8,128)(2,1)}, u32[]{:S(2)}, u32[]{:S(2)}) collective-permute-start(bf16[528,1280]{1,0:T(8,128)(2,1)} %broadcast_select_fusion.1.refs_3_.refs_5_), channel_id=1, source_target_pairs={{0,1},{1,0},{2,3},{3,2},{4,5},{5,4},{6,7},{7,6},{8,9},{9,8},{10,11... | collective-permute-start | bytes 4055048 | tf_op jit(solution)/shard_map/ppermute | solution.py:576
  76.6 54.4 %collective-permute-start.7 = (bf16[528,1280]{1,0:T(8,128)(2,1)S(1)}, bf16[528,1280]{1,0:T(8,128)(2,1)}, u32[]{:S(2)}, u32[]{:S(2)}) collective-permute-start(bf16[528,1280]{1,0:T(8,128)(2,1)S(1)} %collective-permute-done.4), channel_id=1, source_target_pairs={{2,0},{3,1},{4,2},{5,3},{10,8},{11,9},{12,10},{13,11},{18,16},{19,... | collective-permute-start | bytes 4055048 | tf_op jit(solution)/shard_map/ppermute | solution.py:580
  77.9 53.1 %collective-permute-start.8 = (bf16[528,1280]{1,0:T(8,128)(2,1)S(1)}, bf16[528,1280]{1,0:T(8,128)(2,1)}, u32[]{:S(2)}, u32[]{:S(2)}) collective-permute-start(bf16[528,1280]{1,0:T(8,128)(2,1)S(1)} %collective-permute-done.5), channel_id=1, source_target_pairs={{2,4},{3,5},{4,6},{5,7},{10,12},{11,13},{12,14},{13,15},{18,20},{1... | collective-permute-start | bytes 4055048 | tf_op jit(solution)/shard_map/ppermute | solution.py:580
  134.7 45.5 %collective-permute-start.10 = (bf16[528,1280]{1,0:T(8,128)(2,1)}, bf16[528,1280]{1,0:T(8,128)(2,1)S(1)}, u32[]{:S(2)}, u32[]{:S(2)}) collective-permute-start(bf16[528,1280]{1,0:T(8,128)(2,1)} %get-tuple-element.427), channel_id=1, source_target_pairs={{4,6},{5,7},{2,0},{3,1},{12,14},{13,15},{10,8},{11,9},{20,22},{21,... | collective-permute-start | bytes 4055048 | tf_op jit(solution)/shard_map/ppermute | solution.py:580
  136.0 44.2 %collective-permute-start.9 = (bf16[528,1280]{1,0:T(8,128)(2,1)}, bf16[528,1280]{1,0:T(8,128)(2,1)S(1)}, u32[]{:S(2)}, u32[]{:S(2)}) collective-permute-start(bf16[528,1280]{1,0:T(8,128)(2,1)} %get-tuple-element.428.refs_3_.refs_5_), channel_id=1, source_target_pairs={{0,1},{1,0},{2,3},{3,2},{4,5},{5,4},{6,7},{7,6},{8,9},{9,8},{10,11... | collective-permute-start | bytes 4055048 | tf_op jit(solution)/shard_map/ppermute | solution.py:576
  182.6 57.6 %collective-permute-start.11 = (bf16[528,1280]{1,0:T(8,128)(2,1)}, bf16[528,1280]{1,0:T(8,128)(2,1)S(1)}, u32[]{:S(2)}, u32[]{:S(2)}) collective-permute-start(bf16[528,1280]{1,0:T(8,128)(2,1)} %select_select_fusion.refs_3_.refs_5_), channel_id=1, source_target_pairs={{0,1},{1,0},{2,3},{3,2},{4,5},{5,4},{6,7},{7,6},{8,9},{9,8},{10,11... | collective-permute-start | bytes 4055048 | tf_op jit(solution)/shard_map/ppermute | solution.py:576
  185.4 54.8 %collective-permute-start = (bf16[512,1280]{1,0:T(8,128)(2,1)}, bf16[512,1280]{1,0:T(8,128)(2,1)}, u32[]{:S(2)}, u32[]{:S(2)}) collective-permute-start(bf16[512,1280]{1,0:T(8,128)(2,1)} %get-tuple-element.214.refs_0_.normed_ref), channel_id=1, source_target_pairs={{0,1},{1,0},{2,3},{3,2},{4,5},{5,4},{6,7},{7,6},{8,9},{9,8},{10,11... | collective-permute-start | bytes 3932168 | tf_op jit(solution)/shard_map/ppermute | solution.py:576
  185.5 54.7 %collective-permute-start.1 = (bf16[512,1280]{1,0:T(8,128)(2,1)}, bf16[512,1280]{1,0:T(8,128)(2,1)S(1)}, u32[]{:S(2)}, u32[]{:S(2)}) collective-permute-start(bf16[512,1280]{1,0:T(8,128)(2,1)} %get-tuple-element.214.refs_0_.normed_ref), channel_id=1, source_target_pairs={{2,0},{3,1},{4,2},{5,3},{6,4},{7,5},{10,8},{11,9},{12,10},{13,11},... | collective-permute-start | bytes 3932168 | tf_op jit(solution)/shard_map/ppermute | solution.py:580
  186.8 53.4 %collective-permute-start.2 = (bf16[512,1280]{1,0:T(8,128)(2,1)}, bf16[512,1280]{1,0:T(8,128)(2,1)}, u32[]{:S(2)}, u32[]{:S(2)}) collective-permute-start(bf16[512,1280]{1,0:T(8,128)(2,1)} %get-tuple-element.214.refs_0_.normed_ref), channel_id=1, source_target_pairs={{0,2},{1,3},{2,4},{3,5},{4,6},{5,7},{8,10},{9,11},{10,12},{11,13},... | collective-permute-start | bytes 3932168 | tf_op jit(solution)/shard_map/ppermute | solution.py:580
  240.2 38.6 %collective-permute-start.13 = (bf16[512,1280]{1,0:T(8,128)(2,1)S(1)}, bf16[512,1280]{1,0:T(8,128)(2,1)}, u32[]{:S(2)}, u32[]{:S(2)}) collective-permute-start(bf16[512,1280]{1,0:T(8,128)(2,1)S(1)} %collective-permute-done.1), channel_id=1, source_target_pairs={{2,0},{3,1},{4,2},{5,3},{10,8},{11,9},{12,10},{13,11},{18,16},{19,... | collective-permute-start | bytes 3932168 | tf_op jit(solution)/shard_map/ppermute | solution.py:580
  242.7 36.1 %collective-permute-start.14 = (bf16[512,1280]{1,0:T(8,128)(2,1)}, bf16[512,1280]{1,0:T(8,128)(2,1)}, u32[]{:S(2)}, u32[]{:S(2)}) collective-permute-start(bf16[512,1280]{1,0:T(8,128)(2,1)} %collective-permute-done.2), channel_id=1, source_target_pairs={{2,4},{3,5},{4,6},{5,7},{10,12},{11,13},{12,14},{13,15},{18,20},{1... | collective-permute-start | bytes 3932168 | tf_op jit(solution)/shard_map/ppermute | solution.py:580
  244.6 34.2 %collective-permute-start.12 = (bf16[512,1280]{1,0:T(8,128)(2,1)}, bf16[512,1280]{1,0:T(8,128)(2,1)S(1)}, u32[]{:S(2)}, u32[]{:S(2)}) collective-permute-start(bf16[512,1280]{1,0:T(8,128)(2,1)} %broadcast_select_fusion.3.refs_1_), channel_id=1, source_target_pairs={{0,1},{1,0},{2,3},{3,2},{4,5},{5,4},{6,7},{7,6},{8,9},{9,8},{10,11... | collective-permute-start | bytes 3932168 | tf_op jit(solution)/shard_map/ppermute | solution.py:576
  282.8 34.2 %collective-permute-start.15 = (bf16[512,1280]{1,0:T(8,128)(2,1)}, bf16[512,1280]{1,0:T(8,128)(2,1)S(1)}, u32[]{:S(2)}, u32[]{:S(2)}) collective-permute-start(bf16[512,1280]{1,0:T(8,128)(2,1)} %get-tuple-element.432.refs_1_), channel_id=1, source_target_pairs={{0,1},{1,0},{2,3},{3,2},{4,5},{5,4},{6,7},{7,6},{8,9},{9,8},{10,11... | collective-permute-start | bytes 3932168 | tf_op jit(solution)/shard_map/ppermute | solution.py:576
  283.0 36.7 %collective-permute-start.16 = (bf16[512,1280]{1,0:T(8,128)(2,1)}, bf16[512,1280]{1,0:T(8,128)(2,1)S(1)}, u32[]{:S(2)}, u32[]{:S(2)}) collective-permute-start(bf16[512,1280]{1,0:T(8,128)(2,1)} %get-tuple-element.431), channel_id=1, source_target_pairs={{4,6},{5,7},{2,0},{3,1},{12,14},{13,15},{10,8},{11,9},{20,22},{21,... | collective-permute-start | bytes 3932168 | tf_op jit(solution)/shard_map/ppermute | solution.py:580
  320.2 34.4 %collective-permute-start.17 = (bf16[512,1280]{1,0:T(8,128)(2,1)S(1)}, bf16[512,1280]{1,0:T(8,128)(2,1)S(1)}, u32[]{:S(2)}, u32[]{:S(2)}) collective-permute-start(bf16[512,1280]{1,0:T(8,128)(2,1)S(1)} %select_select_fusion.2.refs_1_), channel_id=1, source_target_pairs={{0,1},{1,0},{2,3},{3,2},{4,5},{5,4},{6,7},{7,6},{8,9},{9,8},{10,11... | collective-permute-start | bytes 3932168 | tf_op jit(solution)/shard_map/ppermute | solution.py:576
  373.6 38.2 %collective-permute-start.20 = (bf16[512,1280]{1,0:T(8,128)(2,1)}, bf16[512,1280]{1,0:T(8,128)(2,1)S(1)}, u32[]{:S(2)}, u32[]{:S(2)}) collective-permute-start(bf16[512,1280]{1,0:T(8,128)(2,1)} %get-tuple-element.304), channel_id=1, source_target_pairs={{0,1},{1,0},{2,3},{3,2},{4,5},{5,4},{6,7},{7,6},{8,9},{9,8},{10,11... | collective-permute-start | bytes 3932168 | tf_op jit(solution)/shard_map/ppermute | solution.py:576
  411.8 52.9 %collective-permute-start.22 = (bf16[896,1280]{1,0:T(8,128)(2,1)}, bf16[896,1280]{1,0:T(8,128)(2,1)}, u32[]{:S(2)}, u32[]{:S(2)}) collective-permute-start(bf16[896,1280]{1,0:T(8,128)(2,1)} %get-tuple-element.319), channel_id=1, source_target_pairs={{0,8},{8,0},{16,24},{24,16},{1,9},{9,1},{17,25},{25,17},{2,10},{10... | collective-permute-start | bytes 6881288 | tf_op jit(solution)/shard_map/ppermute | solution.py:758
  411.8 52.9 %collective-permute-start.19 = (bf16[512,1280]{1,0:T(8,128)(2,1)}, bf16[512,1280]{1,0:T(8,128)(2,1)}, u32[]{:S(2)}, u32[]{:S(2)}) collective-permute-start(bf16[512,1280]{1,0:T(8,128)(2,1)} %get-tuple-element.296), channel_id=1, source_target_pairs={{0,1},{1,0},{2,3},{3,2},{4,5},{5,4},{6,7},{7,6},{8,9},{9,8},{10,11... | collective-permute-start | bytes 3932168 | tf_op jit(solution)/shard_map/ppermute | solution.py:576
  414.4 50.3 %collective-permute-start.21 = (bf16[512,1280]{1,0:T(8,128)(2,1)}, bf16[512,1280]{1,0:T(8,128)(2,1)}, u32[]{:S(2)}, u32[]{:S(2)}) collective-permute-start(bf16[512,1280]{1,0:T(8,128)(2,1)} %add_convert_fusion.12.refs_2_), channel_id=1, source_target_pairs={{0,2},{1,3},{6,4},{7,5},{8,10},{9,11},{14,12},{15,13},{16,18},{17,... | collective-permute-start | bytes 3932168 | tf_op jit(solution)/shard_map/ppermute | solution.py:580
  464.7 59.7 %collective-permute-start.25 = (bf16[1280,1792]{1,0:T(8,128)(2,1)}, bf16[1280,1792]{1,0:T(8,128)(2,1)}, u32[]{:S(2)}, u32[]{:S(2)}) collective-permute-start(bf16[1280,1792]{1,0:T(8,128)(2,1)} %get-tuple-element.328), channel_id=1, source_target_pairs={{0,8},{8,0},{16,24},{24,16},{1,9},{9,1},{17,25},{25,17},{2,10},{10... | collective-permute-start | bytes 13762568 | tf_op jit(solution)/shard_map/ppermute | solution.py:758
  464.8 32.0 %collective-permute-start.18 = (bf16[512,1280]{1,0:T(8,128)(2,1)}, bf16[512,1280]{1,0:T(8,128)(2,1)}, u32[]{:S(2)}, u32[]{:S(2)}) collective-permute-start(bf16[512,1280]{1,0:T(8,128)(2,1)} %get-tuple-element.294), channel_id=1, source_target_pairs={{0,1},{1,0},{2,3},{3,2},{4,5},{5,4},{6,7},{7,6},{8,9},{9,8},{10,11... | collective-permute-start | bytes 3932168 | tf_op jit(solution)/shard_map/ppermute | solution.py:576
  469.3 55.2 %collective-permute-start.26 = (bf16[896,1280]{1,0:T(8,128)(2,1)S(1)}, bf16[896,1280]{1,0:T(8,128)(2,1)}, u32[]{:S(2)}, u32[]{:S(2)}) collective-permute-start(bf16[896,1280]{1,0:T(8,128)(2,1)S(1)} %add_convert_fusion.6), channel_id=1, source_target_pairs={{0,16},{8,24},{16,0},{24,8},{1,17},{9,25},{17,1},{25,9},{2,18},{10... | collective-permute-start | bytes 6881288 | tf_op jit(solution)/shard_map/ppermute | solution.py:765
  472.5 51.9 %collective-permute-start.27 = (bf16[512,1280]{1,0:T(8,128)(2,1)}, bf16[512,1280]{1,0:T(8,128)(2,1)}, u32[]{:S(2)}, u32[]{:S(2)}) collective-permute-start(bf16[512,1280]{1,0:T(8,128)(2,1)} %get-tuple-element.331), channel_id=1, source_target_pairs={{0,1},{1,0},{2,3},{3,2},{4,5},{5,4},{6,7},{7,6},{8,9},{9,8},{10,11... | collective-permute-start | bytes 3932168 | tf_op jit(solution)/shard_map/ppermute | solution.py:576
  478.1 46.3 %collective-permute-start.23 = (bf16[512,1280]{1,0:T(8,128)(2,1)}, bf16[512,1280]{1,0:T(8,128)(2,1)}, u32[]{:S(2)}, u32[]{:S(2)}) collective-permute-start(bf16[512,1280]{1,0:T(8,128)(2,1)} %get-tuple-element.326), channel_id=1, source_target_pairs={{0,2},{1,3},{2,4},{3,5},{8,10},{9,11},{10,12},{11,13},{16,18},{17,... | collective-permute-start | bytes 3932168 | tf_op jit(solution)/shard_map/ppermute | solution.py:580
  496.8 27.6 %collective-permute-start.24 = (bf16[512,1280]{1,0:T(8,128)(2,1)}, bf16[512,1280]{1,0:T(8,128)(2,1)}, u32[]{:S(2)}, u32[]{:S(2)}) collective-permute-start(bf16[512,1280]{1,0:T(8,128)(2,1)} %get-tuple-element.327), channel_id=1, source_target_pairs={{6,4},{7,5},{4,2},{5,3},{14,12},{15,13},{12,10},{13,11},{22,20},{2... | collective-permute-start | bytes 3932168 | tf_op jit(solution)/shard_map/ppermute | solution.py:580
  529.1 57.3 %collective-permute-start.38 = (bf16[640,1792]{1,0:T(8,128)(2,1)}, bf16[640,1792]{1,0:T(8,128)(2,1)}, u32[]{:S(2)}, u32[]{:S(2)}) collective-permute-start(bf16[640,1792]{1,0:T(8,128)(2,1)} %get-tuple-element.421), channel_id=1, source_target_pairs={{0,16},{8,24},{16,0},{24,8},{1,17},{9,25},{17,1},{25,9},{2,18},{10... | collective-permute-start | bytes 6881288 | tf_op jit(solution)/shard_map/ppermute | solution.py:765
  541.0 106.6 %collective-permute-start.34 = (bf16[2,4,2,40,3072]{4,3,1,2,0:T(8,128)(2,1)}, bf16[2,4,2,40,3072]{4,3,1,2,0:T(8,128)(2,1)}, u32[]{:S(2)}, u32[]{:S(2)}) collective-permute-start(bf16[2,4,2,40,3072]{4,3,1,2,0:T(8,128)(2,1)} %fusion.3), channel_id=1, source_target_pairs={{0,8},{8,0},{16,24},{24,16},{1,9},{9,1},{17,25},{25,17},{2,10},{10... | collective-permute-start | bytes 11796488 | tf_op jit(solution)/shard_map/ppermute | solution.py:709
  541.5 31.5 %collective-permute-start.35 = (bf16[512,1280]{1,0:T(8,128)(2,1)}, bf16[512,1280]{1,0:T(8,128)(2,1)}, u32[]{:S(2)}, u32[]{:S(2)}) collective-permute-start(bf16[512,1280]{1,0:T(8,128)(2,1)} %get-tuple-element.360), channel_id=1, source_target_pairs={{0,1},{1,0},{2,3},{3,2},{4,5},{5,4},{6,7},{7,6},{8,9},{9,8},{10,11... | collective-permute-start | bytes 3932168 | tf_op jit(solution)/shard_map/ppermute | solution.py:576
  548.2 33.2 %collective-permute-start.36 = (bf16[512,1280]{1,0:T(8,128)(2,1)}, bf16[512,1280]{1,0:T(8,128)(2,1)S(1)}, u32[]{:S(2)}, u32[]{:S(2)}) collective-permute-start(bf16[512,1280]{1,0:T(8,128)(2,1)} %get-tuple-element.366), channel_id=1, source_target_pairs={{0,2},{1,3},{2,4},{3,5},{4,6},{5,7},{8,10},{9,11},{10,12},{11,13},... | collective-permute-start | bytes 3932168 | tf_op jit(solution)/shard_map/ppermute | solution.py:580
  552.8 33.6 %collective-permute-start.37 = (bf16[512,1280]{1,0:T(8,128)(2,1)}, bf16[512,1280]{1,0:T(8,128)(2,1)S(1)}, u32[]{:S(2)}, u32[]{:S(2)}) collective-permute-start(bf16[512,1280]{1,0:T(8,128)(2,1)} %get-tuple-element.367), channel_id=1, source_target_pairs={{6,4},{7,5},{4,2},{5,3},{2,0},{3,1},{14,12},{15,13},{12,10},{13,11... | collective-permute-start | bytes 3932168 | tf_op jit(solution)/shard_map/ppermute | solution.py:580
  573.0 73.7 %collective-permute-start.30 = (bf16[512,1280]{1,0:T(8,128)(2,1)}, bf16[512,1280]{1,0:T(8,128)(2,1)}, u32[]{:S(2)}, u32[]{:S(2)}) collective-permute-start(bf16[512,1280]{1,0:T(8,128)(2,1)} %get-tuple-element.345), channel_id=1, source_target_pairs={{0,1},{1,0},{2,3},{3,2},{4,5},{5,4},{6,7},{7,6},{8,9},{9,8},{10,11... | collective-permute-start | bytes 3932168 | tf_op jit(solution)/shard_map/ppermute | solution.py:576
  581.4 66.2 %collective-permute-start.33 = (bf16[896,1280]{1,0:T(8,128)(2,1)S(1)}, bf16[896,1280]{1,0:T(8,128)(2,1)}, u32[]{:S(2)}, u32[]{:S(2)}) collective-permute-start(bf16[896,1280]{1,0:T(8,128)(2,1)S(1)} %add_convert_fusion.4.mine_ref), channel_id=1, source_target_pairs={{0,8},{8,0},{16,24},{24,16},{1,9},{9,1},{17,25},{25,17},{2,10},{10... | collective-permute-start | bytes 6881288 | tf_op jit(solution)/shard_map/ppermute | solution.py:770
  586.4 61.2 %collective-permute-start.32 = (bf16[640,1792]{1,0:T(8,128)(2,1)S(1)}, bf16[640,1792]{1,0:T(8,128)(2,1)}, u32[]{:S(2)}, u32[]{:S(2)}) collective-permute-start(bf16[640,1792]{1,0:T(8,128)(2,1)S(1)} %copy-done.12), channel_id=1, source_target_pairs={{0,16},{8,24},{16,0},{24,8},{1,17},{9,25},{17,1},{25,9},{2,18},{10... | collective-permute-start | bytes 6881288 | tf_op jit(solution)/shard_map/ppermute | solution.py:765
  586.4 61.2 %collective-permute-start.31 = (bf16[512,1280]{1,0:T(8,128)(2,1)S(1)}, bf16[512,1280]{1,0:T(8,128)(2,1)}, u32[]{:S(2)}, u32[]{:S(2)}) collective-permute-start(bf16[512,1280]{1,0:T(8,128)(2,1)S(1)} %add_convert_fusion.11.refs_2_), channel_id=1, source_target_pairs={{0,2},{1,3},{6,4},{7,5},{8,10},{9,11},{14,12},{15,13},{16,18},{17,... | collective-permute-start | bytes 3932168 | tf_op jit(solution)/shard_map/ppermute | solution.py:580
  646.7 30.0 %collective-permute-start.29 = (bf16[512,1280]{1,0:T(8,128)(2,1)}, bf16[512,1280]{1,0:T(8,128)(2,1)}, u32[]{:S(2)}, u32[]{:S(2)}) collective-permute-start(bf16[512,1280]{1,0:T(8,128)(2,1)} %get-tuple-element.343), channel_id=1, source_target_pairs={{0,1},{1,0},{2,3},{3,2},{4,5},{5,4},{6,7},{7,6},{8,9},{9,8},{10,11... | collective-permute-start | bytes 3932168 | tf_op jit(solution)/shard_map/ppermute | solution.py:576
  650.5 48.5 %collective-permute-start.51 = (bf16[2,4,2,40,1408]{4,3,1,2,0:T(8,128)(2,1)}, bf16[2,4,2,40,1408]{4,3,1,2,0:T(8,128)(2,1)}, u32[]{:S(2)}, u32[]{:S(2)}) collective-permute-start(bf16[2,4,2,40,1408]{4,3,1,2,0:T(8,128)(2,1)} %copy.80), channel_id=1, source_target_pairs={{0,8},{8,0},{16,24},{24,16},{1,9},{9,1},{17,25},{25,17},{2,10},{10... | collective-permute-start | bytes 5406728 | tf_op jit(solution)/shard_map/ppermute | solution.py:709
  655.4 30.6 %collective-permute-start.39 = (bf16[512,1280]{1,0:T(8,128)(2,1)}, bf16[512,1280]{1,0:T(8,128)(2,1)S(1)}, u32[]{:S(2)}, u32[]{:S(2)}) collective-permute-start(bf16[512,1280]{1,0:T(8,128)(2,1)} %get-tuple-element.384), channel_id=1, source_target_pairs={{0,2},{1,3},{2,4},{3,5},{8,10},{9,11},{10,12},{11,13},{16,18},{17,... | collective-permute-start | bytes 3932168 | tf_op jit(solution)/shard_map/ppermute | solution.py:580
  656.8 30.4 %collective-permute-start.40 = (bf16[512,1280]{1,0:T(8,128)(2,1)}, bf16[512,1280]{1,0:T(8,128)(2,1)S(1)}, u32[]{:S(2)}, u32[]{:S(2)}) collective-permute-start(bf16[512,1280]{1,0:T(8,128)(2,1)} %get-tuple-element.385), channel_id=1, source_target_pairs={{6,4},{7,5},{4,2},{5,3},{14,12},{15,13},{12,10},{13,11},{22,20},{2... | collective-permute-start | bytes 3932168 | tf_op jit(solution)/shard_map/ppermute | solution.py:580
  664.3 45.8 %collective-permute-start.57 = (bf16[1,4,2,40,3072]{4,3,1,2,0:T(8,128)(2,1)}, bf16[1,4,2,40,3072]{4,3,1,2,0:T(8,128)(2,1)}, u32[]{:S(2)}, u32[]{:S(2)}) collective-permute-start(bf16[1,4,2,40,3072]{4,3,1,2,0:T(8,128)(2,1)} %constant_dynamic-slice_fusion), channel_id=1, source_target_pairs={{0,16},{8,24},{16,0},{24,8},{1,17},{9,25},{17,1},{25,9},{2,18},{10... | collective-permute-start | bytes 5898248 | tf_op jit(solution)/shard_map/ppermute | solution.py:722
  676.7 69.3 %collective-permute-start.43 = (bf16[2,4,2,40,3840]{4,3,1,2,0:T(8,128)(2,1)}, bf16[2,4,2,40,3840]{4,3,1,2,0:T(8,128)(2,1)}, u32[]{:S(2)}, u32[]{:S(2)}) collective-permute-start(bf16[2,4,2,40,3840]{4,3,1,2,0:T(8,128)(2,1)} %copy.77), channel_id=1, source_target_pairs={{0,8},{8,0},{16,24},{24,16},{1,9},{9,1},{17,25},{25,17},{2,10},{10... | collective-permute-start | bytes 14745608 | tf_op jit(solution)/shard_map/ppermute | solution.py:709
  686.0 30.8 %collective-permute-start.28 = (bf16[512,1280]{1,0:T(8,128)(2,1)}, bf16[512,1280]{1,0:T(8,128)(2,1)S(1)}, u32[]{:S(2)}, u32[]{:S(2)}) collective-permute-start(bf16[512,1280]{1,0:T(8,128)(2,1)} %get-tuple-element.341), channel_id=1, source_target_pairs={{0,1},{1,0},{2,3},{3,2},{4,5},{5,4},{6,7},{7,6},{8,9},{9,8},{10,11... | collective-permute-start | bytes 3932168 | tf_op jit(solution)/shard_map/ppermute | solution.py:576
  693.6 34.1 %collective-permute-start.41 = (bf16[512,1280]{1,0:T(8,128)(2,1)}, bf16[512,1280]{1,0:T(8,128)(2,1)}, u32[]{:S(2)}, u32[]{:S(2)}) collective-permute-start(bf16[512,1280]{1,0:T(8,128)(2,1)} %get-tuple-element.390), channel_id=1, source_target_pairs={{0,2},{1,3},{2,4},{3,5},{4,6},{5,7},{8,10},{9,11},{10,12},{11,13},... | collective-permute-start | bytes 3932168 | tf_op jit(solution)/shard_map/ppermute | solution.py:580
  699.0 32.5 %collective-permute-start.42 = (bf16[512,1280]{1,0:T(8,128)(2,1)}, bf16[512,1280]{1,0:T(8,128)(2,1)}, u32[]{:S(2)}, u32[]{:S(2)}) collective-permute-start(bf16[512,1280]{1,0:T(8,128)(2,1)} %get-tuple-element.391), channel_id=1, source_target_pairs={{6,4},{7,5},{4,2},{5,3},{2,0},{3,1},{14,12},{15,13},{12,10},{13,11... | collective-permute-start | bytes 3932168 | tf_op jit(solution)/shard_map/ppermute | solution.py:580
  710.1 22.1 %collective-permute-start.52 = (bf16[1,4,2,40,1408]{4,3,1,2,0:T(8,128)(2,1)}, bf16[1,4,2,40,1408]{4,3,1,2,0:T(8,128)(2,1)}, u32[]{:S(2)}, u32[]{:S(2)}) collective-permute-start(bf16[1,4,2,40,1408]{4,3,1,2,0:T(8,128)(2,1)} %constant_dynamic-slice_fusion.3), channel_id=1, source_target_pairs={{0,16},{8,24},{16,0},{24,8},{1,17},{9,25},{17,1},{25,9},{2,18},{10... | collective-permute-start | bytes 2703368 | tf_op jit(solution)/shard_map/ppermute | solution.py:722
  716.8 25.0 %collective-permute-start.58 = (bf16[1,4,40,3072]{3,2,1,0:T(8,128)(2,1)}, bf16[1,4,40,3072]{3,2,1,0:T(8,128)(2,1)}, u32[]{:S(2)}, u32[]{:S(2)}) collective-permute-start(bf16[1,4,40,3072]{3,2,1,0:T(8,128)(2,1)} %dynamic-slice_bitcast_fusion.1), channel_id=1, source_target_pairs={{0,1},{1,0},{2,3},{3,2},{4,5},{5,4},{6,7},{7,6},{8,9},{9,8},{10,11... | collective-permute-start | bytes 2949128 | tf_op jit(solution)/shard_map/ppermute | solution.py:576
  727.7 71.1 %collective-permute-start.62 = (bf16[1280,1792]{1,0:T(8,128)(2,1)}, bf16[1280,1792]{1,0:T(8,128)(2,1)}, u32[]{:S(2)}, u32[]{:S(2)}) collective-permute-start(bf16[1280,1792]{1,0:T(8,128)(2,1)} %pad_maximum_fusion.mine_ref), channel_id=1, source_target_pairs={{0,8},{8,0},{16,24},{24,16},{1,9},{9,1},{17,25},{25,17},{2,10},{10... | collective-permute-start | bytes 13762568 | tf_op jit(solution)/shard_map/ppermute | solution.py:770
  733.9 24.7 %collective-permute-start.53 = (bf16[1,4,40,1408]{3,2,1,0:T(8,128)(2,1)S(1)}, bf16[1,4,40,1408]{3,2,1,0:T(8,128)(2,1)S(1)}, u32[]{:S(2)}, u32[]{:S(2)}) collective-permute-start(bf16[1,4,40,1408]{3,2,1,0:T(8,128)(2,1)S(1)} %dynamic-slice_bitcast_fusion.3), channel_id=1, source_target_pairs={{0,1},{1,0},{2,3},{3,2},{4,5},{5,4},{6,7},{7,6},{8,9},{9,8},{10,11... | collective-permute-start | bytes 1351688 | tf_op jit(solution)/shard_map/ppermute | solution.py:576
  743.4 15.2 %collective-permute-start.59 = (bf16[40,3072]{1,0:T(8,128)(2,1)S(1)}, bf16[40,3072]{1,0:T(8,128)(2,1)S(1)}, u32[]{:S(2)}, u32[]{:S(2)}) collective-permute-start(bf16[40,3072]{1,0:T(8,128)(2,1)S(1)} %get-tuple-element.438), channel_id=1, source_target_pairs={{0,2},{1,3},{2,4},{3,5},{4,6},{5,7},{6,0},{7,1},{8,10},{9,11},{10,... | collective-permute-start | bytes 737288 | tf_op jit(solution)/shard_map/ppermute | solution.py:580
  751.5 25.6 %collective-permute-start.45 = (bf16[1,4,2,40,1920]{4,3,1,2,0:T(8,128)(2,1)S(1)}, bf16[1,4,2,40,1920]{4,3,1,2,0:T(8,128)(2,1)S(1)}, u32[]{:S(2)}, u32[]{:S(2)}) collective-permute-start(bf16[1,4,2,40,1920]{4,3,1,2,0:T(8,128)(2,1)S(1)} %constant_dynamic-slice_fusion.5), channel_id=1, source_target_pairs={{0,16},{8,24},{16,0},{24,8},{1,17},{9,25},{17,1},{25,9},{2,18},{10... | collective-permute-start | bytes 3686408 | tf_op jit(solution)/shard_map/ppermute | solution.py:722
  753.7 25.9 %collective-permute-start.44 = (bf16[2,4,40,1920]{3,2,1,0:T(8,128)(2,1)S(1)}, bf16[2,4,40,1920]{3,2,1,0:T(8,128)(2,1)S(1)}, u32[]{:S(2)}, u32[]{:S(2)}) collective-permute-start(bf16[2,4,40,1920]{3,2,1,0:T(8,128)(2,1)S(1)} %dynamic-slice_bitcast_fusion), channel_id=1, source_target_pairs={{0,1},{1,0},{2,3},{3,2},{4,5},{5,4},{6,7},{7,6},{8,9},{9,8},{10,11... | collective-permute-start | bytes 3686408 | tf_op jit(solution)/shard_map/ppermute | solution.py:576
  758.6 12.2 %collective-permute-start.60 = (bf16[40,3072]{1,0:T(8,128)(2,1)S(1)}, bf16[40,3072]{1,0:T(8,128)(2,1)S(1)}, u32[]{:S(2)}, u32[]{:S(2)}) collective-permute-start(bf16[40,3072]{1,0:T(8,128)(2,1)S(1)} %get-tuple-element.437), channel_id=1, source_target_pairs={{0,4},{1,5},{2,6},{3,7},{4,0},{5,1},{6,2},{7,3},{8,12},{9,13},{10,... | collective-permute-start | bytes 737288 | tf_op jit(solution)/shard_map/ppermute | solution.py:580
  758.6 13.4 %collective-permute-start.61 = (bf16[40,3072]{1,0:T(8,128)(2,1)S(1)}, bf16[40,3072]{1,0:T(8,128)(2,1)S(1)}, u32[]{:S(2)}, u32[]{:S(2)}) collective-permute-start(bf16[40,3072]{1,0:T(8,128)(2,1)S(1)} %get-tuple-element.436), channel_id=1, source_target_pairs={{0,6},{1,7},{2,0},{3,1},{4,2},{5,3},{6,4},{7,5},{8,14},{9,15},{10,... | collective-permute-start | bytes 737288 | tf_op jit(solution)/shard_map/ppermute | solution.py:580
  770.8 11.3 %collective-permute-start.54 = (bf16[40,1408]{1,0:T(8,128)(2,1)S(1)}, bf16[40,1408]{1,0:T(8,128)(2,1)S(1)}, u32[]{:S(2)}, u32[]{:S(2)}) collective-permute-start(bf16[40,1408]{1,0:T(8,128)(2,1)S(1)} %get-tuple-element.441), channel_id=1, source_target_pairs={{0,2},{1,3},{2,4},{3,5},{4,6},{5,7},{6,0},{7,1},{8,10},{9,11},{10,... | collective-permute-start | bytes 337928 | tf_op jit(solution)/shard_map/ppermute | solution.py:580
  772.0 11.7 %collective-permute-start.55 = (bf16[40,1408]{1,0:T(8,128)(2,1)S(1)}, bf16[40,1408]{1,0:T(8,128)(2,1)S(1)}, u32[]{:S(2)}, u32[]{:S(2)}) collective-permute-start(bf16[40,1408]{1,0:T(8,128)(2,1)S(1)} %get-tuple-element.440), channel_id=1, source_target_pairs={{0,4},{1,5},{2,6},{3,7},{4,0},{5,1},{6,2},{7,3},{8,12},{9,13},{10,... | collective-permute-start | bytes 337928 | tf_op jit(solution)/shard_map/ppermute | solution.py:580
  780.0 11.9 %collective-permute-start.47 = (bf16[1,4,40,1920]{3,2,1,0:T(8,128)(2,1)S(1)}, bf16[1,4,40,1920]{3,2,1,0:T(8,128)(2,1)S(1)}, u32[]{:S(2)}, u32[]{:S(2)}) collective-permute-start(bf16[1,4,40,1920]{3,2,1,0:T(8,128)(2,1)S(1)} %dynamic-slice_bitcast_fusion.2), channel_id=1, source_target_pairs={{0,1},{1,0},{2,3},{3,2},{4,5},{5,4},{6,7},{7,6},{8,9},{9,8},{10,11... | collective-permute-start | bytes 1843208 | tf_op jit(solution)/shard_map/ppermute | solution.py:576
  782.0 11.1 %collective-permute-start.46 = (bf16[1,4,40,1920]{3,2,1,0:T(8,128)(2,1)S(1)}, bf16[1,4,40,1920]{3,2,1,0:T(8,128)(2,1)S(1)}, u32[]{:S(2)}, u32[]{:S(2)}) collective-permute-start(bf16[1,4,40,1920]{3,2,1,0:T(8,128)(2,1)S(1)} %constant_dynamic-slice_fusion.4), channel_id=1, source_target_pairs={{0,16},{8,24},{16,0},{24,8},{1,17},{9,25},{17,1},{25,9},{2,18},{10... | collective-permute-start | bytes 1843208 | tf_op jit(solution)/shard_map/ppermute | solution.py:722
  793.6 16.4 %collective-permute-start.48 = (bf16[40,3840]{1,0:T(8,128)(2,1)S(1)}, bf16[40,3840]{1,0:T(8,128)(2,1)S(1)}, u32[]{:S(2)}, u32[]{:S(2)}) collective-permute-start(bf16[40,3840]{1,0:T(8,128)(2,1)S(1)} %get-tuple-element.434), channel_id=1, source_target_pairs={{0,2},{1,3},{2,4},{3,5},{4,6},{5,7},{6,0},{7,1},{8,10},{9,11},{10,... | collective-permute-start | bytes 921608 | tf_op jit(solution)/shard_map/ppermute | solution.py:580
  794.2 19.2 %collective-permute-start.49 = (bf16[40,3840]{1,0:T(8,128)(2,1)S(1)}, bf16[40,3840]{1,0:T(8,128)(2,1)S(1)}, u32[]{:S(2)}, u32[]{:S(2)}) collective-permute-start(bf16[40,3840]{1,0:T(8,128)(2,1)S(1)} %get-tuple-element.435), channel_id=1, source_target_pairs={{0,4},{1,5},{2,6},{3,7},{4,0},{5,1},{6,2},{7,3},{8,12},{9,13},{10,... | collective-permute-start | bytes 921608 | tf_op jit(solution)/shard_map/ppermute | solution.py:580
  796.9 16.5 %collective-permute-start.50 = (bf16[40,3840]{1,0:T(8,128)(2,1)S(1)}, bf16[40,3840]{1,0:T(8,128)(2,1)S(1)}, u32[]{:S(2)}, u32[]{:S(2)}) collective-permute-start(bf16[40,3840]{1,0:T(8,128)(2,1)S(1)} %get-tuple-element.433), channel_id=1, source_target_pairs={{0,6},{1,7},{2,0},{3,1},{4,2},{5,3},{6,4},{7,5},{8,14},{9,15},{10,... | collective-permute-start | bytes 921608 | tf_op jit(solution)/shard_map/ppermute | solution.py:580
  (45 other events, 895.6 us)
Sparse Core Ops, SparseCore 0:
  12.4 135.3 all-gather.2
  319.9 98.0 all-gather.4

commit v4 on v3

--- a/solution.py
+++ b/solution.py
@@ -844,7 +844,7 @@
             [rows_flow] + more, (back, out, kept[0], shares_in)
         )
         through()
-        if shared_full is None and len(arrived) > 5:
+        if shared_full is None and len(arrived) > 3:
             shared_full = lax.all_gather(shares_in, BOTH, axis=0, tiled=True)
     x, hidden, result_grad, gate_up_grad = kept[0]
 
@@ -865,7 +865,7 @@
     )
     in_flow = Flow(dp_sum_steps(*grad_in, core, 2))
     pre, layer_sum, grad_shared_in, grad_shared_out = advance(
-        [back_flow, in_flow, down_flow, out_flow],
+        [back_flow, in_flow, down_flow],
         shared_expert(normed_second, cotangent, residual, shared_full, shared_out_full),
     )
 
@@ -879,7 +879,7 @@
         )
 
     shared_flow = Flow(home_steps(of_core(core[0]), of_core(1 - core[0]), split=False))
-    advance([back_flow, in_flow])
+    advance([back_flow, in_flow, out_flow])
     own, up, down = back_flow.result
 
     gr, grb, datt, prod = middle(pre, own, up, down, residual, cotangent, gains, attn_full)

time: 836 us -> 815 us (0.975)
  starting transfers between devices: 112 us -> 98.4 us
    ppermute x20, waiting for transfers between devices: 172 us -> 127 us  [across(): return lax.ppermute(array, 'expert', [(i, i ^ 1) for i in range(2 * LINE)])]
    ppermute x3, waiting for transfers between devices: 0.01 us -> 22.5 us  [dp_sum_steps(): lax.ppermute(piece, 'dp', [(i, i ^ step) for i in range(count)])]
    ppermute x29, waiting for transfers between devices: 77.6 us -> 96.1 us  [along(): lax.ppermute(array, 'expert', [(2 * a + side, 2 * b + side) for a, b in h...]
    ppermute x29, starting transfers between devices: 75.5 us -> 62.8 us  [along(): lax.ppermute(array, 'expert', [(2 * a + side, 2 * b + side) for a, b in h...]
  transfers between devices with their start and end apart: 65 -> 65, of which waited for: 28 -> 30; matrix products, arithmetic and copies ran while one was open for 11% -> 12% of each run, Pallas kernels for 38% -> 39%
where the time goes in v4:
time: 815 us; the launch traced here: 802 us
  Pallas kernels  311 us (38%)
  waiting for transfers between devices  263 us (32%)
  starting transfers between devices  98.4 us (12%)
  other arithmetic  67.7 us (8%)
  local copies, waits for them, and re-layouts  45.8 us (6%)
  between operations  16.1 us (2%)
    pallas_call x5, Pallas kernels, expert_rows(): pl.pallas_call(functools.partial(expert_body, count=count, capacity=capac...  134 us
    ppermute x20, waiting for transfers between devices, across(): return lax.ppermute(array, 'expert', [(i, i ^ 1) for i in range(2 * LINE)])  127 us
    ppermute x29, waiting for transfers between devices, along(): lax.ppermute(array, 'expert', [(2 * a + side, 2 * b + side) for a, b in h...  96.1 us
    ppermute x29, starting transfers between devices, along(): lax.ppermute(array, 'expert', [(2 * a + side, 2 * b + side) for a, b in h...  62.8 us
    pallas_call x2, Pallas kernels, expert_grads(): pl.pallas_call(expert_grads_body, grid_spec=pltpu.PrefetchScalarGridSpec(...  45.3 us
    convert_element_type x17, other arithmetic, add(): return (left.astype(F32) + right.astype(F32)).astype(BF)  40.1 us
    pallas_call x1, Pallas kernels, attend_back(): pl.pallas_call(functools.partial(attend_back_body, chips=chips), grid=(st...  39 us
    ppermute x20, starting transfers between devices, across(): return lax.ppermute(array, 'expert', [(i, i ^ 1) for i in range(2 * LINE)])  25 us
  transfers between devices with their start and end apart: 65, of which 30 were waited for; matrix products, arithmetic and copies ran while one was open for 12% of the time, Pallas kernels for 39%

profile of v4, /device:TPU:0, one launch (start us, length us, event | category | flops | bytes accessed | tf_op | source)
XLA Modules:
  0.0 801.7 jit_solution(1987605433823633668)
XLA Ops:
  14.3 3.0 collective-permute-start.3
  18.6 4.6 collective-permute-start.5
  23.2 27.0 %collective-permute-done.3.refs_2_.refs_4_ = bf16[528,1280]{1,0:T(8,128)(2,1)} collective-permute-done((bf16[528,1280]{1,0:T(8,128)(2,1)}, bf16[528,1280]{1,0:T(8,128)(2,1)}, u32[]{:S(2)}, u32[]{:S(2)}) %collective-permute-start.3) | collective-permute-done | bytes 1351712 | tf_op jit(solution)/shard_map/ppermute | solution.py:576
  50.3 25.1 %collective-permute-done.4 = bf16[528,1280]{1,0:T(8,128)(2,1)S(1)} collective-permute-done((bf16[528,1280]{1,0:T(8,128)(2,1)}, bf16[528,1280]{1,0:T(8,128)(2,1)S(1)}, u32[]{:S(2)}, u32[]{:S(2)}) %collective-permute-start.4) | collective-permute-done | bytes 1351712 | tf_op jit(solution)/shard_map/ppermute | solution.py:580
  79.7 44.1 %collective-permute-done.6.refs_2_.refs_4_ = bf16[528,1280]{1,0:T(8,128)(2,1)} collective-permute-done((bf16[528,1280]{1,0:T(8,128)(2,1)}, bf16[528,1280]{1,0:T(8,128)(2,1)}, u32[]{:S(2)}, u32[]{:S(2)}) %collective-permute-start.6) | collective-permute-done | bytes 1351712 | tf_op jit(solution)/shard_map/ppermute | solution.py:576
  123.8 7.2 collective-permute-done.7
  131.0 3.6 broadcast_select_fusion
  135.9 3.5 collective-permute-start.9
  140.6 7.2 all-gather.3.cloned.1.call-done.wq_ref.wk_ref.wv_ref.wo_ref.gains_in_ref
  147.8 24.1 %attend.1 = (bf16[512,1280]{1,0:T(8,128)(2,1)S(1)}, bf16[512,1280]{1,0:T(8,128)(2,1)S(1)}, bf16[512,1280]{1,0:T(8,128)(2,1)S(1)}, bf16[512,1280]{1,0:T(8,128)(2,...) custom-call(s32[1]{0:T(128)} %copy.117.length_ref, ...), custom_call_target="tpu_custom_call" | custom-call | flops 10000000000 | bytes 25000000 | tf_op jit(solution)/shard_map/attend/pallas_call | solution.py:135
  172.0 7.9 collective-permute-done.10
  182.3 3.0 collective-permute-start.11
  186.7 7.6 collective-permute-start.2
  195.0 17.7 %expert_rows.5 = (bf16[512,1280]{1,0:T(8,128)(2,1)}, bf16[512,1280]{1,0:T(8,128)(2,1)}, bf16[2,8,240,1280]{3,2,1,0:T(8,128)(2,1)}, bf16[2,8,240,896]{3,2,1,0:T(8...) custom-call(s32[1]{0:T(128)} %bitcast.6.mine_ref, ...), custom_call_target="tpu_custom_call" | custom-call | flops 9299999744 | bytes 22000000 | tf_op jit(solution)/shard_map/expert_rows/pallas_call | solution.py:441
  212.7 27.3 %collective-permute-done.refs_0_ = bf16[512,1280]{1,0:T(8,128)(2,1)} collective-permute-done((bf16[512,1280]{1,0:T(8,128)(2,1)}, bf16[512,1280]{1,0:T(8,128)(2,1)}, u32[]{:S(2)}, u32[]{:S(2)}) %collective-permute-start) | collective-permute-done | bytes 1310752 | tf_op jit(solution)/shard_map/ppermute | solution.py:576
  246.3 32.3 %expert_rows.6 = (bf16[512,1280]{1,0:T(8,128)(2,1)}, bf16[512,1280]{1,0:T(8,128)(2,1)}, bf16[512,1280]{1,0:T(8,128)(2,1)}, bf16[512,1280]{1,0:T(8,128)(2,1)}, bf...) custom-call(s32[1]{0:T(128)} %bitcast.6.mine_ref, ...), custom_call_target="tpu_custom_call", output_to_operand_aliasing={{4}: (9, {}), {5}: (10, {}), {6}: (11, {}), {7}: (12, {})} | custom-call | flops 18599999488 | bytes 30000000 | tf_op jit(solution)/shard_map/expert_rows/pallas_call | solution.py:441
  279.8 3.0 broadcast_select_fusion.2
  284.6 32.4 %expert_rows.7 = (bf16[512,1280]{1,0:T(8,128)(2,1)}, bf16[512,1280]{1,0:T(8,128)(2,1)}, bf16[512,1280]{1,0:T(8,128)(2,1)}, bf16[512,1280]{1,0:T(8,128)(2,1)}, bf...) custom-call(s32[1]{0:T(128)} %bitcast.6.mine_ref, ...), custom_call_target="tpu_custom_call", output_to_operand_aliasing={{4}: (9, {}), {5}: (10, {}), {6}: (11, {}), {7}: (12, {})} | custom-call | flops 18599999488 | bytes 30000000 | tf_op jit(solution)/shard_map/expert_rows/pallas_call | solution.py:441
  317.0 18.6 %collective-permute-done.16 = bf16[512,1280]{1,0:T(8,128)(2,1)S(1)} collective-permute-done((bf16[512,1280]{1,0:T(8,128)(2,1)S(1)}, bf16[512,1280]{1,0:T(8,128)(2,1)S(1)}, u32[]{:S(2)}, u32[]{:S(2)}) %collective-permute-start.16) | collective-permute-done | bytes 1310752 | tf_op jit(solution)/shard_map/ppermute | solution.py:580
  337.4 33.8 %expert_rows.8 = (bf16[512,1280]{1,0:T(8,128)(2,1)}, bf16[512,1280]{1,0:T(8,128)(2,1)}, bf16[512,1280]{1,0:T(8,128)(2,1)}, bf16[512,1280]{1,0:T(8,128)(2,1)}, bf...) custom-call(s32[1]{0:T(128)} %bitcast.6.mine_ref, ...), custom_call_target="tpu_custom_call", output_to_operand_aliasing={{4}: (9, {}), {5}: (10, {}), {6}: (11, {}), {7}: (12, {})} | custom-call | flops 18599999488 | bytes 30000000 | tf_op jit(solution)/shard_map/expert_rows/pallas_call | solution.py:441
  372.3 17.8 %expert_rows.9 = (bf16[512,1280]{1,0:T(8,128)(2,1)}, bf16[512,1280]{1,0:T(8,128)(2,1)}, bf16[2,8,240,1280]{3,2,1,0:T(8,128)(2,1)}, bf16[2,8,240,896]{3,2,1,0:T(8...) custom-call(s32[1]{0:T(128)} %bitcast.6.mine_ref, ...), custom_call_target="tpu_custom_call", output_to_operand_aliasing={{2}: (6, {}), {3}: (7, {}), {4}: (8, {}), {5}: (9, {})} | custom-call | flops 9299999744 | bytes 22000000 | tf_op jit(solution)/shard_map/expert_rows/pallas_call | solution.py:441
  391.2 16.2 %expert_grads.2 = (bf16[896,1280]{1,0:T(8,128)(2,1)}, bf16[896,1280]{1,0:T(8,128)(2,1)}) custom-call(s32[1]{0:T(128)} %select_n.273.core_ref, bf16[2,8,240,896]{3,2,1,0:T(8,128)(2,1)} %get-tuple-element.303.left_ref, bf16[2,8,240,1280]{3,2,1,0:T(8,128)(2,1)} %get-tuple-element.304.right_ref), custom_call_target="tpu_custom_call" | custom-call | flops 8808038400 | bytes 40000000 | tf_op jit(solution)/shard_map/expert_grads/pallas_call | solution.py:485
  410.4 4.9 collective-permute-start.21
  415.3 29.1 %expert_grads.3 = (bf16[1280,1792]{1,0:T(8,128)(2,1)}, bf16[1280,1792]{1,0:T(8,128)(2,1)}) custom-call(s32[1]{0:T(128)} %select_n.273.core_ref, bf16[2,8,240,1280]{3,2,1,0:T(8,128)(2,1)} %get-tuple-element.318.left_ref, bf16[2,8,240,1792]{3,2,1,0:T(8,128)(2,1)} %get-tuple-element.319.right_ref), custom_call_target="tpu_custom_call" | custom-call | flops 17616076800 | bytes 40000000 | tf_op jit(solution)/shard_map/expert_grads/pallas_call | solution.py:485
  448.2 4.1 reshape.249.wout_ref
  452.4 2.9 add_convert_fusion.6
  455.3 2.5 collective-permute-start.26
  459.0 5.0 outer_sums.2
  468.6 18.3 %shared_expert.1 = (f32[512,1280]{1,0:T(8,128)}, f32[512,1280]{1,0:T(8,128)}, bf16[1280,1792]{1,0:T(8,128)(2,1)}, bf16[896,1280]{1,0:T(8,128)(2,1)}) custom-call(bf16[512,1280]{1,0:T(8,128)(2,1)} %get-tuple-element.213.refs_0_.normed_ref, bf16[512,1280]{1,0:T(8,128)(2,1)} %cot_ref.3, f32[512,1280]{1,0:T(8,128)} %get-tuple-element.329.residual_ref, ...), custom_call_target="tpu_custom_call" | custom-call | flops 14000000000 | bytes 25000000 | tf_op jit(solution)/shard_map/shared_expert/pallas_call | solution.py:554
  490.2 3.8 collective-permute-done.23.refs_3_
  494.0 14.4 %collective-permute-done.26 = bf16[896,1280]{1,0:T(8,128)(2,1)} collective-permute-done((bf16[896,1280]{1,0:T(8,128)(2,1)S(1)}, bf16[896,1280]{1,0:T(8,128)(2,1)}, u32[]{:S(2)}, u32[]{:S(2)}) %collective-permute-start.26) | collective-permute-done | bytes 2293792 | tf_op jit(solution)/shard_map/ppermute | solution.py:765
  508.4 4.5 add_convert_fusion.4
  517.6 5.2 inner_sums.2
  526.7 2.6 reshape.251
  530.8 2.6 constant_dynamic-slice_fusion.2
  541.3 2.5 add_convert_fusion.3.mine_ref
  543.9 3.6 collective-permute-done.34
  548.7 3.3 collective-permute-done.31.one_ref
  552.1 5.2 collective-permute-done.32.two_ref
  557.7 8.1 %collective-permute-done.33 = bf16[640,1792]{1,0:T(8,128)(2,1)} collective-permute-done((bf16[640,1792]{1,0:T(8,128)(2,1)}, bf16[640,1792]{1,0:T(8,128)(2,1)}, u32[]{:S(2)}, u32[]{:S(2)}) %collective-permute-start.33) | collective-permute-done | bytes 2293792 | tf_op jit(solution)/shard_map/ppermute | solution.py:765
  571.8 11.5 %middle.1 = (f32[512,1280]{1,0:T(8,128)}, bf16[512,1280]{1,0:T(8,128)(2,1)S(1)}, bf16[512,1280]{1,0:T(8,128)(2,1)S(1)}, bf16[512,1280]{1,0:T(8,128)(2,1)S(1)}) custom-call(f32[512,1280]{1,0:T(8,128)} %get-tuple-element.364.pre_ref, bf16[512,1280]{1,0:T(8,128)(2,1)S(1)} %add_convert_fusion.10.own_ref, bf16[512,1280]{1,0:T(8,128)(2,1)} %collective-permute-done.31.one_ref, ...), custom_call_target="tpu_custom_call" | custom-call | flops 4000000000 | bytes 25000000 | tf_op jit(solution)/shard_map/middle/pallas_call | solution.py:197
  586.6 39.0 %attend_back.1 = (bf16[640,3840]{1,0:T(8,128)(2,1)}, bf16[640,3840]{1,0:T(8,128)(2,1)}, f32[512,1280]{1,0:T(8,128)}, bf16[640,1408]{1,0:T(8,128)(2,1)}, bf16[640,1408]{1,0:T(8,128)(2,1)}) custom-call(s32[2]{0:T(128)} %pad_add_fusion.length_ref, bf16[512,1280]{1,0:T(8,128)(2,1)} %get-tuple-element.359.normed_ref, ...), custom_call_target="tpu_custom_call" | custom-call | flops 14000000000 | bytes 40000000 | tf_op jit(solution)/shard_map/attend_back/pallas_call | solution.py:307
  626.9 2.9 copy.80
  629.9 5.0 outer_sums.3
  637.0 4.1 add_convert_fusion
  645.5 4.3 add_convert_fusion.2
  649.8 2.5 copy.77
  654.7 3.7 add_convert_fusion.1
  658.4 7.0 collective-permute-done.39.refs_3_
  667.5 5.3 inner_sums.3
  672.8 5.4 collective-permute-start.41
  682.7 6.6 collective-permute-done.57
  697.0 2.4 pad_maximum_fusion.mine_ref
  699.5 7.4 both_experts.3
  706.8 4.0 collective-permute-done.42
  713.8 7.4 collective-permute-done.58
  722.8 2.5 collective-permute-start.59
  725.4 5.0 fusion
  733.7 3.6 add_convert_fusion.8
  739.9 9.6 %collective-permute-done.60 = bf16[40,3072]{1,0:T(8,128)(2,1)S(1)} collective-permute-done((bf16[40,3072]{1,0:T(8,128)(2,1)S(1)}, bf16[40,3072]{1,0:T(8,128)(2,1)S(1)}, u32[]{:S(2)}, u32[]{:S(2)}) %collective-permute-start.60) | collective-permute-done | bytes 245792 | tf_op jit(solution)/shard_map/ppermute | solution.py:580
  750.7 3.4 collective-permute-start.55
  762.7 8.3 %collective-permute-done.47 = bf16[1,4,40,1920]{3,2,1,0:T(8,128)(2,1)S(1)} collective-permute-done((bf16[1,4,40,1920]{3,2,1,0:T(8,128)(2,1)S(1)}, bf16[1,4,40,1920]{3,2,1,0:T(8,128)(2,1)S(1)}, u32[]{:S(2)}, u32[]{:S(2)}) %collective-permute-start.47) | collective-permute-done | bytes 614432 | tf_op jit(solution)/shard_map/ppermute | solution.py:576
  777.6 11.1 %both_experts.2 = f32[2,1280,1792]{2,1,0:T(8,128)} custom-call(s32[1]{0:T(128)} %select_n.273.core_ref, bf16[1280,1792]{1,0:T(8,128)(2,1)} %pad_maximum_fusion.mine_ref, bf16[1280,1792]{1,0:T(8,128)(2,1)} %collective-permute-done.62.other_ref), custom_call_target="tpu_custom_call" | custom-call | flops 2293760 | bytes 27525120 | tf_op jit(solution)/shard_map/both_experts/pallas_call | solution.py:517
  788.7 3.9 collective-permute-done.49
  (255 shorter events, 129.7 us)
Async XLA Ops:
  7.2 140.6 %all-gather.3.cloned.1.call-start = ((), (), s32[]{:S(2)}) async-start(), calls=%async_computation | async-start | bytes 13854720 | tf_op jit(solution)/shard_map/all_gather | solution.py:799
  12.3 432.1 %all-gather.5.cloned.1.call-start = ((), (), s32[]{:S(2)}) async-start(), calls=%async_computation.1 | async-start | bytes 8110080 | tf_op jit(solution)/shard_map/all_gather | solution.py:848
  14.3 35.9 %collective-permute-start.3 = (bf16[528,1280]{1,0:T(8,128)(2,1)}, bf16[528,1280]{1,0:T(8,128)(2,1)}, u32[]{:S(2)}, u32[]{:S(2)}) collective-permute-start(bf16[528,1280]{1,0:T(8,128)(2,1)} %pad_maximum_fusion.1.refs_1_.refs_2_), channel_id=1, source_target_pairs={{0,1},{1,0},{2,3},{3,2},{4,5},{5,4},{6,7},{7,6},{8,9},{9,8},{10,11... | collective-permute-start | bytes 4055048 | tf_op jit(solution)/shard_map/ppermute | solution.py:576
  17.3 58.0 %collective-permute-start.4 = (bf16[528,1280]{1,0:T(8,128)(2,1)}, bf16[528,1280]{1,0:T(8,128)(2,1)S(1)}, u32[]{:S(2)}, u32[]{:S(2)}) collective-permute-start(bf16[528,1280]{1,0:T(8,128)(2,1)} %pad_maximum_fusion.1.refs_1_.refs_2_), channel_id=1, source_target_pairs={{2,0},{3,1},{4,2},{5,3},{6,4},{7,5},{10,8},{11,9},{12,10},{13,11},... | collective-permute-start | bytes 4055048 | tf_op jit(solution)/shard_map/ppermute | solution.py:580
  18.6 56.8 %collective-permute-start.5 = (bf16[528,1280]{1,0:T(8,128)(2,1)}, bf16[528,1280]{1,0:T(8,128)(2,1)S(1)}, u32[]{:S(2)}, u32[]{:S(2)}) collective-permute-start(bf16[528,1280]{1,0:T(8,128)(2,1)} %pad_maximum_fusion.1.refs_1_.refs_2_), channel_id=1, source_target_pairs={{0,2},{1,3},{2,4},{3,5},{4,6},{5,7},{8,10},{9,11},{10,12},{11,13},... | collective-permute-start | bytes 4055048 | tf_op jit(solution)/shard_map/ppermute | solution.py:580
  76.6 47.2 %collective-permute-start.6 = (bf16[528,1280]{1,0:T(8,128)(2,1)}, bf16[528,1280]{1,0:T(8,128)(2,1)}, u32[]{:S(2)}, u32[]{:S(2)}) collective-permute-start(bf16[528,1280]{1,0:T(8,128)(2,1)} %broadcast_select_fusion.1.refs_3_.refs_5_), channel_id=1, source_target_pairs={{0,1},{1,0},{2,3},{3,2},{4,5},{5,4},{6,7},{7,6},{8,9},{9,8},{10,11... | collective-permute-start | bytes 4055048 | tf_op jit(solution)/shard_map/ppermute | solution.py:576
  76.6 54.4 %collective-permute-start.7 = (bf16[528,1280]{1,0:T(8,128)(2,1)S(1)}, bf16[528,1280]{1,0:T(8,128)(2,1)}, u32[]{:S(2)}, u32[]{:S(2)}) collective-permute-start(bf16[528,1280]{1,0:T(8,128)(2,1)S(1)} %collective-permute-done.4), channel_id=1, source_target_pairs={{2,0},{3,1},{4,2},{5,3},{10,8},{11,9},{12,10},{13,11},{18,16},{19,... | collective-permute-start | bytes 4055048 | tf_op jit(solution)/shard_map/ppermute | solution.py:580
  77.9 53.1 %collective-permute-start.8 = (bf16[528,1280]{1,0:T(8,128)(2,1)S(1)}, bf16[528,1280]{1,0:T(8,128)(2,1)}, u32[]{:S(2)}, u32[]{:S(2)}) collective-permute-start(bf16[528,1280]{1,0:T(8,128)(2,1)S(1)} %collective-permute-done.5), channel_id=1, source_target_pairs={{2,4},{3,5},{4,6},{5,7},{10,12},{11,13},{12,14},{13,15},{18,20},{1... | collective-permute-start | bytes 4055048 | tf_op jit(solution)/shard_map/ppermute | solution.py:580
  134.6 45.3 %collective-permute-start.10 = (bf16[528,1280]{1,0:T(8,128)(2,1)}, bf16[528,1280]{1,0:T(8,128)(2,1)S(1)}, u32[]{:S(2)}, u32[]{:S(2)}) collective-permute-start(bf16[528,1280]{1,0:T(8,128)(2,1)} %get-tuple-element.425), channel_id=1, source_target_pairs={{4,6},{5,7},{2,0},{3,1},{12,14},{13,15},{10,8},{11,9},{20,22},{21,... | collective-permute-start | bytes 4055048 | tf_op jit(solution)/shard_map/ppermute | solution.py:580
  135.9 44.0 %collective-permute-start.9 = (bf16[528,1280]{1,0:T(8,128)(2,1)}, bf16[528,1280]{1,0:T(8,128)(2,1)S(1)}, u32[]{:S(2)}, u32[]{:S(2)}) collective-permute-start(bf16[528,1280]{1,0:T(8,128)(2,1)} %get-tuple-element.426.refs_3_.refs_5_), channel_id=1, source_target_pairs={{0,1},{1,0},{2,3},{3,2},{4,5},{5,4},{6,7},{7,6},{8,9},{9,8},{10,11... | collective-permute-start | bytes 4055048 | tf_op jit(solution)/shard_map/ppermute | solution.py:576
  182.3 57.7 %collective-permute-start.11 = (bf16[528,1280]{1,0:T(8,128)(2,1)}, bf16[528,1280]{1,0:T(8,128)(2,1)S(1)}, u32[]{:S(2)}, u32[]{:S(2)}) collective-permute-start(bf16[528,1280]{1,0:T(8,128)(2,1)} %select_select_fusion.refs_3_.refs_5_), channel_id=1, source_target_pairs={{0,1},{1,0},{2,3},{3,2},{4,5},{5,4},{6,7},{7,6},{8,9},{9,8},{10,11... | collective-permute-start | bytes 4055048 | tf_op jit(solution)/shard_map/ppermute | solution.py:576
  185.3 54.7 %collective-permute-start = (bf16[512,1280]{1,0:T(8,128)(2,1)}, bf16[512,1280]{1,0:T(8,128)(2,1)}, u32[]{:S(2)}, u32[]{:S(2)}) collective-permute-start(bf16[512,1280]{1,0:T(8,128)(2,1)} %get-tuple-element.213.refs_0_.normed_ref), channel_id=1, source_target_pairs={{0,1},{1,0},{2,3},{3,2},{4,5},{5,4},{6,7},{7,6},{8,9},{9,8},{10,11... | collective-permute-start | bytes 3932168 | tf_op jit(solution)/shard_map/ppermute | solution.py:576
  185.4 54.7 %collective-permute-start.1 = (bf16[512,1280]{1,0:T(8,128)(2,1)}, bf16[512,1280]{1,0:T(8,128)(2,1)S(1)}, u32[]{:S(2)}, u32[]{:S(2)}) collective-permute-start(bf16[512,1280]{1,0:T(8,128)(2,1)} %get-tuple-element.213.refs_0_.normed_ref), channel_id=1, source_target_pairs={{2,0},{3,1},{4,2},{5,3},{6,4},{7,5},{10,8},{11,9},{12,10},{13,11},... | collective-permute-start | bytes 3932168 | tf_op jit(solution)/shard_map/ppermute | solution.py:580
  186.7 53.4 %collective-permute-start.2 = (bf16[512,1280]{1,0:T(8,128)(2,1)}, bf16[512,1280]{1,0:T(8,128)(2,1)}, u32[]{:S(2)}, u32[]{:S(2)}) collective-permute-start(bf16[512,1280]{1,0:T(8,128)(2,1)} %get-tuple-element.213.refs_0_.normed_ref), channel_id=1, source_target_pairs={{0,2},{1,3},{2,4},{3,5},{4,6},{5,7},{8,10},{9,11},{10,12},{11,13},... | collective-permute-start | bytes 3932168 | tf_op jit(solution)/shard_map/ppermute | solution.py:580
  240.1 38.6 %collective-permute-start.13 = (bf16[512,1280]{1,0:T(8,128)(2,1)S(1)}, bf16[512,1280]{1,0:T(8,128)(2,1)}, u32[]{:S(2)}, u32[]{:S(2)}) collective-permute-start(bf16[512,1280]{1,0:T(8,128)(2,1)S(1)} %collective-permute-done.1), channel_id=1, source_target_pairs={{2,0},{3,1},{4,2},{5,3},{10,8},{11,9},{12,10},{13,11},{18,16},{19,... | collective-permute-start | bytes 3932168 | tf_op jit(solution)/shard_map/ppermute | solution.py:580
  242.6 37.2 %collective-permute-start.14 = (bf16[512,1280]{1,0:T(8,128)(2,1)}, bf16[512,1280]{1,0:T(8,128)(2,1)}, u32[]{:S(2)}, u32[]{:S(2)}) collective-permute-start(bf16[512,1280]{1,0:T(8,128)(2,1)} %collective-permute-done.2), channel_id=1, source_target_pairs={{2,4},{3,5},{4,6},{5,7},{10,12},{11,13},{12,14},{13,15},{18,20},{1... | collective-permute-start | bytes 3932168 | tf_op jit(solution)/shard_map/ppermute | solution.py:580
  244.5 34.2 %collective-permute-start.12 = (bf16[512,1280]{1,0:T(8,128)(2,1)}, bf16[512,1280]{1,0:T(8,128)(2,1)S(1)}, u32[]{:S(2)}, u32[]{:S(2)}) collective-permute-start(bf16[512,1280]{1,0:T(8,128)(2,1)} %broadcast_select_fusion.3.refs_1_), channel_id=1, source_target_pairs={{0,1},{1,0},{2,3},{3,2},{4,5},{5,4},{6,7},{7,6},{8,9},{9,8},{10,11... | collective-permute-start | bytes 3932168 | tf_op jit(solution)/shard_map/ppermute | solution.py:576
  282.8 34.2 %collective-permute-start.15 = (bf16[512,1280]{1,0:T(8,128)(2,1)}, bf16[512,1280]{1,0:T(8,128)(2,1)S(1)}, u32[]{:S(2)}, u32[]{:S(2)}) collective-permute-start(bf16[512,1280]{1,0:T(8,128)(2,1)} %get-tuple-element.430.refs_1_), channel_id=1, source_target_pairs={{0,1},{1,0},{2,3},{3,2},{4,5},{5,4},{6,7},{7,6},{8,9},{9,8},{10,11... | collective-permute-start | bytes 3932168 | tf_op jit(solution)/shard_map/ppermute | solution.py:576
  283.1 52.6 %collective-permute-start.16 = (bf16[512,1280]{1,0:T(8,128)(2,1)S(1)}, bf16[512,1280]{1,0:T(8,128)(2,1)S(1)}, u32[]{:S(2)}, u32[]{:S(2)}) collective-permute-start(bf16[512,1280]{1,0:T(8,128)(2,1)S(1)} %get-tuple-element.429), channel_id=1, source_target_pairs={{4,6},{5,7},{2,0},{3,1},{12,14},{13,15},{10,8},{11,9},{20,22},{21,... | collective-permute-start | bytes 3932168 | tf_op jit(solution)/shard_map/ppermute | solution.py:580
  336.0 35.2 %collective-permute-start.17 = (bf16[512,1280]{1,0:T(8,128)(2,1)S(1)}, bf16[512,1280]{1,0:T(8,128)(2,1)S(1)}, u32[]{:S(2)}, u32[]{:S(2)}) collective-permute-start(bf16[512,1280]{1,0:T(8,128)(2,1)S(1)} %select_select_fusion.2.refs_1_), channel_id=1, source_target_pairs={{0,1},{1,0},{2,3},{3,2},{4,5},{5,4},{6,7},{7,6},{8,9},{9,8},{10,11... | collective-permute-start | bytes 3932168 | tf_op jit(solution)/shard_map/ppermute | solution.py:576
  390.1 17.9 %collective-permute-start.20 = (bf16[512,1280]{1,0:T(8,128)(2,1)}, bf16[512,1280]{1,0:T(8,128)(2,1)S(1)}, u32[]{:S(2)}, u32[]{:S(2)}) collective-permute-start(bf16[512,1280]{1,0:T(8,128)(2,1)} %get-tuple-element.302), channel_id=1, source_target_pairs={{0,1},{1,0},{2,3},{3,2},{4,5},{5,4},{6,7},{7,6},{8,9},{9,8},{10,11... | collective-permute-start | bytes 3932168 | tf_op jit(solution)/shard_map/ppermute | solution.py:576
  408.0 44.3 %collective-permute-start.22 = (bf16[896,1280]{1,0:T(8,128)(2,1)}, bf16[896,1280]{1,0:T(8,128)(2,1)}, u32[]{:S(2)}, u32[]{:S(2)}) collective-permute-start(bf16[896,1280]{1,0:T(8,128)(2,1)} %get-tuple-element.317), channel_id=1, source_target_pairs={{0,8},{8,0},{16,24},{24,16},{1,9},{9,1},{17,25},{25,17},{2,10},{10... | collective-permute-start | bytes 6881288 | tf_op jit(solution)/shard_map/ppermute | solution.py:758
  408.0 44.3 %collective-permute-start.19 = (bf16[512,1280]{1,0:T(8,128)(2,1)}, bf16[512,1280]{1,0:T(8,128)(2,1)}, u32[]{:S(2)}, u32[]{:S(2)}) collective-permute-start(bf16[512,1280]{1,0:T(8,128)(2,1)} %get-tuple-element.294), channel_id=1, source_target_pairs={{0,1},{1,0},{2,3},{3,2},{4,5},{5,4},{6,7},{7,6},{8,9},{9,8},{10,11... | collective-permute-start | bytes 3932168 | tf_op jit(solution)/shard_map/ppermute | solution.py:576
  410.4 41.9 %collective-permute-start.21 = (bf16[512,1280]{1,0:T(8,128)(2,1)}, bf16[512,1280]{1,0:T(8,128)(2,1)}, u32[]{:S(2)}, u32[]{:S(2)}) collective-permute-start(bf16[512,1280]{1,0:T(8,128)(2,1)} %add_convert_fusion.12.refs_2_), channel_id=1, source_target_pairs={{0,2},{1,3},{6,4},{7,5},{8,10},{9,11},{14,12},{15,13},{16,18},{17,... | collective-permute-start | bytes 3932168 | tf_op jit(solution)/shard_map/ppermute | solution.py:580
  452.3 56.1 %collective-permute-start.25 = (bf16[1280,1792]{1,0:T(8,128)(2,1)}, bf16[1280,1792]{1,0:T(8,128)(2,1)}, u32[]{:S(2)}, u32[]{:S(2)}) collective-permute-start(bf16[1280,1792]{1,0:T(8,128)(2,1)} %get-tuple-element.326), channel_id=1, source_target_pairs={{0,8},{8,0},{16,24},{24,16},{1,9},{9,1},{17,25},{25,17},{2,10},{10... | collective-permute-start | bytes 13762568 | tf_op jit(solution)/shard_map/ppermute | solution.py:758
  455.3 53.1 %collective-permute-start.26 = (bf16[896,1280]{1,0:T(8,128)(2,1)S(1)}, bf16[896,1280]{1,0:T(8,128)(2,1)}, u32[]{:S(2)}, u32[]{:S(2)}) collective-permute-start(bf16[896,1280]{1,0:T(8,128)(2,1)S(1)} %add_convert_fusion.6), channel_id=1, source_target_pairs={{0,16},{8,24},{16,0},{24,8},{1,17},{9,25},{17,1},{25,9},{2,18},{10... | collective-permute-start | bytes 6881288 | tf_op jit(solution)/shard_map/ppermute | solution.py:765
  457.8 31.2 %collective-permute-start.18 = (bf16[512,1280]{1,0:T(8,128)(2,1)}, bf16[512,1280]{1,0:T(8,128)(2,1)}, u32[]{:S(2)}, u32[]{:S(2)}) collective-permute-start(bf16[512,1280]{1,0:T(8,128)(2,1)} %get-tuple-element.292), channel_id=1, source_target_pairs={{0,1},{1,0},{2,3},{3,2},{4,5},{5,4},{6,7},{7,6},{8,9},{9,8},{10,11... | collective-permute-start | bytes 3932168 | tf_op jit(solution)/shard_map/ppermute | solution.py:576
  464.0 30.0 %collective-permute-start.23 = (bf16[512,1280]{1,0:T(8,128)(2,1)}, bf16[512,1280]{1,0:T(8,128)(2,1)}, u32[]{:S(2)}, u32[]{:S(2)}) collective-permute-start(bf16[512,1280]{1,0:T(8,128)(2,1)} %get-tuple-element.324), channel_id=1, source_target_pairs={{0,2},{1,3},{2,4},{3,5},{8,10},{9,11},{10,12},{11,13},{16,18},{17,... | collective-permute-start | bytes 3932168 | tf_op jit(solution)/shard_map/ppermute | solution.py:580
  466.4 27.6 %collective-permute-start.24 = (bf16[512,1280]{1,0:T(8,128)(2,1)}, bf16[512,1280]{1,0:T(8,128)(2,1)}, u32[]{:S(2)}, u32[]{:S(2)}) collective-permute-start(bf16[512,1280]{1,0:T(8,128)(2,1)} %get-tuple-element.325), channel_id=1, source_target_pairs={{6,4},{7,5},{4,2},{5,3},{14,12},{15,13},{12,10},{13,11},{22,20},{2... | collective-permute-start | bytes 3932168 | tf_op jit(solution)/shard_map/ppermute | solution.py:580
  489.0 46.8 %collective-permute-start.30 = (bf16[512,1280]{1,0:T(8,128)(2,1)}, bf16[512,1280]{1,0:T(8,128)(2,1)}, u32[]{:S(2)}, u32[]{:S(2)}) collective-permute-start(bf16[512,1280]{1,0:T(8,128)(2,1)} %get-tuple-element.344), channel_id=1, source_target_pairs={{0,1},{1,0},{2,3},{3,2},{4,5},{5,4},{6,7},{7,6},{8,9},{9,8},{10,11... | collective-permute-start | bytes 3932168 | tf_op jit(solution)/shard_map/ppermute | solution.py:576
  512.9 53.0 %collective-permute-start.33 = (bf16[640,1792]{1,0:T(8,128)(2,1)}, bf16[640,1792]{1,0:T(8,128)(2,1)}, u32[]{:S(2)}, u32[]{:S(2)}) collective-permute-start(bf16[640,1792]{1,0:T(8,128)(2,1)} %get-tuple-element.420), channel_id=1, source_target_pairs={{0,16},{8,24},{16,0},{24,8},{1,17},{9,25},{17,1},{25,9},{2,18},{10... | collective-permute-start | bytes 6881288 | tf_op jit(solution)/shard_map/ppermute | solution.py:765
  516.3 31.2 %collective-permute-start.34 = (bf16[512,1280]{1,0:T(8,128)(2,1)}, bf16[512,1280]{1,0:T(8,128)(2,1)}, u32[]{:S(2)}, u32[]{:S(2)}) collective-permute-start(bf16[512,1280]{1,0:T(8,128)(2,1)} %get-tuple-element.354), channel_id=1, source_target_pairs={{0,1},{1,0},{2,3},{3,2},{4,5},{5,4},{6,7},{7,6},{8,9},{9,8},{10,11... | collective-permute-start | bytes 3932168 | tf_op jit(solution)/shard_map/ppermute | solution.py:576
  522.8 29.2 %collective-permute-start.31 = (bf16[512,1280]{1,0:T(8,128)(2,1)}, bf16[512,1280]{1,0:T(8,128)(2,1)}, u32[]{:S(2)}, u32[]{:S(2)}) collective-permute-start(bf16[512,1280]{1,0:T(8,128)(2,1)} %get-tuple-element.350), channel_id=1, source_target_pairs={{0,2},{1,3},{2,4},{3,5},{4,6},{5,7},{8,10},{9,11},{10,12},{11,13},... | collective-permute-start | bytes 3932168 | tf_op jit(solution)/shard_map/ppermute | solution.py:580
  525.2 32.0 %collective-permute-start.32 = (bf16[512,1280]{1,0:T(8,128)(2,1)}, bf16[512,1280]{1,0:T(8,128)(2,1)}, u32[]{:S(2)}, u32[]{:S(2)}) collective-permute-start(bf16[512,1280]{1,0:T(8,128)(2,1)} %get-tuple-element.351), channel_id=1, source_target_pairs={{6,4},{7,5},{4,2},{5,3},{2,0},{3,1},{14,12},{15,13},{12,10},{13,11... | collective-permute-start | bytes 3932168 | tf_op jit(solution)/shard_map/ppermute | solution.py:580
  535.8 91.1 %collective-permute-start.38 = (bf16[2,4,2,40,3072]{4,3,1,2,0:T(8,128)(2,1)}, bf16[2,4,2,40,3072]{4,3,1,2,0:T(8,128)(2,1)}, u32[]{:S(2)}, u32[]{:S(2)}) collective-permute-start(bf16[2,4,2,40,3072]{4,3,1,2,0:T(8,128)(2,1)} %fusion.3), channel_id=1, source_target_pairs={{0,8},{8,0},{16,24},{24,16},{1,9},{9,1},{17,25},{25,17},{2,10},{10... | collective-permute-start | bytes 11796488 | tf_op jit(solution)/shard_map/ppermute | solution.py:709
  547.5 78.1 %collective-permute-start.29 = (bf16[512,1280]{1,0:T(8,128)(2,1)}, bf16[512,1280]{1,0:T(8,128)(2,1)}, u32[]{:S(2)}, u32[]{:S(2)}) collective-permute-start(bf16[512,1280]{1,0:T(8,128)(2,1)} %get-tuple-element.342), channel_id=1, source_target_pairs={{0,1},{1,0},{2,3},{3,2},{4,5},{5,4},{6,7},{7,6},{8,9},{9,8},{10,11... | collective-permute-start | bytes 3932168 | tf_op jit(solution)/shard_map/ppermute | solution.py:576
  552.0 74.9 %collective-permute-start.37 = (bf16[896,1280]{1,0:T(8,128)(2,1)S(1)}, bf16[896,1280]{1,0:T(8,128)(2,1)}, u32[]{:S(2)}, u32[]{:S(2)}) collective-permute-start(bf16[896,1280]{1,0:T(8,128)(2,1)S(1)} %add_convert_fusion.3.mine_ref), channel_id=1, source_target_pairs={{0,8},{8,0},{16,24},{24,16},{1,9},{9,1},{17,25},{25,17},{2,10},{10... | collective-permute-start | bytes 6881288 | tf_op jit(solution)/shard_map/ppermute | solution.py:770
  557.3 69.7 %collective-permute-start.36 = (bf16[640,1792]{1,0:T(8,128)(2,1)S(1)}, bf16[640,1792]{1,0:T(8,128)(2,1)}, u32[]{:S(2)}, u32[]{:S(2)}) collective-permute-start(bf16[640,1792]{1,0:T(8,128)(2,1)S(1)} %copy-done.12), channel_id=1, source_target_pairs={{0,16},{8,24},{16,0},{24,8},{1,17},{9,25},{17,1},{25,9},{2,18},{10... | collective-permute-start | bytes 6881288 | tf_op jit(solution)/shard_map/ppermute | solution.py:765
  567.6 59.3 %collective-permute-start.35 = (bf16[512,1280]{1,0:T(8,128)(2,1)S(1)}, bf16[512,1280]{1,0:T(8,128)(2,1)}, u32[]{:S(2)}, u32[]{:S(2)}) collective-permute-start(bf16[512,1280]{1,0:T(8,128)(2,1)S(1)} %add_convert_fusion.11.refs_2_), channel_id=1, source_target_pairs={{0,2},{1,3},{6,4},{7,5},{8,10},{9,11},{14,12},{15,13},{16,18},{17,... | collective-permute-start | bytes 3932168 | tf_op jit(solution)/shard_map/ppermute | solution.py:580
  625.6 29.1 %collective-permute-start.28 = (bf16[512,1280]{1,0:T(8,128)(2,1)}, bf16[512,1280]{1,0:T(8,128)(2,1)}, u32[]{:S(2)}, u32[]{:S(2)}) collective-permute-start(bf16[512,1280]{1,0:T(8,128)(2,1)} %get-tuple-element.340), channel_id=1, source_target_pairs={{0,1},{1,0},{2,3},{3,2},{4,5},{5,4},{6,7},{7,6},{8,9},{9,8},{10,11... | collective-permute-start | bytes 3932168 | tf_op jit(solution)/shard_map/ppermute | solution.py:576
  629.9 48.4 %collective-permute-start.51 = (bf16[2,4,2,40,1408]{4,3,1,2,0:T(8,128)(2,1)}, bf16[2,4,2,40,1408]{4,3,1,2,0:T(8,128)(2,1)}, u32[]{:S(2)}, u32[]{:S(2)}) collective-permute-start(bf16[2,4,2,40,1408]{4,3,1,2,0:T(8,128)(2,1)} %copy.80), channel_id=1, source_target_pairs={{0,8},{8,0},{16,24},{24,16},{1,9},{9,1},{17,25},{25,17},{2,10},{10... | collective-permute-start | bytes 5406728 | tf_op jit(solution)/shard_map/ppermute | solution.py:709
  634.8 30.6 %collective-permute-start.39 = (bf16[512,1280]{1,0:T(8,128)(2,1)}, bf16[512,1280]{1,0:T(8,128)(2,1)S(1)}, u32[]{:S(2)}, u32[]{:S(2)}) collective-permute-start(bf16[512,1280]{1,0:T(8,128)(2,1)} %get-tuple-element.382), channel_id=1, source_target_pairs={{0,2},{1,3},{2,4},{3,5},{8,10},{9,11},{10,12},{11,13},{16,18},{17,... | collective-permute-start | bytes 3932168 | tf_op jit(solution)/shard_map/ppermute | solution.py:580
  636.2 30.0 %collective-permute-start.40 = (bf16[512,1280]{1,0:T(8,128)(2,1)}, bf16[512,1280]{1,0:T(8,128)(2,1)S(1)}, u32[]{:S(2)}, u32[]{:S(2)}) collective-permute-start(bf16[512,1280]{1,0:T(8,128)(2,1)} %get-tuple-element.383), channel_id=1, source_target_pairs={{6,4},{7,5},{4,2},{5,3},{14,12},{15,13},{12,10},{13,11},{22,20},{2... | collective-permute-start | bytes 3932168 | tf_op jit(solution)/shard_map/ppermute | solution.py:580
  643.7 45.6 %collective-permute-start.57 = (bf16[1,4,2,40,3072]{4,3,1,2,0:T(8,128)(2,1)}, bf16[1,4,2,40,3072]{4,3,1,2,0:T(8,128)(2,1)}, u32[]{:S(2)}, u32[]{:S(2)}) collective-permute-start(bf16[1,4,2,40,3072]{4,3,1,2,0:T(8,128)(2,1)} %constant_dynamic-slice_fusion), channel_id=1, source_target_pairs={{0,16},{8,24},{16,0},{24,8},{1,17},{9,25},{17,1},{25,9},{2,18},{10... | collective-permute-start | bytes 5898248 | tf_op jit(solution)/shard_map/ppermute | solution.py:722
  654.7 70.7 %collective-permute-start.43 = (bf16[2,4,2,40,3840]{4,3,1,2,0:T(8,128)(2,1)}, bf16[2,4,2,40,3840]{4,3,1,2,0:T(8,128)(2,1)}, u32[]{:S(2)}, u32[]{:S(2)}) collective-permute-start(bf16[2,4,2,40,3840]{4,3,1,2,0:T(8,128)(2,1)} %copy.77), channel_id=1, source_target_pairs={{0,8},{8,0},{16,24},{24,16},{1,9},{9,1},{17,25},{25,17},{2,10},{10... | collective-permute-start | bytes 14745608 | tf_op jit(solution)/shard_map/ppermute | solution.py:709
  665.4 30.8 %collective-permute-start.27 = (bf16[512,1280]{1,0:T(8,128)(2,1)}, bf16[512,1280]{1,0:T(8,128)(2,1)S(1)}, u32[]{:S(2)}, u32[]{:S(2)}) collective-permute-start(bf16[512,1280]{1,0:T(8,128)(2,1)} %get-tuple-element.338), channel_id=1, source_target_pairs={{0,1},{1,0},{2,3},{3,2},{4,5},{5,4},{6,7},{7,6},{8,9},{9,8},{10,11... | collective-permute-start | bytes 3932168 | tf_op jit(solution)/shard_map/ppermute | solution.py:576
  672.8 34.0 %collective-permute-start.41 = (bf16[512,1280]{1,0:T(8,128)(2,1)}, bf16[512,1280]{1,0:T(8,128)(2,1)}, u32[]{:S(2)}, u32[]{:S(2)}) collective-permute-start(bf16[512,1280]{1,0:T(8,128)(2,1)} %get-tuple-element.388), channel_id=1, source_target_pairs={{0,2},{1,3},{2,4},{3,5},{4,6},{5,7},{8,10},{9,11},{10,12},{11,13},... | collective-permute-start | bytes 3932168 | tf_op jit(solution)/shard_map/ppermute | solution.py:580
  678.2 32.6 %collective-permute-start.42 = (bf16[512,1280]{1,0:T(8,128)(2,1)}, bf16[512,1280]{1,0:T(8,128)(2,1)}, u32[]{:S(2)}, u32[]{:S(2)}) collective-permute-start(bf16[512,1280]{1,0:T(8,128)(2,1)} %get-tuple-element.389), channel_id=1, source_target_pairs={{6,4},{7,5},{4,2},{5,3},{2,0},{3,1},{14,12},{15,13},{12,10},{13,11... | collective-permute-start | bytes 3932168 | tf_op jit(solution)/shard_map/ppermute | solution.py:580
  689.3 22.0 %collective-permute-start.52 = (bf16[1,4,2,40,1408]{4,3,1,2,0:T(8,128)(2,1)}, bf16[1,4,2,40,1408]{4,3,1,2,0:T(8,128)(2,1)}, u32[]{:S(2)}, u32[]{:S(2)}) collective-permute-start(bf16[1,4,2,40,1408]{4,3,1,2,0:T(8,128)(2,1)} %constant_dynamic-slice_fusion.3), channel_id=1, source_target_pairs={{0,16},{8,24},{16,0},{24,8},{1,17},{9,25},{17,1},{25,9},{2,18},{10... | collective-permute-start | bytes 2703368 | tf_op jit(solution)/shard_map/ppermute | solution.py:722
  696.2 25.0 %collective-permute-start.58 = (bf16[1,4,40,3072]{3,2,1,0:T(8,128)(2,1)}, bf16[1,4,40,3072]{3,2,1,0:T(8,128)(2,1)}, u32[]{:S(2)}, u32[]{:S(2)}) collective-permute-start(bf16[1,4,40,3072]{3,2,1,0:T(8,128)(2,1)} %dynamic-slice_bitcast_fusion.1), channel_id=1, source_target_pairs={{0,1},{1,0},{2,3},{3,2},{4,5},{5,4},{6,7},{7,6},{8,9},{9,8},{10,11... | collective-permute-start | bytes 2949128 | tf_op jit(solution)/shard_map/ppermute | solution.py:576
  706.8 70.8 %collective-permute-start.62 = (bf16[1280,1792]{1,0:T(8,128)(2,1)}, bf16[1280,1792]{1,0:T(8,128)(2,1)}, u32[]{:S(2)}, u32[]{:S(2)}) collective-permute-start(bf16[1280,1792]{1,0:T(8,128)(2,1)} %pad_maximum_fusion.mine_ref), channel_id=1, source_target_pairs={{0,8},{8,0},{16,24},{24,16},{1,9},{9,1},{17,25},{25,17},{2,10},{10... | collective-permute-start | bytes 13762568 | tf_op jit(solution)/shard_map/ppermute | solution.py:770
  713.0 24.4 %collective-permute-start.53 = (bf16[1,4,40,1408]{3,2,1,0:T(8,128)(2,1)S(1)}, bf16[1,4,40,1408]{3,2,1,0:T(8,128)(2,1)S(1)}, u32[]{:S(2)}, u32[]{:S(2)}) collective-permute-start(bf16[1,4,40,1408]{3,2,1,0:T(8,128)(2,1)S(1)} %dynamic-slice_bitcast_fusion.3), channel_id=1, source_target_pairs={{0,1},{1,0},{2,3},{3,2},{4,5},{5,4},{6,7},{7,6},{8,9},{9,8},{10,11... | collective-permute-start | bytes 1351688 | tf_op jit(solution)/shard_map/ppermute | solution.py:576
  722.8 14.5 %collective-permute-start.59 = (bf16[40,3072]{1,0:T(8,128)(2,1)S(1)}, bf16[40,3072]{1,0:T(8,128)(2,1)S(1)}, u32[]{:S(2)}, u32[]{:S(2)}) collective-permute-start(bf16[40,3072]{1,0:T(8,128)(2,1)S(1)} %get-tuple-element.436), channel_id=1, source_target_pairs={{0,2},{1,3},{2,4},{3,5},{4,6},{5,7},{6,0},{7,1},{8,10},{9,11},{10,... | collective-permute-start | bytes 737288 | tf_op jit(solution)/shard_map/ppermute | solution.py:580
  730.9 25.4 %collective-permute-start.45 = (bf16[1,4,2,40,1920]{4,3,1,2,0:T(8,128)(2,1)S(1)}, bf16[1,4,2,40,1920]{4,3,1,2,0:T(8,128)(2,1)S(1)}, u32[]{:S(2)}, u32[]{:S(2)}) collective-permute-start(bf16[1,4,2,40,1920]{4,3,1,2,0:T(8,128)(2,1)S(1)} %constant_dynamic-slice_fusion.5), channel_id=1, source_target_pairs={{0,16},{8,24},{16,0},{24,8},{1,17},{9,25},{17,1},{25,9},{2,18},{10... | collective-permute-start | bytes 3686408 | tf_op jit(solution)/shard_map/ppermute | solution.py:722
  732.8 26.3 %collective-permute-start.44 = (bf16[2,4,40,1920]{3,2,1,0:T(8,128)(2,1)S(1)}, bf16[2,4,40,1920]{3,2,1,0:T(8,128)(2,1)S(1)}, u32[]{:S(2)}, u32[]{:S(2)}) collective-permute-start(bf16[2,4,40,1920]{3,2,1,0:T(8,128)(2,1)S(1)} %dynamic-slice_bitcast_fusion), channel_id=1, source_target_pairs={{0,1},{1,0},{2,3},{3,2},{4,5},{5,4},{6,7},{7,6},{8,9},{9,8},{10,11... | collective-permute-start | bytes 3686408 | tf_op jit(solution)/shard_map/ppermute | solution.py:576
  737.3 12.2 %collective-permute-start.60 = (bf16[40,3072]{1,0:T(8,128)(2,1)S(1)}, bf16[40,3072]{1,0:T(8,128)(2,1)S(1)}, u32[]{:S(2)}, u32[]{:S(2)}) collective-permute-start(bf16[40,3072]{1,0:T(8,128)(2,1)S(1)} %get-tuple-element.435), channel_id=1, source_target_pairs={{0,4},{1,5},{2,6},{3,7},{4,0},{5,1},{6,2},{7,3},{8,12},{9,13},{10,... | collective-permute-start | bytes 737288 | tf_op jit(solution)/shard_map/ppermute | solution.py:580
  737.4 13.4 %collective-permute-start.61 = (bf16[40,3072]{1,0:T(8,128)(2,1)S(1)}, bf16[40,3072]{1,0:T(8,128)(2,1)S(1)}, u32[]{:S(2)}, u32[]{:S(2)}) collective-permute-start(bf16[40,3072]{1,0:T(8,128)(2,1)S(1)} %get-tuple-element.434), channel_id=1, source_target_pairs={{0,6},{1,7},{2,0},{3,1},{4,2},{5,3},{6,4},{7,5},{8,14},{9,15},{10,... | collective-permute-start | bytes 737288 | tf_op jit(solution)/shard_map/ppermute | solution.py:580
  749.5 10.9 %collective-permute-start.54 = (bf16[40,1408]{1,0:T(8,128)(2,1)S(1)}, bf16[40,1408]{1,0:T(8,128)(2,1)S(1)}, u32[]{:S(2)}, u32[]{:S(2)}) collective-permute-start(bf16[40,1408]{1,0:T(8,128)(2,1)S(1)} %get-tuple-element.439), channel_id=1, source_target_pairs={{0,2},{1,3},{2,4},{3,5},{4,6},{5,7},{6,0},{7,1},{8,10},{9,11},{10,... | collective-permute-start | bytes 337928 | tf_op jit(solution)/shard_map/ppermute | solution.py:580
  750.7 11.7 %collective-permute-start.55 = (bf16[40,1408]{1,0:T(8,128)(2,1)S(1)}, bf16[40,1408]{1,0:T(8,128)(2,1)S(1)}, u32[]{:S(2)}, u32[]{:S(2)}) collective-permute-start(bf16[40,1408]{1,0:T(8,128)(2,1)S(1)} %get-tuple-element.438), channel_id=1, source_target_pairs={{0,4},{1,5},{2,6},{3,7},{4,0},{5,1},{6,2},{7,3},{8,12},{9,13},{10,... | collective-permute-start | bytes 337928 | tf_op jit(solution)/shard_map/ppermute | solution.py:580
  759.6 11.5 %collective-permute-start.47 = (bf16[1,4,40,1920]{3,2,1,0:T(8,128)(2,1)S(1)}, bf16[1,4,40,1920]{3,2,1,0:T(8,128)(2,1)S(1)}, u32[]{:S(2)}, u32[]{:S(2)}) collective-permute-start(bf16[1,4,40,1920]{3,2,1,0:T(8,128)(2,1)S(1)} %dynamic-slice_bitcast_fusion.2), channel_id=1, source_target_pairs={{0,1},{1,0},{2,3},{3,2},{4,5},{5,4},{6,7},{7,6},{8,9},{9,8},{10,11... | collective-permute-start | bytes 1843208 | tf_op jit(solution)/shard_map/ppermute | solution.py:576
  760.4 11.5 %collective-permute-start.46 = (bf16[1,4,40,1920]{3,2,1,0:T(8,128)(2,1)S(1)}, bf16[1,4,40,1920]{3,2,1,0:T(8,128)(2,1)S(1)}, u32[]{:S(2)}, u32[]{:S(2)}) collective-permute-start(bf16[1,4,40,1920]{3,2,1,0:T(8,128)(2,1)S(1)} %constant_dynamic-slice_fusion.4), channel_id=1, source_target_pairs={{0,16},{8,24},{16,0},{24,8},{1,17},{9,25},{17,1},{25,9},{2,18},{10... | collective-permute-start | bytes 1843208 | tf_op jit(solution)/shard_map/ppermute | solution.py:722
  772.3 16.4 %collective-permute-start.48 = (bf16[40,3840]{1,0:T(8,128)(2,1)S(1)}, bf16[40,3840]{1,0:T(8,128)(2,1)S(1)}, u32[]{:S(2)}, u32[]{:S(2)}) collective-permute-start(bf16[40,3840]{1,0:T(8,128)(2,1)S(1)} %get-tuple-element.432), channel_id=1, source_target_pairs={{0,2},{1,3},{2,4},{3,5},{4,6},{5,7},{6,0},{7,1},{8,10},{9,11},{10,... | collective-permute-start | bytes 921608 | tf_op jit(solution)/shard_map/ppermute | solution.py:580
  773.3 19.3 %collective-permute-start.49 = (bf16[40,3840]{1,0:T(8,128)(2,1)S(1)}, bf16[40,3840]{1,0:T(8,128)(2,1)S(1)}, u32[]{:S(2)}, u32[]{:S(2)}) collective-permute-start(bf16[40,3840]{1,0:T(8,128)(2,1)S(1)} %get-tuple-element.433), channel_id=1, source_target_pairs={{0,4},{1,5},{2,6},{3,7},{4,0},{5,1},{6,2},{7,3},{8,12},{9,13},{10,... | collective-permute-start | bytes 921608 | tf_op jit(solution)/shard_map/ppermute | solution.py:580
  775.6 17.1 %collective-permute-start.50 = (bf16[40,3840]{1,0:T(8,128)(2,1)S(1)}, bf16[40,3840]{1,0:T(8,128)(2,1)S(1)}, u32[]{:S(2)}, u32[]{:S(2)}) collective-permute-start(bf16[40,3840]{1,0:T(8,128)(2,1)S(1)} %get-tuple-element.431), channel_id=1, source_target_pairs={{0,6},{1,7},{2,0},{3,1},{4,2},{5,3},{6,4},{7,5},{8,14},{9,15},{10,... | collective-permute-start | bytes 921608 | tf_op jit(solution)/shard_map/ppermute | solution.py:580
  (43 other events, 847.4 us)
Sparse Core Ops, SparseCore 0:
  12.4 135.3 all-gather.2
  279.9 95.3 all-gather.4
